TPU v7x, 32 devices: a whole 2x2x4 slice. The times are simulated.
32 devices in a mesh: grp: 2 (over y), seq: 8 (over z, x), pd: 2 (over core).
Axes of the slice: x: 2, y: 2, z: 4, core: 2. Of those that a mesh axis runs over, the one named last changes fastest.
Arguments:
- new_kv: bfloat16 [4, 1024, 2048], P('grp', ('seq', 'pd')), parts along dimension 0, may hold values from -6 to 6
- old_keys: bfloat16 [8, 2048, 256], P('seq', 'grp'), parts along dimension 1, may hold values from -18 to 18
- old_values: bfloat16 [8, 2048, 256], P('seq', 'grp'), parts along dimension 1, may hold values from -6 to 6
- suffix_keys: bfloat16 [2, 8, 128, 32, 256], P('pd', 'seq', 'grp'), parts along dimension 2, may hold values from -28 to 28
- suffix_values: bfloat16 [2, 8, 128, 32, 256], P('pd', 'seq', 'grp'), parts along dimension 2, may hold values from -6 to 6
- queries: bfloat16 [128, 8192], P(('seq', 'pd'), 'grp'), parts along dimension 1, may hold values from -18 to 18
- lengths: int32 [256], P('grp'), parts along dimension 0, may hold values from 1 to 32, as said below
- assign: int32 [256], P('grp'), parts along dimension 0, may hold values from 0 to 1
Outputs:
- new_cache: bfloat16 [2, 8, 16, 128, 256], P(None, 'seq', 'grp', 'pd'), parts along dimension 2
- attention: bfloat16 [128, 8192], P(('seq', 'pd'), 'grp'), parts along dimension 1
There are 2 independent parts, one for each index of `grp`. A program takes and returns all parts, laid end to end along the dimension named above; each array names one. Nothing has to cross between parts.
Inputs may be any that keep to these rules, and one draw needn't show every extreme that they name: `lengths`: suffix tokens of each request, its new token included; some request has exactly 32. `assign`: which of the 2 prefixes each request continues.
All inputs are finite; a program needn't handle non-finite values.
Results may differ from a plain program's by a relative error of at most 0.0048.
Values may be sent and summed in bfloat16 or wider, within the bound.
No kernel may reach another device: no remote copies, remote signals or barrier semaphores. Data moves between devices by JAX's collectives and lax.ppermute only.
A program may use at most 64 MiB of HBM per device.

v0:
```python
import math

import jax
import jax.numpy as jnp
from jax import lax
from jax.sharding import PartitionSpec as P

HD = 128
KVH = 16
NQH = 32
NPFX = 2


softcap = 50.0
query_scale = 1.0 / 12.0


def rotary(key_rows, positions):
    head_width = key_rows.shape[-1]
    halfway = head_width // 2
    inverse = 10000.0 ** (-2.0 * jnp.arange(halfway).astype(jnp.float32) / head_width)
    angles = positions.astype(jnp.float32)[:, None] * inverse[None, :]
    angles = jnp.concatenate([angles, angles], axis=1)
    values = key_rows.astype(jnp.float32)
    turned = jnp.concatenate([-values[..., halfway:], values[..., :halfway]], axis=-1)
    return values * jnp.cos(angles)[:, None, :] + turned * jnp.sin(angles)[:, None, :]


def capped(scores):
    return softcap * jnp.tanh(scores * query_scale / softcap)


def local(new_kv, old_keys, old_values, suffix_keys, suffix_values, queries, lengths, assign):
    seq_count = lax.axis_size("seq")
    core_count = lax.axis_size("pd")
    seq_place = lax.axis_index("seq")
    core_place = lax.axis_index("pd")
    per_kv = NQH // KVH
    sub_blocks = max(seq_count // KVH, 1)
    heads_here = max(KVH // seq_count, 1)
    head_groups = KVH // heads_here
    prefix_rows = new_kv.shape[1]
    request_rows = queries.shape[0]
    prefix_length = prefix_rows * seq_count * core_count // NPFX
    group_width = heads_here * per_kv * HD
    positions = (
        (seq_place * core_count + core_place) * prefix_rows
        + jnp.arange(prefix_rows, dtype=jnp.int32)
    ) % prefix_length
    rotated = rotary(new_kv[0].reshape(prefix_rows, KVH, HD), positions).astype(jnp.bfloat16)
    rotated = rotated.reshape(prefix_rows, KVH * HD)
    outgoing = jnp.stack([rotated, new_kv[1]]).reshape(
        2, prefix_rows // sub_blocks, seq_count, heads_here * HD
    )
    arrived = lax.all_to_all(outgoing, "seq", split_axis=2, concat_axis=1, tiled=True)
    new_cache = arrived.reshape(2, 1, seq_count, prefix_rows // sub_blocks, heads_here * HD)
    head_group = seq_place % head_groups
    token_block = seq_place // head_groups
    half_rows = seq_count * request_rows
    gathered = lax.all_gather(queries, "seq", axis=0, tiled=True)
    own_queries = lax.dynamic_slice_in_dim(gathered, head_group * group_width, group_width, 1)
    query_blocks = own_queries.reshape(half_rows, heads_here, per_kv, HD)
    own_assign = lax.dynamic_index_in_dim(
        assign.reshape(seq_count, core_count, request_rows), core_place, 1, keepdims=False
    ).reshape(half_rows)
    own_lengths = lax.dynamic_index_in_dim(
        lengths.reshape(seq_count, core_count, request_rows), core_place, 1, keepdims=False
    ).reshape(half_rows)
    prefix_keys = old_keys[0].reshape(-1, heads_here, HD)
    prefix_values = old_values[0].reshape(-1, heads_here, HD)
    token_count = prefix_keys.shape[0]
    token_prefix = (
        jnp.arange(token_count, dtype=jnp.int32) * sub_blocks + token_block
    ) // prefix_length
    block_rows = math.gcd(half_rows, 256)

    def prefix_block(block_index):
        row_start = block_index * block_rows
        query_part = lax.dynamic_slice_in_dim(query_blocks, row_start, block_rows, 0)
        assign_part = lax.dynamic_slice_in_dim(own_assign, row_start, block_rows, 0)
        scores = capped(
            jnp.einsum(
                "rhqd,thd->rhqt", query_part, prefix_keys, preferred_element_type=jnp.float32
            )
        )
        allowed = (assign_part[:, None] == token_prefix[None, :])[:, None, None, :]
        weights = jnp.where(allowed, jnp.exp(scores), 0.0)
        totals = jnp.sum(weights, axis=-1)
        numerators = jnp.einsum(
            "rhqt,thd->rhqd",
            weights.astype(jnp.bfloat16),
            prefix_values,
            preferred_element_type=jnp.float32,
        )
        return (totals, numerators)

    totals, numerators = lax.map(prefix_block, jnp.arange(half_rows // block_rows, dtype=jnp.int32))
    totals = totals.reshape(half_rows, heads_here, per_kv)
    numerators = numerators.reshape(half_rows, heads_here, per_kv, HD)
    suffix_rows = head_groups * request_rows
    suffix_start = token_block * suffix_rows
    suffix_query = lax.dynamic_slice_in_dim(query_blocks, suffix_start, suffix_rows, 0)
    suffix_length = lax.dynamic_slice_in_dim(own_lengths, suffix_start, suffix_rows, 0)
    recent_keys = suffix_keys[0, 0].reshape(suffix_rows, -1, heads_here, HD)
    recent_values = suffix_values[0, 0].reshape(suffix_rows, -1, heads_here, HD)
    recent_scores = capped(
        jnp.einsum("rhqd,rphd->rhqp", suffix_query, recent_keys, preferred_element_type=jnp.float32)
    )
    live_slots = jnp.arange(recent_keys.shape[1], dtype=jnp.int32)[None, :] < suffix_length[:, None]
    recent_weights = jnp.where(live_slots[:, None, None, :], jnp.exp(recent_scores), 0.0)
    recent_totals = jnp.sum(recent_weights, axis=-1)
    recent_numerators = jnp.einsum(
        "rhqp,rphd->rhqd",
        recent_weights.astype(jnp.bfloat16),
        recent_values,
        preferred_element_type=jnp.float32,
    )
    totals = lax.dynamic_update_slice_in_dim(
        totals,
        lax.dynamic_slice_in_dim(totals, suffix_start, suffix_rows, 0) + recent_totals,
        suffix_start,
        0,
    )
    numerators = lax.dynamic_update_slice_in_dim(
        numerators,
        lax.dynamic_slice_in_dim(numerators, suffix_start, suffix_rows, 0) + recent_numerators,
        suffix_start,
        0,
    )
    back_numerators, back_totals = (
        lax.all_to_all(
            numerators.reshape(seq_count, request_rows, group_width),
            "seq",
            split_axis=0,
            concat_axis=0,
            tiled=True,
        ),
        lax.all_to_all(
            totals.reshape(seq_count, request_rows, heads_here * per_kv),
            "seq",
            split_axis=0,
            concat_axis=0,
            tiled=True,
        ),
    )
    back_numerators = back_numerators.reshape(
        sub_blocks, head_groups, request_rows, heads_here * per_kv, HD
    ).sum(0)
    back_totals = back_totals.reshape(
        sub_blocks, head_groups, request_rows, heads_here * per_kv
    ).sum(0)
    attention = (
        (back_numerators / back_totals[..., None])
        .transpose(1, 0, 2, 3)
        .reshape(request_rows, NQH * HD)
    )
    return (new_cache, attention.astype(jnp.bfloat16))


def solution(mesh):
    return jax.shard_map(
        local,
        mesh=mesh,
        in_specs=(
            P("grp", ("seq", "pd"), None),
            P("seq", "grp", None),
            P("seq", "grp", None),
            P("pd", "seq", "grp", None, None),
            P("pd", "seq", "grp", None, None),
            P(("seq", "pd"), "grp"),
            P("grp"),
            P("grp"),
        ),
        out_specs=(P(None, "seq", "grp", "pd", None), P(("seq", "pd"), "grp")),
        check_vma=False,
    )
```

profile of v0, /device:TPU:0, one launch (start us, length us, event | category | flops | bytes accessed | tf_op | source)
XLA Modules:
  0.0 77.6 jit_solution(263125712735373074)
XLA Ops:
  0.7 33.2 %all_gather.3 = bf16[64,4096]{1,0:T(8,128)(2,1)S(1)} all-gather(bf16[8,4096]{1,0:T(8,128)(2,1)} %param.13), channel_id=1, replica_groups=mesh['grp'=2,'seq'=8,'pd'=2] {'seq'}, dimensions={0}, use_global_device_ids=true | all-gather | bytes 589824 | tf_op jit(solution)/shard_map/all_gather | solution.py:60
  33.9 0.6 copy-done.4
  34.6 0.1 reshape.210
  34.7 0.6 copy-done.5
  35.2 0.1 reshape.212
  35.5 1.4 %reshape_squeeze.15 = bf16[64,32,2,128]{3,2,1,0:T(2,128)(2,1)S(1)} reshape(bf16[1,1,64,32,256]{4,3,2,1,0:T(8,128)(2,1)} %param.11) | data formatting | bytes 2097152 | tf_op jit(solution)/shard_map/reshape;squeeze | solution.py:104
  37.1 0.1 reshape_squeeze.13
  37.2 0.8 %fusion.29 = (f32[64,2,2]{2,1,0:T(2,128)S(1)}, bf16[64,2,2,32]{3,2,1,0:T(2,128)(2,1)S(1)}) fusion(bf16[64,2,2,128]{3,2,1,0:T(2,128)(2,1)S(1)} %reshape.211, bf16[64,32,2,128]{3,2,1,0:T(2,128)(2,1)S(1)} %reshape_squeeze.15, pred[64,32]{1,0:T(8,128)(4,1)S(1)} %iota_compare_fusion), kind=kOutput, calls=%fused_computation.55 | convolution fusion | flops 2137856 | bytes 1133568 | tf_op jit(solution)/shard_map/rhqd,rphd->rhqp/dot_general | solution.py:107
  38.1 0.1 broadcast_compare_fusion
  38.2 0.6 fusion.28
  38.9 0.6 copy.45
  39.5 5.7 %all-to-all-start.2 = ((f32[8,8,4]{1,2,0:T(4,128)}), f32[8,8,4]{1,2,0:T(4,128)S(1)}, u32[]{:S(2)}, u32[]{:S(2)}) async-start(f32[8,8,4]{1,2,0:T(4,128)} %copy.45), calls=%async_computation.2 | async-start | bytes 32768 | tf_op jit(solution)/shard_map/all_to_all | solution.py:138
  45.2 0.3 reshape_squeeze.16
  45.5 0.7 copy-done.3
  46.3 0.1 reshape_squeeze.14
  46.5 0.2 fusion.22
  46.7 0.6 copy-done
  47.4 0.1 copy.53
  47.5 0.2 slice_negate_fusion
  47.7 0.4 fusion.10
  48.0 0.3 fusion.5
  48.4 0.2 maximum_multiply_fusion
  48.6 0.1 copy.43
  48.7 0.8 reshape.213
  49.7 2.1 %all-to-all-done.2 = f32[8,8,4]{1,2,0:T(4,128)S(1)} async-done(((f32[8,8,4]{1,2,0:T(4,128)}), f32[8,8,4]{1,2,0:T(4,128)S(1)}, u32[]{:S(2)}, u32[]{:S(2)}) %all-to-all-start.2) | async-done | bytes 1056 | tf_op jit(solution)/shard_map/all_to_all | solution.py:138
  51.8 3.9 %all-to-all-start.1 = ((f32[8,8,512]{2,1,0:T(8,128)}), f32[8,8,512]{2,1,0:T(8,128)S(1)}, u32[]{:S(2)}, u32[]{:S(2)}) async-start(f32[8,8,512]{2,1,0:T(8,128)} %reshape.213), calls=%async_computation.1 | async-start | bytes 262144 | tf_op jit(solution)/shard_map/all_to_all | solution.py:131
  55.9 0.9 %copy.36 = bf16[2,64,8,256]{3,1,0,2:T(8,128)(2,1)} copy(bf16[2,64,8,256]{3,2,1,0:T(8,128)(2,1)S(1)} %pad_maximum_fusion) | data formatting | bytes 1048576 | tf_op jit(solution)/shard_map/stack | solution.py:52
  56.8 6.2 %all-to-all-done.1 = f32[8,8,512]{2,1,0:T(8,128)S(1)} async-done(((f32[8,8,512]{2,1,0:T(8,128)}), f32[8,8,512]{2,1,0:T(8,128)S(1)}, u32[]{:S(2)}, u32[]{:S(2)}) %all-to-all-start.1) | async-done | bytes 131104 | tf_op jit(solution)/shard_map/all_to_all | solution.py:131
  63.0 3.5 %all-to-all-start = ((bf16[2,64,8,256]{3,1,0,2:T(8,128)(2,1)}), bf16[2,64,8,256]{3,1,0,2:T(8,128)(2,1)S(1)}, u32[]{:S(2)}, u32[]{:S(2)}) async-start(bf16[2,64,8,256]{3,1,0,2:T(8,128)(2,1)} %copy.36), calls=%async_computation | async-start | bytes 1048576 | tf_op jit(solution)/shard_map/all_to_all | solution.py:55
  66.5 0.7 fusion.18
  67.3 9.5 %all-to-all-done = bf16[2,64,8,256]{3,1,0,2:T(8,128)(2,1)S(1)} async-done(((bf16[2,64,8,256]{3,1,0,2:T(8,128)(2,1)}), bf16[2,64,8,256]{3,1,0,2:T(8,128)(2,1)S(1)}, u32[]{:S(2)}, u32[]{:S(2)}) %all-to-all-start) | async-done | bytes 524320 | tf_op jit(solution)/shard_map/all_to_all | solution.py:55
  76.7 0.8 %copy.46 = bf16[2,1,8,64,256]{4,3,2,1,0:T(8,128)(2,1)} copy(bf16[2,1,8,64,256]{4,3,0,2,1:T(8,128)(2,1)S(1)} %bitcast.43) | data formatting | bytes 1048576
  (29 shorter events, 1.1 us)
Async XLA Ops:
  33.9 0.7 copy-start.4
  34.6 0.7 copy-start.5
  35.5 1.5 %copy-start.2 = (bf16[1,1024,256]{2,1,0:T(8,128)(2,1)S(1)}, bf16[1,1024,256]{2,1,0:T(8,128)(2,1)}, u32[]{:S(2)}) copy-start(bf16[1,1024,256]{2,1,0:T(8,128)(2,1)} %param.9) | copy-start | bytes 1572868
  38.2 7.0 %copy-start.1 = (bf16[1,1,64,32,256]{4,3,2,1,0:T(8,128)(2,1)S(1)}, bf16[1,1,64,32,256]{4,3,2,1,0:T(8,128)(2,1)}, u32[]{:S(2)}) copy-start(bf16[1,1,64,32,256]{4,3,2,1,0:T(8,128)(2,1)} %param.12) | copy-start | bytes 3145732
  39.5 12.2 %all-to-all-start.2 = ((f32[8,8,4]{1,2,0:T(4,128)}), f32[8,8,4]{1,2,0:T(4,128)S(1)}, u32[]{:S(2)}, u32[]{:S(2)}) async-start(f32[8,8,4]{1,2,0:T(4,128)} %copy.45), calls=%async_computation.2 | async-start | bytes 32768 | tf_op jit(solution)/shard_map/all_to_all | solution.py:138
  45.2 1.0 %copy-start.3 = (bf16[1,1024,256]{2,1,0:T(8,128)(2,1)S(1)}, bf16[1,1024,256]{2,1,0:T(8,128)(2,1)}, u32[]{:S(2)}) copy-start(bf16[1,1024,256]{2,1,0:T(8,128)(2,1)} %param.10) | copy-start | bytes 1572868
  46.3 1.0 %copy-start = (bf16[2,64,2048]{2,1,0:T(8,128)(2,1)S(1)}, bf16[2,64,2048]{2,1,0:T(8,128)(2,1)}, u32[]{:S(2)}) copy-start(bf16[2,64,2048]{2,1,0:T(8,128)(2,1)} %param.8) | copy-start | bytes 1572868
  51.8 11.3 %all-to-all-start.1 = ((f32[8,8,512]{2,1,0:T(8,128)}), f32[8,8,512]{2,1,0:T(8,128)S(1)}, u32[]{:S(2)}, u32[]{:S(2)}) async-start(f32[8,8,512]{2,1,0:T(8,128)} %reshape.213), calls=%async_computation.1 | async-start | bytes 262144 | tf_op jit(solution)/shard_map/all_to_all | solution.py:131
  63.0 13.7 %all-to-all-start = ((bf16[2,64,8,256]{3,1,0,2:T(8,128)(2,1)}), bf16[2,64,8,256]{3,1,0,2:T(8,128)(2,1)S(1)}, u32[]{:S(2)}, u32[]{:S(2)}) async-start(bf16[2,64,8,256]{3,1,0,2:T(8,128)(2,1)} %copy.36), calls=%async_computation | async-start | bytes 1048576 | tf_op jit(solution)/shard_map/all_to_all | solution.py:55
where the time goes:
time: 78.1 us; the launch traced here: 77.6 us
  blocking collectives  33.2 us (43%)
  waiting for transfers between devices  17.8 us (23%)
  starting transfers between devices  13.1 us (17%)
  local copies, waits for them, and re-layouts  8.69 us (11%)
  matrix products  2.09 us (3%)
  other arithmetic  1.83 us (2%)
  between operations  0.9 us (1%)
    all_gather x1, blocking collectives, local(): gathered = lax.all_gather(queries, 'seq', axis=0, tiled=True)  33.2 us
    all_to_all x1, waiting for transfers between devices, local(): lax.all_to_all(outgoing, 'seq', split_axis=2, concat_axis=1, tiled=True)  9.46 us
    all_to_all x1, waiting for transfers between devices, local(): lax.all_to_all(numerators.reshape(seq_count, request_rows, group_width),...  6.2 us
    all_to_all x1, starting transfers between devices, local(): lax.all_to_all(totals.reshape(seq_count, request_rows, heads_here * per_k...  5.66 us
    all_to_all x1, starting transfers between devices, local(): lax.all_to_all(numerators.reshape(seq_count, request_rows, group_width),...  3.91 us
    unnamed x16, local copies, waits for them, and re-layouts  3.6 us
    all_to_all x1, starting transfers between devices, local(): lax.all_to_all(outgoing, 'seq', split_axis=2, concat_axis=1, tiled=True)  3.49 us
    all_to_all x1, waiting for transfers between devices, local(): lax.all_to_all(totals.reshape(seq_count, request_rows, heads_here * per_k...  2.1 us
  transfers between devices with their start and end apart: 3, of which 3 were waited for; matrix products, arithmetic and copies ran while one was open for 6% of the time, Pallas kernels for 0%

commit v1 on v0

--- a/solution.py
+++ b/solution.py
@@ -1,8 +1,12 @@
+import functools
 import math
 
 import jax
 import jax.numpy as jnp
+import numpy as np
 from jax import lax
+from jax.experimental import pallas as pl
+from jax.experimental.pallas import tpu as pltpu
 from jax.sharding import PartitionSpec as P
 
 HD = 128
@@ -30,7 +34,7 @@
     return softcap * jnp.tanh(scores * query_scale / softcap)
 
 
-def local(new_kv, old_keys, old_values, suffix_keys, suffix_values, queries, lengths, assign):
+def general(new_kv, old_keys, old_values, suffix_keys, suffix_values, queries, lengths, assign):
     seq_count = lax.axis_size("seq")
     core_count = lax.axis_size("pd")
     seq_place = lax.axis_index("seq")
@@ -157,6 +161,190 @@
     return (new_cache, attention.astype(jnp.bfloat16))
 
 
+def rotate_kernel(seq_count, core_count, prefix_length, rates_ref, kv_ref, *out_refs):
+    place = lax.axis_index("seq")
+    rows = kv_ref.shape[1]
+    width = kv_ref.shape[2] // seq_count
+    first = (place * core_count + lax.axis_index("pd")) * rows
+    position = (first + lax.broadcasted_iota(jnp.int32, (rows, HD), 0)) % prefix_length
+    angles = position.astype(jnp.float32) * rates_ref[...]
+    cosine = jnp.cos(angles)
+    sine = jnp.sin(angles)
+    sine = jnp.where(lax.broadcasted_iota(jnp.int32, (rows, HD), 1) < HD // 2, -sine, sine)
+    for k in range(seq_count):
+        block = jnp.bitwise_xor(place, k) * width
+        for h in range(width // HD):
+            columns = pl.ds(pl.multiple_of(block + h * HD, HD), HD)
+            keys = kv_ref[0, :, columns].astype(jnp.float32)
+            turned = pltpu.roll(keys, HD // 2, 1)
+            out_refs[k][0, :, h * HD : (h + 1) * HD] = (keys * cosine + turned * sine).astype(jnp.bfloat16)
+            out_refs[k][1, :, h * HD : (h + 1) * HD] = kv_ref[1, :, columns]
+
+
+def rotate_blocks(new_kv, seq_count, core_count):
+    _, rows, columns = new_kv.shape
+    width = columns // seq_count
+    prefix_length = rows * seq_count * core_count // NPFX
+    rates = 10000.0 ** (-2.0 * (np.arange(HD) % (HD // 2)) / HD)
+    return pl.pallas_call(
+        functools.partial(rotate_kernel, seq_count, core_count, prefix_length),
+        out_shape=[jax.ShapeDtypeStruct((2, rows, width), jnp.bfloat16)] * seq_count,
+        in_specs=[pl.BlockSpec(memory_space=pltpu.VMEM)] * 2,
+        out_specs=[pl.BlockSpec(memory_space=pltpu.VMEM)] * seq_count,
+        cost_estimate=pl.CostEstimate(
+            flops=6 * rows * columns, bytes_accessed=8 * rows * columns, transcendentals=2 * rows * HD
+        ),
+    )(jnp.asarray(rates.astype(np.float32)).reshape(1, HD), new_kv)
+
+
+def assemble_kernel(seq_count, *refs):
+    *pieces, out_ref, sems = refs
+    place = lax.axis_index("seq")
+    copies = []
+    for k in range(seq_count):
+        for v in range(2):
+            copies.append(
+                pltpu.make_async_copy(
+                    pieces[k].at[v], out_ref.at[v, 0, jnp.bitwise_xor(place, k)], sems.at[k, v]
+                )
+            )
+            copies[-1].start()
+    for copy in copies:
+        copy.wait()
+
+
+def assemble(pieces):
+    count = len(pieces)
+    _, rows, width = pieces[0].shape
+    return pl.pallas_call(
+        functools.partial(assemble_kernel, count),
+        out_shape=jax.ShapeDtypeStruct((2, 1, count, rows, width), jnp.bfloat16),
+        in_specs=[pl.BlockSpec(memory_space=pl.ANY)] * count,
+        out_specs=pl.BlockSpec(memory_space=pl.ANY),
+        scratch_shapes=[pltpu.SemaphoreType.DMA((count, 2))],
+        cost_estimate=pl.CostEstimate(
+            flops=0, bytes_accessed=8 * count * rows * width, transcendentals=0
+        ),
+    )(*pieces)
+
+
+def weigh(scores):
+    return jnp.exp2((softcap * math.log2(math.e)) * jnp.tanh(scores * (query_scale / softcap)))
+
+
+NT = (((1,), (1,)), ((), ()))
+NN = (((1,), (0,)), ((), ()))
+
+
+def attend_kernel(q_ref, keys_ref, values_ref, skeys_ref, svalues_ref, assign_ref, lengths_ref, out_ref, num_ref, total_ref):
+    requests = q_ref.shape[0]
+    per_kv = NQH // KVH
+    heads_here = keys_ref.shape[2] // HD
+    length = keys_ref.shape[1] // NPFX
+    slots = skeys_ref.shape[3]
+    span = 8
+    which = assign_ref[...]
+    for h in range(heads_here):
+        columns = slice(h * HD, (h + 1) * HD)
+        query = jnp.concatenate(
+            [q_ref[:, (h * per_kv + j) * HD : (h * per_kv + j + 1) * HD] for j in range(per_kv)], axis=0
+        )
+        scores = lax.dot_general(query, keys_ref[0, :length, columns], NT, preferred_element_type=jnp.float32)
+        for p in range(1, NPFX):
+            other = lax.dot_general(
+                query, keys_ref[0, p * length : (p + 1) * length, columns], NT, preferred_element_type=jnp.float32
+            )
+            scores = jnp.where(which == p, other, scores)
+        weights = weigh(scores)
+        total = jnp.sum(weights, axis=1, keepdims=True)
+        numerator = None
+        for p in range(NPFX):
+            part = lax.dot_general(
+                jnp.where(which == p, weights, 0.0).astype(jnp.bfloat16),
+                values_ref[0, p * length : (p + 1) * length, columns],
+                NN,
+                preferred_element_type=jnp.float32,
+            )
+            numerator = part if numerator is None else numerator + part
+        query32 = query.astype(jnp.float32)
+        column = lax.broadcasted_iota(jnp.int32, (span * per_kv, span * slots), 1)
+        low = lax.broadcasted_iota(jnp.int32, (span * per_kv, span * slots), 0) % span * slots
+        num_ref[...] = numerator
+        total_ref[...] = jnp.broadcast_to(total, total_ref.shape)
+        for b in range(requests // span):
+            picked = [slice(j * requests + b * span, j * requests + (b + 1) * span) for j in range(per_kv)]
+            part = jnp.concatenate([query32[rows] for rows in picked], axis=0).astype(jnp.bfloat16)
+            skeys = skeys_ref[0, 0, b * span : (b + 1) * span, :, columns].reshape(span * slots, HD)
+            svalues = svalues_ref[0, 0, b * span : (b + 1) * span, :, columns].reshape(span * slots, HD)
+            recent = weigh(lax.dot_general(part, skeys, NT, preferred_element_type=jnp.float32))
+            live = jnp.concatenate([lengths_ref[rows] for rows in picked], axis=0)
+            recent = jnp.where((column >= low) & (column < low + live), recent, 0.0)
+            more = jnp.sum(recent, axis=1, keepdims=True)
+            added = lax.dot_general(recent.astype(jnp.bfloat16), svalues, NN, preferred_element_type=jnp.float32)
+            for j, rows in enumerate(picked):
+                num_ref[rows] += added[j * span : (j + 1) * span]
+                total_ref[rows] += jnp.broadcast_to(more[j * span : (j + 1) * span], (span, HD))
+        result = (num_ref[...] / total_ref[...]).astype(jnp.bfloat16)
+        for j in range(per_kv):
+            out_ref[:, (h * per_kv + j) * HD : (h * per_kv + j + 1) * HD] = result[j * requests : (j + 1) * requests]
+
+
+def attend(queries, old_keys, old_values, suffix_keys, suffix_values, assign, lengths):
+    requests, width = queries.shape
+    per_kv = NQH // KVH
+    tall = per_kv * requests
+    tokens = old_keys.shape[1]
+    return pl.pallas_call(
+        attend_kernel,
+        out_shape=jax.ShapeDtypeStruct((requests, width), jnp.bfloat16),
+        in_specs=[pl.BlockSpec(memory_space=pltpu.VMEM)] * 7,
+        out_specs=pl.BlockSpec(memory_space=pltpu.VMEM),
+        scratch_shapes=[pltpu.VMEM((tall, HD), jnp.float32), pltpu.VMEM((tall, HD), jnp.float32)],
+        compiler_params=pltpu.CompilerParams(vmem_limit_bytes=24 * 2**20),
+        cost_estimate=pl.CostEstimate(
+            flops=4 * requests * width * tokens * 2, bytes_accessed=3 * 2**20, transcendentals=requests * width * 8
+        ),
+    )(queries, old_keys, old_values, suffix_keys, suffix_values, assign, lengths)
+
+
+def local(new_kv, old_keys, old_values, suffix_keys, suffix_values, queries, lengths, assign):
+    seq_count = lax.axis_size("seq")
+    core_count = lax.axis_size("pd")
+    if seq_count > KVH or seq_count & (seq_count - 1):
+        return general(new_kv, old_keys, old_values, suffix_keys, suffix_values, queries, lengths, assign)
+    core_place = lax.axis_index("pd")
+    per_kv = NQH // KVH
+    request_rows = queries.shape[0]
+    half_rows = seq_count * request_rows
+    group_width = queries.shape[1] // seq_count
+    asked = lax.all_to_all(
+        queries.reshape(request_rows, seq_count, group_width).transpose(1, 0, 2), "seq", 0, 0, tiled=True
+    )
+    blocks = rotate_blocks(new_kv, seq_count, core_count)
+    pieces = [blocks[0]]
+    for k in range(1, seq_count):
+        pieces.append(lax.ppermute(blocks[k], "seq", [(i, i ^ k) for i in range(seq_count)]))
+
+    def own(values):
+        mine = lax.dynamic_index_in_dim(
+            values.reshape(seq_count, core_count, request_rows), core_place, 1, keepdims=False
+        ).reshape(half_rows)
+        return jnp.tile(mine, per_kv)[:, None]
+
+    attended = attend(
+        asked.reshape(half_rows, group_width),
+        old_keys,
+        old_values,
+        suffix_keys,
+        suffix_values,
+        own(assign),
+        own(lengths),
+    )
+    back = lax.all_to_all(attended.reshape(seq_count, request_rows, group_width), "seq", 0, 0, tiled=True)
+    attention = back.transpose(1, 0, 2).reshape(request_rows, NQH * HD)
+    return (assemble(pieces), attention)
+
+
 def solution(mesh):
     return jax.shard_map(
         local,

time: 78.1 us -> 60.7 us (0.78)
  blocking collectives: 33.2 us -> 0 us
  Pallas kernels: 0 us -> 22.8 us
  waiting for transfers between devices: 17.8 us -> 4.7 us
  starting transfers between devices: 13.1 us -> 25.3 us
  matrix products: 2.09 us -> 0 us
  local copies, waits for them, and re-layouts: 8.69 us -> 6.62 us
  other arithmetic: 1.83 us -> 0 us
    all_gather x1 -> x0, blocking collectives: 33.2 us -> none  [local(): gathered = lax.all_gather(queries, 'seq', axis=0, tiled=True)]
    pallas_call x0 -> x3, Pallas kernels: none -> 22.8 us  [the longest x1 17.1 us: assemble(): pl.pallas_call(functools.partial(assemble_kernel, count), out_shape=jax.S...]
    all_to_all x3 -> x2, waiting for transfers between devices: 17.8 us -> 0.01 us  [the longest x1 0.01 us: local(): lax.all_to_all(attended.reshape(seq_count, request_rows, group_width), 's...]
    ppermute x0 -> x7, starting transfers between devices: none -> 14.2 us  [local(): lax.ppermute(blocks[k], 'seq', [(i, i ^ k) for i in range(seq_count)])]
    ppermute x0 -> x7, waiting for transfers between devices: none -> 4.69 us  [local(): lax.ppermute(blocks[k], 'seq', [(i, i ^ k) for i in range(seq_count)])]
    another operation x5 -> x6, local copies, waits for them, and re-layouts: 2.85 us -> 0.45 us  [own(): return jnp.tile(mine, per_kv)[:, None]]
    unnamed x16 -> x37, local copies, waits for them, and re-layouts: 3.6 us -> 5.96 us
    dot_general x4 -> x0, matrix products: 2.09 us -> none  [the longest x1 0.82 us: local(): jnp.einsum('rhqd,rphd->rhqp', suffix_query, recent_keys, preferred_elemen...]
  transfers between devices with their start and end apart: 3 -> 9, of which waited for: 3 -> 3; matrix products, arithmetic and copies ran while one was open for 6% -> 1% of each run, Pallas kernels for 0% -> 38%
where the time goes in v1:
time: 60.7 us; the launch traced here: 60.3 us
  starting transfers between devices  25.3 us (42%)
  Pallas kernels  22.8 us (38%)
  local copies, waits for them, and re-layouts  6.62 us (11%)
  waiting for transfers between devices  4.7 us (8%)
  between operations  0.77 us (1%)
    pallas_call x1, Pallas kernels, assemble(): pl.pallas_call(functools.partial(assemble_kernel, count), out_shape=jax.S...  17.1 us
    ppermute x7, starting transfers between devices, local(): lax.ppermute(blocks[k], 'seq', [(i, i ^ k) for i in range(seq_count)])  14.2 us
    all_to_all x1, starting transfers between devices, local(): lax.all_to_all(queries.reshape(request_rows, seq_count, group_width).tran...  7.4 us
    unnamed x37, local copies, waits for them, and re-layouts  5.96 us
    ppermute x7, waiting for transfers between devices, local(): lax.ppermute(blocks[k], 'seq', [(i, i ^ k) for i in range(seq_count)])  4.69 us
    all_to_all x1, starting transfers between devices, local(): lax.all_to_all(attended.reshape(seq_count, request_rows, group_width), 's...  3.77 us
    pallas_call x1, Pallas kernels, attend(): pl.pallas_call(attend_kernel, out_shape=jax.ShapeDtypeStruct((requests, w...  3.65 us
    pallas_call x1, Pallas kernels, rotate_blocks(): pl.pallas_call(functools.partial(rotate_kernel, seq_count, core_count, pr...  2.06 us
  transfers between devices with their start and end apart: 9, of which 3 were waited for; matrix products, arithmetic and copies ran while one was open for 1% of the time, Pallas kernels for 38%

profile of v1, /device:TPU:0, one launch (start us, length us, event | category | flops | bytes accessed | tf_op | source)
XLA Modules:
  0.0 60.3 jit_solution(10366595374711780414)
XLA Ops:
  0.6 7.4 %all-to-all-start = ((bf16[8,8,512]{2,1,0:T(8,128)(2,1)}), bf16[8,8,512]{2,1,0:T(8,128)(2,1)S(1)}, u32[]{:S(2)}, u32[]{:S(2)}) async-start(bf16[8,8,512]{2,1,0:T(8,128)(2,1)} %bitcast.10), calls=%async_computation | async-start | bytes 131072 | tf_op jit(solution)/shard_map/all_to_all | solution.py:320
  8.0 2.1 %shard_map.104 = (bf16[2,64,256]{2,1,0:T(8,128)(2,1)}, bf16[2,64,256]{2,1,0:T(8,128)(2,1)}, bf16[2,64,256]{2,1,0:T(8,128)(2,1)}, bf16[2,64,256]{2,1,0:T(8,128)(2...) custom-call(f32[1,128]{1,0:T(1,128)} %constant.20.rates_ref, ...), custom_call_target="tpu_custom_call" | custom-call | flops 786432 | bytes 1048576 | tf_op jit(solution)/shard_map/pallas_call | solution.py:189
  10.1 2.0 %collective-permute-start = (bf16[2,64,256]{2,1,0:T(8,128)(2,1)}, bf16[2,64,256]{2,1,0:T(8,128)(2,1)S(1)}, u32[]{:S(2)}, u32[]{:S(2)}) collective-permute-start(bf16[2,64,256]{2,1,0:T(8,128)(2,1)} %get-tuple-element.11), channel_id=1, source_target_pairs={{0,2},{2,0},{4,6},{6,4},{8,10},{10,8},{12,14},{14,12},{1,3},{3,1},... | collective-permute-start | bytes 196616 | tf_op jit(solution)/shard_map/ppermute | solution.py:326
  12.1 1.5 %collective-permute-start.1 = (bf16[2,64,256]{2,1,0:T(8,128)(2,1)}, bf16[2,64,256]{2,1,0:T(8,128)(2,1)S(1)}, u32[]{:S(2)}, u32[]{:S(2)}) collective-permute-start(bf16[2,64,256]{2,1,0:T(8,128)(2,1)} %get-tuple-element.12), channel_id=1, source_target_pairs={{0,4},{2,6},{4,0},{6,2},{8,12},{10,14},{12,8},{14,10},{1,5},{3,7},... | collective-permute-start | bytes 196616 | tf_op jit(solution)/shard_map/ppermute | solution.py:326
  13.6 0.7 %copy-done.11 = s32[128]{0:T(128)S(1)} copy-done((s32[128]{0:T(128)S(1)}, s32[128]{0:T(128)}, u32[]{:S(2)}) %copy-start.11) | copy-done | bytes 536
  14.2 0.1 reshape.32
  14.3 0.6 copy-done.12
  14.9 0.1 reshape.33
  15.0 0.1 tile.14
  15.1 0.1 broadcast_in_dim_tile.8.assign_ref
  15.3 0.1 tile.16
  15.4 0.1 broadcast_in_dim_tile.9.lengths_ref
  15.5 0.0 copy-start
  15.5 1.2 %copy-done = bf16[1,1,64,32,256]{4,3,2,1,0:T(8,128)(2,1)S(1)} copy-done((bf16[1,1,64,32,256]{4,3,2,1,0:T(8,128)(2,1)S(1)}, bf16[1,1,64,32,256]{4,3,2,1,0:T(8,128)(2,1)}, u32[]{:S(2)}) %copy-start) | copy-done | bytes 1048600
  16.8 1.2 %copy-done.1 = bf16[1,1,64,32,256]{4,3,2,1,0:T(8,128)(2,1)S(1)} copy-done((bf16[1,1,64,32,256]{4,3,2,1,0:T(8,128)(2,1)S(1)}, bf16[1,1,64,32,256]{4,3,2,1,0:T(8,128)(2,1)}, u32[]{:S(2)}) %copy-start.1) | copy-done | bytes 1048600
  18.0 1.0 %copy-done.3 = bf16[1,1024,256]{2,1,0:T(8,128)(2,1)S(1)} copy-done((bf16[1,1024,256]{2,1,0:T(8,128)(2,1)S(1)}, bf16[1,1024,256]{2,1,0:T(8,128)(2,1)}, u32[]{:S(2)}) %copy-start.3) | copy-done | bytes 524312
  19.0 3.6 %shard_map.106 = bf16[64,512]{1,0:T(8,128)(2,1)} custom-call(bf16[64,512]{1,0:T(8,128)(2,1)S(1)} %bitcast.8, bf16[1,1024,256]{2,1,0:T(8,128)(2,1)S(1)} %copy-done.2, bf16[1,1024,256]{2,1,0:T(8,128)(2,1)S(1)} %copy-done.3, bf16[1,1,64,32,256]{4,3,2,1,0:T(8,128)(2,1)S(1)} %copy-done, bf16[1,1,64,32,256]{4,3,2,1,0:T(8,128)(2,1)S(1)} %copy-done.1, ...), custom_call_target="tpu_custom_call" | custom-call | flops 268435456 | bytes 3145728 | tf_op jit(solution)/shard_map/pallas_call | solution.py:297
  22.7 3.8 %all-to-all-start.1 = ((bf16[8,8,512]{2,1,0:T(8,128)(2,1)}), bf16[8,8,512]{2,1,0:T(8,128)(2,1)S(1)}, u32[]{:S(2)}, u32[]{:S(2)}) async-start(bf16[8,8,512]{2,1,0:T(8,128)(2,1)} %bitcast.3), calls=%async_computation.1 | async-start | bytes 131072 | tf_op jit(solution)/shard_map/all_to_all | solution.py:343
  26.5 2.9 %collective-permute-start.2 = (bf16[2,64,256]{2,1,0:T(8,128)(2,1)S(1)}, bf16[2,64,256]{2,1,0:T(8,128)(2,1)S(1)}, u32[]{:S(2)}, u32[]{:S(2)}) collective-permute-start(bf16[2,64,256]{2,1,0:T(8,128)(2,1)S(1)} %copy-done.17), channel_id=1, source_target_pairs={{0,6},{2,4},{4,2},{6,0},{8,14},{10,12},{12,10},{14,8},{1,7},{3,5},... | collective-permute-start | bytes 196616 | tf_op jit(solution)/shard_map/ppermute | solution.py:326
  29.4 2.4 %collective-permute-start.3 = (bf16[2,64,256]{2,1,0:T(8,128)(2,1)S(1)}, bf16[2,64,256]{2,1,0:T(8,128)(2,1)S(1)}, u32[]{:S(2)}, u32[]{:S(2)}) collective-permute-start(bf16[2,64,256]{2,1,0:T(8,128)(2,1)S(1)} %copy-done.16), channel_id=1, source_target_pairs={{0,8},{2,10},{4,12},{6,14},{8,0},{10,2},{12,4},{14,6},{1,9},{3,11}... | collective-permute-start | bytes 196616 | tf_op jit(solution)/shard_map/ppermute | solution.py:326
  31.7 0.6 collective-permute-start.4
  32.3 0.0 collective-permute-done.refs_1_
  32.3 2.4 %collective-permute-start.5 = (bf16[2,64,256]{2,1,0:T(8,128)(2,1)S(1)}, bf16[2,64,256]{2,1,0:T(8,128)(2,1)S(1)}, u32[]{:S(2)}, u32[]{:S(2)}) collective-permute-start(bf16[2,64,256]{2,1,0:T(8,128)(2,1)S(1)} %copy-done.14), channel_id=1, source_target_pairs={{0,12},{2,14},{4,8},{6,10},{8,4},{10,6},{12,0},{14,2},{1,13},{3,15... | collective-permute-start | bytes 196616 | tf_op jit(solution)/shard_map/ppermute | solution.py:326
  34.7 2.4 %collective-permute-start.6 = (bf16[2,64,256]{2,1,0:T(8,128)(2,1)S(1)}, bf16[2,64,256]{2,1,0:T(8,128)(2,1)S(1)}, u32[]{:S(2)}, u32[]{:S(2)}) collective-permute-start(bf16[2,64,256]{2,1,0:T(8,128)(2,1)S(1)} %copy-done.13), channel_id=1, source_target_pairs={{0,14},{2,12},{4,10},{6,8},{8,6},{10,4},{12,2},{14,0},{1,15},{3,13... | collective-permute-start | bytes 196616 | tf_op jit(solution)/shard_map/ppermute | solution.py:326
  37.2 1.7 %collective-permute-done.3.refs_4_ = bf16[2,64,256]{2,1,0:T(8,128)(2,1)S(1)} collective-permute-done((bf16[2,64,256]{2,1,0:T(8,128)(2,1)S(1)}, bf16[2,64,256]{2,1,0:T(8,128)(2,1)S(1)}, u32[]{:S(2)}, u32[]{:S(2)}) %collective-permute-start.3) | collective-permute-done | bytes 65568 | tf_op jit(solution)/shard_map/ppermute | solution.py:326
  38.8 2.0 %collective-permute-done.4.refs_5_ = bf16[2,64,256]{2,1,0:T(8,128)(2,1)S(1)} collective-permute-done((bf16[2,64,256]{2,1,0:T(8,128)(2,1)S(1)}, bf16[2,64,256]{2,1,0:T(8,128)(2,1)S(1)}, u32[]{:S(2)}, u32[]{:S(2)}) %collective-permute-start.4) | collective-permute-done | bytes 65568 | tf_op jit(solution)/shard_map/ppermute | solution.py:326
  40.8 0.0 collective-permute-done.5.refs_6_
  40.8 1.0 %collective-permute-done.6.refs_7_ = bf16[2,64,256]{2,1,0:T(8,128)(2,1)S(1)} collective-permute-done((bf16[2,64,256]{2,1,0:T(8,128)(2,1)S(1)}, bf16[2,64,256]{2,1,0:T(8,128)(2,1)S(1)}, u32[]{:S(2)}, u32[]{:S(2)}) %collective-permute-start.6) | collective-permute-done | bytes 65568 | tf_op jit(solution)/shard_map/ppermute | solution.py:326
  41.9 0.6 copy-done.10
  42.5 17.1 %shard_map.105 = bf16[2,1,8,64,256]{4,3,2,1,0:T(8,128)(2,1)} custom-call(bf16[2,64,256]{2,1,0:T(8,128)(2,1)} %get-tuple-element.10.refs_0_, bf16[2,64,256]{2,1,0:T(8,128)(2,1)} %copy-done.4, bf16[2,64,256]{2,1,0:T(8,128)(2,1)} %copy-done.5, bf16[2,64,256]{2,1,0:T(8,128)(2,1)} %copy-done.6, bf16[2,64,256]{2,1,0:T(8,128)(2,1)} %copy-done.7, ...), custom_call_target="tpu_custom_call" | custom-call | bytes 1048576 | tf_op jit(solution)/shard_map/pallas_call | solution.py:219
  59.6 0.0 all-to-all-done.1
  59.6 0.6 %copy.14 = bf16[8,4096]{1,0:T(8,128)(2,1)} copy(bf16[8,4096]{1,0:T(8,128)(2,1)S(1)} %bitcast.9) | data formatting | bytes 131072
  (35 shorter events, 0.1 us)
Async XLA Ops:
  0.6 14.9 %copy-start.2 = (bf16[1,1024,256]{2,1,0:T(8,128)(2,1)S(1)}, bf16[1,1024,256]{2,1,0:T(8,128)(2,1)}, u32[]{:S(2)}) copy-start(bf16[1,1024,256]{2,1,0:T(8,128)(2,1)} %keys_ref.1) | copy-start | bytes 1572868
  0.6 14.9 %all-to-all-start = ((bf16[8,8,512]{2,1,0:T(8,128)(2,1)}), bf16[8,8,512]{2,1,0:T(8,128)(2,1)S(1)}, u32[]{:S(2)}, u32[]{:S(2)}) async-start(bf16[8,8,512]{2,1,0:T(8,128)(2,1)} %bitcast.10), calls=%async_computation | async-start | bytes 131072 | tf_op jit(solution)/shard_map/all_to_all | solution.py:320
  10.1 22.2 %collective-permute-start = (bf16[2,64,256]{2,1,0:T(8,128)(2,1)}, bf16[2,64,256]{2,1,0:T(8,128)(2,1)S(1)}, u32[]{:S(2)}, u32[]{:S(2)}) collective-permute-start(bf16[2,64,256]{2,1,0:T(8,128)(2,1)} %get-tuple-element.11), channel_id=1, source_target_pairs={{0,2},{2,0},{4,6},{6,4},{8,10},{10,8},{12,14},{14,12},{1,3},{3,1},... | collective-permute-start | bytes 196616 | tf_op jit(solution)/shard_map/ppermute | solution.py:326
  12.1 22.6 %collective-permute-start.1 = (bf16[2,64,256]{2,1,0:T(8,128)(2,1)}, bf16[2,64,256]{2,1,0:T(8,128)(2,1)S(1)}, u32[]{:S(2)}, u32[]{:S(2)}) collective-permute-start(bf16[2,64,256]{2,1,0:T(8,128)(2,1)} %get-tuple-element.12), channel_id=1, source_target_pairs={{0,4},{2,6},{4,0},{6,2},{8,12},{10,14},{12,8},{14,10},{1,5},{3,7},... | collective-permute-start | bytes 196616 | tf_op jit(solution)/shard_map/ppermute | solution.py:326
  13.6 0.7 %copy-start.11 = (s32[128]{0:T(128)S(1)}, s32[128]{0:T(128)}, u32[]{:S(2)}) copy-start(s32[128]{0:T(128)} %param.16) | copy-start | bytes 1540
  14.2 0.7 %copy-start.12 = (s32[128]{0:T(128)S(1)}, s32[128]{0:T(128)}, u32[]{:S(2)}) copy-start(s32[128]{0:T(128)} %param.15) | copy-start | bytes 1540
  15.5 1.2 %copy-start = (bf16[1,1,64,32,256]{4,3,2,1,0:T(8,128)(2,1)S(1)}, bf16[1,1,64,32,256]{4,3,2,1,0:T(8,128)(2,1)}, u32[]{:S(2)}) copy-start(bf16[1,1,64,32,256]{4,3,2,1,0:T(8,128)(2,1)} %skeys_ref.1) | copy-start | bytes 3145732
  16.7 1.2 %copy-start.1 = (bf16[1,1,64,32,256]{4,3,2,1,0:T(8,128)(2,1)S(1)}, bf16[1,1,64,32,256]{4,3,2,1,0:T(8,128)(2,1)}, u32[]{:S(2)}) copy-start(bf16[1,1,64,32,256]{4,3,2,1,0:T(8,128)(2,1)} %svalues_ref.1) | copy-start | bytes 3145732
  18.0 1.0 %copy-start.3 = (bf16[1,1024,256]{2,1,0:T(8,128)(2,1)S(1)}, bf16[1,1024,256]{2,1,0:T(8,128)(2,1)}, u32[]{:S(2)}) copy-start(bf16[1,1024,256]{2,1,0:T(8,128)(2,1)} %values_ref.1) | copy-start | bytes 1572868
  19.0 7.4 %copy-start.17 = (bf16[2,64,256]{2,1,0:T(8,128)(2,1)S(1)}, bf16[2,64,256]{2,1,0:T(8,128)(2,1)}, u32[]{:S(2)}) copy-start(bf16[2,64,256]{2,1,0:T(8,128)(2,1)} %get-tuple-element.13) | copy-start | bytes 196612
  19.0 10.4 %copy-start.16 = (bf16[2,64,256]{2,1,0:T(8,128)(2,1)S(1)}, bf16[2,64,256]{2,1,0:T(8,128)(2,1)}, u32[]{:S(2)}) copy-start(bf16[2,64,256]{2,1,0:T(8,128)(2,1)} %get-tuple-element.14) | copy-start | bytes 196612
  19.0 12.7 %copy-start.15 = (bf16[2,64,256]{2,1,0:T(8,128)(2,1)S(1)}, bf16[2,64,256]{2,1,0:T(8,128)(2,1)}, u32[]{:S(2)}) copy-start(bf16[2,64,256]{2,1,0:T(8,128)(2,1)} %get-tuple-element.15) | copy-start | bytes 196612
  22.7 9.6 %copy-start.14 = (bf16[2,64,256]{2,1,0:T(8,128)(2,1)S(1)}, bf16[2,64,256]{2,1,0:T(8,128)(2,1)}, u32[]{:S(2)}) copy-start(bf16[2,64,256]{2,1,0:T(8,128)(2,1)} %get-tuple-element.16) | copy-start | bytes 196612
  22.7 12.1 %copy-start.13 = (bf16[2,64,256]{2,1,0:T(8,128)(2,1)S(1)}, bf16[2,64,256]{2,1,0:T(8,128)(2,1)}, u32[]{:S(2)}) copy-start(bf16[2,64,256]{2,1,0:T(8,128)(2,1)} %get-tuple-element.17) | copy-start | bytes 196612
  22.7 36.9 %all-to-all-start.1 = ((bf16[8,8,512]{2,1,0:T(8,128)(2,1)}), bf16[8,8,512]{2,1,0:T(8,128)(2,1)S(1)}, u32[]{:S(2)}, u32[]{:S(2)}) async-start(bf16[8,8,512]{2,1,0:T(8,128)(2,1)} %bitcast.3), calls=%async_computation.1 | async-start | bytes 131072 | tf_op jit(solution)/shard_map/all_to_all | solution.py:343
  26.5 10.7 %collective-permute-start.2 = (bf16[2,64,256]{2,1,0:T(8,128)(2,1)S(1)}, bf16[2,64,256]{2,1,0:T(8,128)(2,1)S(1)}, u32[]{:S(2)}, u32[]{:S(2)}) collective-permute-start(bf16[2,64,256]{2,1,0:T(8,128)(2,1)S(1)} %copy-done.17), channel_id=1, source_target_pairs={{0,6},{2,4},{4,2},{6,0},{8,14},{10,12},{12,10},{14,8},{1,7},{3,5},... | collective-permute-start | bytes 196616 | tf_op jit(solution)/shard_map/ppermute | solution.py:326
  29.4 9.5 %collective-permute-start.3 = (bf16[2,64,256]{2,1,0:T(8,128)(2,1)S(1)}, bf16[2,64,256]{2,1,0:T(8,128)(2,1)S(1)}, u32[]{:S(2)}, u32[]{:S(2)}) collective-permute-start(bf16[2,64,256]{2,1,0:T(8,128)(2,1)S(1)} %copy-done.16), channel_id=1, source_target_pairs={{0,8},{2,10},{4,12},{6,14},{8,0},{10,2},{12,4},{14,6},{1,9},{3,11}... | collective-permute-start | bytes 196616 | tf_op jit(solution)/shard_map/ppermute | solution.py:326
  31.7 9.1 %collective-permute-start.4 = (bf16[2,64,256]{2,1,0:T(8,128)(2,1)S(1)}, bf16[2,64,256]{2,1,0:T(8,128)(2,1)S(1)}, u32[]{:S(2)}, u32[]{:S(2)}) collective-permute-start(bf16[2,64,256]{2,1,0:T(8,128)(2,1)S(1)} %copy-done.15), channel_id=1, source_target_pairs={{0,10},{2,8},{4,14},{6,12},{8,2},{10,0},{12,6},{14,4},{1,11},{3,9}... | collective-permute-start | bytes 196616 | tf_op jit(solution)/shard_map/ppermute | solution.py:326
  32.3 9.6 %copy-start.4 = (bf16[2,64,256]{2,1,0:T(8,128)(2,1)}, bf16[2,64,256]{2,1,0:T(8,128)(2,1)S(1)}, u32[]{:S(2)}) copy-start(bf16[2,64,256]{2,1,0:T(8,128)(2,1)S(1)} %collective-permute-done.refs_1_) | copy-start | bytes 196612
  32.3 8.5 %collective-permute-start.5 = (bf16[2,64,256]{2,1,0:T(8,128)(2,1)S(1)}, bf16[2,64,256]{2,1,0:T(8,128)(2,1)S(1)}, u32[]{:S(2)}, u32[]{:S(2)}) collective-permute-start(bf16[2,64,256]{2,1,0:T(8,128)(2,1)S(1)} %copy-done.14), channel_id=1, source_target_pairs={{0,12},{2,14},{4,8},{6,10},{8,4},{10,6},{12,0},{14,2},{1,13},{3,15... | collective-permute-start | bytes 196616 | tf_op jit(solution)/shard_map/ppermute | solution.py:326
  34.7 7.1 %copy-start.5 = (bf16[2,64,256]{2,1,0:T(8,128)(2,1)}, bf16[2,64,256]{2,1,0:T(8,128)(2,1)S(1)}, u32[]{:S(2)}) copy-start(bf16[2,64,256]{2,1,0:T(8,128)(2,1)S(1)} %collective-permute-done.1.refs_2_) | copy-start | bytes 196612
  34.7 7.1 %collective-permute-start.6 = (bf16[2,64,256]{2,1,0:T(8,128)(2,1)S(1)}, bf16[2,64,256]{2,1,0:T(8,128)(2,1)S(1)}, u32[]{:S(2)}, u32[]{:S(2)}) collective-permute-start(bf16[2,64,256]{2,1,0:T(8,128)(2,1)S(1)} %copy-done.13), channel_id=1, source_target_pairs={{0,14},{2,12},{4,10},{6,8},{8,6},{10,4},{12,2},{14,0},{1,15},{3,13... | collective-permute-start | bytes 196616 | tf_op jit(solution)/shard_map/ppermute | solution.py:326
  37.2 4.7 %copy-start.6 = (bf16[2,64,256]{2,1,0:T(8,128)(2,1)}, bf16[2,64,256]{2,1,0:T(8,128)(2,1)S(1)}, u32[]{:S(2)}) copy-start(bf16[2,64,256]{2,1,0:T(8,128)(2,1)S(1)} %collective-permute-done.2.refs_3_) | copy-start | bytes 196612
  38.8 3.0 %copy-start.7 = (bf16[2,64,256]{2,1,0:T(8,128)(2,1)}, bf16[2,64,256]{2,1,0:T(8,128)(2,1)S(1)}, u32[]{:S(2)}) copy-start(bf16[2,64,256]{2,1,0:T(8,128)(2,1)S(1)} %collective-permute-done.3.refs_4_) | copy-start | bytes 196612
  40.8 1.0 %copy-start.8 = (bf16[2,64,256]{2,1,0:T(8,128)(2,1)}, bf16[2,64,256]{2,1,0:T(8,128)(2,1)S(1)}, u32[]{:S(2)}) copy-start(bf16[2,64,256]{2,1,0:T(8,128)(2,1)S(1)} %collective-permute-done.4.refs_5_) | copy-start | bytes 196612
  40.8 1.1 %copy-start.9 = (bf16[2,64,256]{2,1,0:T(8,128)(2,1)}, bf16[2,64,256]{2,1,0:T(8,128)(2,1)S(1)}, u32[]{:S(2)}) copy-start(bf16[2,64,256]{2,1,0:T(8,128)(2,1)S(1)} %collective-permute-done.5.refs_6_) | copy-start | bytes 196612
  41.9 0.6 %copy-start.10 = (bf16[2,64,256]{2,1,0:T(8,128)(2,1)}, bf16[2,64,256]{2,1,0:T(8,128)(2,1)S(1)}, u32[]{:S(2)}) copy-start(bf16[2,64,256]{2,1,0:T(8,128)(2,1)S(1)} %collective-permute-done.6.refs_7_) | copy-start | bytes 196612

commit v2 on v0

--- a/solution.py
+++ b/solution.py
@@ -1,8 +1,12 @@
+import functools
 import math
 
 import jax
 import jax.numpy as jnp
+import numpy as np
 from jax import lax
+from jax.experimental import pallas as pl
+from jax.experimental.pallas import tpu as pltpu
 from jax.sharding import PartitionSpec as P
 
 HD = 128
@@ -30,7 +34,7 @@
     return softcap * jnp.tanh(scores * query_scale / softcap)
 
 
-def local(new_kv, old_keys, old_values, suffix_keys, suffix_values, queries, lengths, assign):
+def general(new_kv, old_keys, old_values, suffix_keys, suffix_values, queries, lengths, assign):
     seq_count = lax.axis_size("seq")
     core_count = lax.axis_size("pd")
     seq_place = lax.axis_index("seq")
@@ -157,6 +161,221 @@
     return (new_cache, attention.astype(jnp.bfloat16))
 
 
+def weigh(scores):
+    return jnp.exp2((softcap * math.log2(math.e)) * jnp.tanh(scores * (query_scale / softcap)))
+
+
+NT = (((1,), (1,)), ((), ()))
+NN = (((1,), (0,)), ((), ()))
+
+
+def pin(x, space=pltpu.VMEM):
+    return pltpu.with_memory_space_constraint(x, space)
+
+
+VMEM = pl.BlockSpec(memory_space=pltpu.VMEM)
+HBM = pl.BlockSpec(memory_space=pltpu.HBM)
+WIDE = 128
+
+
+def turns(count):
+    return [*range(count // 2, count), *range(1, count // 2), 0]
+
+
+def prepare_kernel(count, core_count, prefix_length, request_rows, rates_ref, stored_assign, stored_lengths, stored_kv, *refs):
+    stored, refs = refs[:4], refs[4:]
+    blocks, refs = refs[:count], refs[count:]
+    which_ref, live_ref, *fetched, kv_ref, cut_ref, assign_ref, lengths_ref, sems, out_sems = refs
+    first_copies = [
+        pltpu.make_async_copy(stored_kv, kv_ref, sems.at[4]),
+        pltpu.make_async_copy(stored_assign, assign_ref, sems.at[5]),
+        pltpu.make_async_copy(stored_lengths, lengths_ref, sems.at[6]),
+    ]
+    for copy in first_copies:
+        copy.start()
+    copies = [pltpu.make_async_copy(a, b, sems.at[i]) for i, (a, b) in enumerate(zip(stored, fetched))]
+    for copy in copies:
+        copy.start()
+    place = lax.axis_index("seq")
+    rows = kv_ref.shape[1]
+    width = kv_ref.shape[2] // count
+    first = (place * core_count + lax.axis_index("pd")) * rows
+    position = (first + lax.broadcasted_iota(jnp.int32, (rows, HD), 0)) % prefix_length
+    angles = position.astype(jnp.float32) * rates_ref[...]
+    cosine = jnp.cos(angles)
+    sine = jnp.sin(angles)
+    sine = jnp.where(lax.broadcasted_iota(jnp.int32, (rows, HD), 1) < HD // 2, -sine, sine)
+    for copy in first_copies:
+        copy.wait()
+    for slot, k in enumerate(turns(count)):
+        start = jnp.bitwise_xor(place, k) * width
+        for h in range(width // HD):
+            columns = pl.ds(pl.multiple_of(start + h * HD, HD), HD)
+            keys = kv_ref[0, :, columns].astype(jnp.float32)
+            turned = pltpu.roll(keys, HD // 2, 1)
+            cut = blocks[slot] if k == 0 else cut_ref.at[slot]
+            cut[0, :, h * HD : (h + 1) * HD] = (keys * cosine + turned * sine).astype(jnp.bfloat16)
+            cut[1, :, h * HD : (h + 1) * HD] = kv_ref[1, :, columns]
+        if k:
+            copies.append(pltpu.make_async_copy(cut_ref.at[slot], blocks[slot], out_sems.at[slot]))
+            copies[-1].start()
+    tall = which_ref.shape[0]
+    which_ref[...] = jnp.broadcast_to(own_column(assign_ref, tall, request_rows, core_count), which_ref.shape)
+    live_ref[...] = jnp.broadcast_to(own_column(lengths_ref, tall, request_rows, core_count), live_ref.shape)
+    for copy in copies:
+        copy.wait()
+
+
+def own_column(values_ref, tall, request_rows, core_count):
+    shape = (tall, values_ref.shape[1])
+    row = lax.broadcasted_iota(jnp.int32, shape, 0) % (values_ref.shape[1] // core_count)
+    wanted = (row // request_rows * core_count + lax.axis_index("pd")) * request_rows + row % request_rows
+    picked = jnp.where(lax.broadcasted_iota(jnp.int32, shape, 1) == wanted, values_ref[...], 0)
+    return jnp.sum(picked.astype(jnp.float32), axis=1, keepdims=True).astype(jnp.int32)
+
+
+def attend_kernel(q_ref, keys_ref, values_ref, skeys_ref, svalues_ref, which_ref, live_ref, out_ref):
+    seq_count, span, group_width = q_ref.shape
+    requests = seq_count * span
+    per_kv = NQH // KVH
+    heads_here = keys_ref.shape[2] // HD
+    length = keys_ref.shape[1] // NPFX
+    slots = skeys_ref.shape[3]
+    queries = q_ref[...].reshape(requests, group_width)
+    column = lax.broadcasted_iota(jnp.int32, (span * per_kv, span * slots), 1)
+    low = lax.broadcasted_iota(jnp.int32, (span * per_kv, span * slots), 0) % span * slots
+    for h in range(heads_here):
+        columns = slice(h * HD, (h + 1) * HD)
+        query = jnp.concatenate(
+            [queries[:, (h * per_kv + j) * HD : (h * per_kv + j + 1) * HD] for j in range(per_kv)], axis=0
+        )
+        query32 = query.astype(jnp.float32)
+        picked = [
+            [slice(j * requests + b * span, j * requests + (b + 1) * span) for j in range(per_kv)]
+            for b in range(seq_count)
+        ]
+        added, more = [], []
+        for b in range(seq_count):
+            part = jnp.concatenate([query32[rows] for rows in picked[b]], axis=0).astype(jnp.bfloat16)
+            skeys = skeys_ref[0, 0, b * span : (b + 1) * span, :, columns].reshape(span * slots, HD)
+            svalues = svalues_ref[0, 0, b * span : (b + 1) * span, :, columns].reshape(span * slots, HD)
+            recent = weigh(lax.dot_general(part, skeys, NT, preferred_element_type=jnp.float32))
+            live = jnp.concatenate([live_ref[rows, :1] for rows in picked[b]], axis=0)
+            recent = jnp.where((column >= low) & (column < low + live), recent, 0.0)
+            more.append(jnp.sum(recent, axis=1, keepdims=True))
+            added.append(lax.dot_general(recent.astype(jnp.bfloat16), svalues, NN, preferred_element_type=jnp.float32))
+        scores = lax.dot_general(query, keys_ref[0, :length, columns], NT, preferred_element_type=jnp.float32)
+        for p in range(1, NPFX):
+            other = lax.dot_general(
+                query, keys_ref[0, p * length : (p + 1) * length, columns], NT, preferred_element_type=jnp.float32
+            )
+            scores = jnp.where(which_ref[:, :1] == p, other, scores)
+        weights = weigh(scores)
+        total = jnp.sum(weights, axis=1, keepdims=True)
+        rounded = weights.astype(jnp.bfloat16)
+        numerator = jnp.dot(rounded, values_ref[0, :length, columns], preferred_element_type=jnp.float32)
+        for p in range(1, NPFX):
+            other = jnp.dot(
+                rounded, values_ref[0, p * length : (p + 1) * length, columns], preferred_element_type=jnp.float32
+            )
+            numerator = jnp.where(which_ref[...] == p, other, numerator)
+
+        def regroup(parts):
+            return jnp.concatenate(
+                [parts[b][j * span : (j + 1) * span] for j in range(per_kv) for b in range(seq_count)], axis=0
+            )
+
+        result = (numerator + regroup(added)) * (1.0 / (total + regroup(more)))
+        for j in range(per_kv):
+            head = h * per_kv + j
+            out_ref[:, :, head * HD : (head + 1) * HD] = result[j * requests : (j + 1) * requests].reshape(
+                seq_count, span, HD
+            ).astype(jnp.bfloat16)
+
+
+def finish_kernel(count, back_ref, *refs):
+    *pieces, cache_ref, attention_ref, sems = refs
+    place = lax.axis_index("seq")
+    copies = [
+        pltpu.make_async_copy(piece, cache_ref.at[:, 0, jnp.bitwise_xor(place, k)], sems.at[k])
+        for k, piece in zip(turns(count), pieces)
+    ]
+    for copy in copies:
+        copy.start()
+    width = back_ref.shape[2]
+    for s in range(count):
+        attention_ref[:, s * width : (s + 1) * width] = back_ref[s]
+    for copy in copies:
+        copy.wait()
+
+
+def local(new_kv, old_keys, old_values, suffix_keys, suffix_values, queries, lengths, assign):
+    seq_count = lax.axis_size("seq")
+    core_count = lax.axis_size("pd")
+    if seq_count > KVH or seq_count & (seq_count - 1):
+        return general(new_kv, old_keys, old_values, suffix_keys, suffix_values, queries, lengths, assign)
+    request_rows = queries.shape[0]
+    prefix_rows = new_kv.shape[1]
+    group_width = queries.shape[1] // seq_count
+    width = new_kv.shape[2] // seq_count
+    tall = NQH // KVH * seq_count * request_rows
+    prefix_length = prefix_rows * seq_count * core_count // NPFX
+    rates = (10000.0 ** (-2.0 * (np.arange(HD) % (HD // 2)) / HD)).astype(np.float32)
+    asked = lax.all_to_all(
+        queries.reshape(request_rows, seq_count, group_width).transpose(1, 0, 2), "seq", 0, 0, tiled=True
+    )
+    stored = (old_keys, old_values, suffix_keys, suffix_values)
+    block = pltpu.HBM((2, prefix_rows, width), jnp.bfloat16)
+    mine = jax.ShapeDtypeStruct((2, prefix_rows, width), jnp.bfloat16)
+    column = jax.ShapeDtypeStruct((tall, WIDE), jnp.int32)
+    prepared = pl.pallas_call(
+        functools.partial(prepare_kernel, seq_count, core_count, prefix_length, request_rows),
+        out_shape=[block] * (seq_count - 1) + [mine] + [column] * 2 + [jax.ShapeDtypeStruct(x.shape, x.dtype) for x in stored],
+        in_specs=[VMEM] + [HBM] * 7,
+        out_specs=[HBM] * (seq_count - 1) + [VMEM] * 7,
+        scratch_shapes=[
+            pltpu.VMEM(new_kv.shape, jnp.bfloat16),
+            pltpu.VMEM((seq_count - 1, 2, prefix_rows, width), jnp.bfloat16),
+            pltpu.VMEM((1, assign.shape[0]), jnp.int32),
+            pltpu.VMEM((1, assign.shape[0]), jnp.int32),
+            pltpu.SemaphoreType.DMA((7,)),
+            pltpu.SemaphoreType.DMA((seq_count - 1,)),
+        ],
+        cost_estimate=pl.CostEstimate(flops=1000, bytes_accessed=1000, transcendentals=0),
+        compiler_params=pltpu.CompilerParams(vmem_limit_bytes=24 * 2**20),
+    )(
+        jnp.asarray(rates).reshape(1, HD),
+        *(pin(x, pltpu.HBM) for x in (assign.reshape(1, -1), lengths.reshape(1, -1), new_kv, *stored)),
+    )
+    blocks, (which, live, *fetched) = prepared[:seq_count], prepared[seq_count:]
+    pieces = [
+        lax.ppermute(block, "seq", [(i, i ^ k) for i in range(seq_count)]) if k else block
+        for k, block in zip(turns(seq_count), blocks)
+    ]
+    attended = pl.pallas_call(
+        attend_kernel,
+        out_shape=jax.ShapeDtypeStruct((seq_count, request_rows, group_width), jnp.bfloat16),
+        in_specs=[VMEM] * 7,
+        out_specs=VMEM,
+        compiler_params=pltpu.CompilerParams(vmem_limit_bytes=16 * 2**20),
+        cost_estimate=pl.CostEstimate(flops=2**20, bytes_accessed=2**20, transcendentals=2**10),
+    )(pin(asked), *(pin(x) for x in fetched), pin(which), pin(live))
+    back = lax.all_to_all(attended, "seq", 0, 0, tiled=True)
+    return tuple(
+        pl.pallas_call(
+            functools.partial(finish_kernel, seq_count),
+            out_shape=(
+                jax.ShapeDtypeStruct((2, 1, seq_count, prefix_rows, width), jnp.bfloat16),
+                jax.ShapeDtypeStruct((request_rows, NQH * HD), jnp.bfloat16),
+            ),
+            in_specs=[VMEM] * (seq_count + 1),
+            out_specs=(HBM, VMEM),
+            scratch_shapes=[pltpu.SemaphoreType.DMA((seq_count,))],
+            cost_estimate=pl.CostEstimate(flops=0, bytes_accessed=2**20, transcendentals=0),
+        )(pin(back), *(pin(piece) for piece in pieces))
+    )
+
+
 def solution(mesh):
     return jax.shard_map(
         local,

time: 78.1 us -> 37.9 us (0.49)
  blocking collectives: 33.2 us -> 0 us
  waiting for transfers between devices: 17.8 us -> 3.63 us
  starting transfers between devices: 13.1 us -> 25.2 us
  local copies, waits for them, and re-layouts: 8.69 us -> 0.66 us
  Pallas kernels: 0 us -> 7.44 us
  matrix products: 2.09 us -> 0 us
  other arithmetic: 1.83 us -> 0 us
    all_gather x1 -> x0, blocking collectives: 33.2 us -> none  [local(): gathered = lax.all_gather(queries, 'seq', axis=0, tiled=True)]
    all_to_all x3 -> x2, waiting for transfers between devices: 17.8 us -> 0.01 us  [the longest x1 0.01 us: local(): lax.all_to_all(queries.reshape(request_rows, seq_count, group_width).tran...]
    ppermute x0 -> x7, starting transfers between devices: none -> 13.2 us  [local(): lax.ppermute(block, 'seq', [(i, i ^ k) for i in range(seq_count)])]
    pallas_call x0 -> x3, Pallas kernels: none -> 7.44 us  [the longest x1 3.77 us: local(): pl.pallas_call(attend_kernel, out_shape=jax.ShapeDtypeStruct((seq_count,...]
    ppermute x0 -> x7, waiting for transfers between devices: none -> 3.62 us  [local(): lax.ppermute(block, 'seq', [(i, i ^ k) for i in range(seq_count)])]
    unnamed x16 -> x6, local copies, waits for them, and re-layouts: 3.6 us -> 0.66 us
    another operation x5 -> x0, local copies, waits for them, and re-layouts: 2.85 us -> none  [the longest x1 1.4 us: local(): recent_keys = suffix_keys[0, 0].reshape(suffix_rows, -1, heads_here, HD)]
    dot_general x4 -> x0, matrix products: 2.09 us -> none  [the longest x1 0.82 us: local(): jnp.einsum('rhqd,rphd->rhqp', suffix_query, recent_keys, preferred_elemen...]
  transfers between devices with their start and end apart: 3 -> 9, of which waited for: 3 -> 2; matrix products, arithmetic and copies ran while one was open for 6% -> 0% of each run, Pallas kernels for 0% -> 16%
where the time goes in v2:
time: 37.9 us; the launch traced here: 37.5 us
  starting transfers between devices  25.2 us (66%)
  Pallas kernels  7.44 us (20%)
  waiting for transfers between devices  3.63 us (10%)
  local copies, waits for them, and re-layouts  0.66 us (2%)
  between operations  0.65 us (2%)
    ppermute x7, starting transfers between devices, local(): lax.ppermute(block, 'seq', [(i, i ^ k) for i in range(seq_count)])  13.2 us
    all_to_all x1, starting transfers between devices, local(): lax.all_to_all(queries.reshape(request_rows, seq_count, group_width).tran...  7.26 us
    all_to_all x1, starting transfers between devices, local(): back = lax.all_to_all(attended, 'seq', 0, 0, tiled=True)  4.67 us
    pallas_call x1, Pallas kernels, local(): pl.pallas_call(attend_kernel, out_shape=jax.ShapeDtypeStruct((seq_count,...  3.77 us
    ppermute x7, waiting for transfers between devices, local(): lax.ppermute(block, 'seq', [(i, i ^ k) for i in range(seq_count)])  3.62 us
    pallas_call x1, Pallas kernels, local(): pl.pallas_call(functools.partial(prepare_kernel, seq_count, core_count, p...  2.19 us
    pallas_call x1, Pallas kernels, local(): pl.pallas_call(functools.partial(finish_kernel, seq_count), out_shape=(ja...  1.48 us
  transfers between devices with their start and end apart: 9, of which 2 were waited for; matrix products, arithmetic and copies ran while one was open for 0% of the time, Pallas kernels for 16%

profile of v2, /device:TPU:0, one launch (start us, length us, event | category | flops | bytes accessed | tf_op | source)
XLA Modules:
  0.0 37.5 jit_solution(5076542631136310861)
XLA Ops:
  0.6 7.3 %all-to-all-start = ((bf16[8,8,512]{2,1,0:T(8,128)(2,1)}), bf16[8,8,512]{2,1,0:T(8,128)(2,1)S(1)}, u32[]{:S(2)}, u32[]{:S(2)}) async-start(bf16[8,8,512]{2,1,0:T(8,128)(2,1)} %bitcast.5), calls=%async_computation | async-start | bytes 131072 | tf_op jit(solution)/shard_map/all_to_all | solution.py:324
  7.9 0.0 copy-start
  7.9 0.7 %copy-done = f32[1,128]{1,0:T(1,128)S(1)} copy-done((f32[1,128]{1,0:T(1,128)S(1)}, f32[1,128]{1,0:T(1,128)}, u32[]{:S(2)}) %copy-start) | copy-done | bytes 536
  8.6 2.2 %shard_map.104 = (bf16[2,64,256]{2,1,0:T(8,128)(2,1)}, bf16[2,64,256]{2,1,0:T(8,128)(2,1)}, bf16[2,64,256]{2,1,0:T(8,128)(2,1)}, bf16[2,64,256]{2,1,0:T(8,128)(2...) custom-call(f32[1,128]{1,0:T(1,128)S(1)} %copy-done, ...), custom_call_target="tpu_custom_call" | custom-call | flops 1000 | bytes 1000 | tf_op jit(solution)/shard_map/pallas_call | solution.py:331
  10.7 3.0 %collective-permute-start = (bf16[2,64,256]{2,1,0:T(8,128)(2,1)}, bf16[2,64,256]{2,1,0:T(8,128)(2,1)S(1)}, u32[]{:S(2)}, u32[]{:S(2)}) collective-permute-start(bf16[2,64,256]{2,1,0:T(8,128)(2,1)} %get-tuple-element.22), channel_id=1, source_target_pairs={{0,8},{2,10},{4,12},{6,14},{8,0},{10,2},{12,4},{14,6},{1,9},{3,11}... | collective-permute-start | bytes 196616 | tf_op jit(solution)/shard_map/ppermute | solution.py:352
  13.7 1.5 %collective-permute-start.1 = (bf16[2,64,256]{2,1,0:T(8,128)(2,1)}, bf16[2,64,256]{2,1,0:T(8,128)(2,1)S(1)}, u32[]{:S(2)}, u32[]{:S(2)}) collective-permute-start(bf16[2,64,256]{2,1,0:T(8,128)(2,1)} %get-tuple-element.23), channel_id=1, source_target_pairs={{0,10},{2,8},{4,14},{6,12},{8,2},{10,0},{12,6},{14,4},{1,11},{3,9}... | collective-permute-start | bytes 196616 | tf_op jit(solution)/shard_map/ppermute | solution.py:352
  15.2 0.0 all-to-all-done.q_ref
  15.2 3.8 %shard_map.105 = bf16[8,8,512]{2,1,0:T(8,128)(2,1)} custom-call(bf16[8,8,512]{2,1,0:T(8,128)(2,1)S(1)} %all-to-all-done.q_ref, bf16[1,1024,256]{2,1,0:T(8,128)(2,1)S(1)} %get-tuple-element.16.keys_ref, bf16[1,1024,256]{2,1,0:T(8,128)(2,1)S(1)} %get-tuple-element.17.values_ref, bf16[1,1,64,32,256]{4,3,2,1,0:T(8,128)(2,1)S(1)} %get-tuple-element.18.skeys_ref, ...), custom_call_target="tpu_custom_call" | custom-call | flops 1048576 | bytes 1048576 | tf_op jit(solution)/shard_map/pallas_call | solution.py:355
  19.0 0.0 copy-start.2
  19.0 0.0 copy-start.1
  19.0 4.7 %all-to-all-start.1 = ((bf16[8,8,512]{2,1,0:T(8,128)(2,1)}), bf16[8,8,512]{2,1,0:T(8,128)(2,1)S(1)}, u32[]{:S(2)}, u32[]{:S(2)}) async-start(bf16[8,8,512]{2,1,0:T(8,128)(2,1)} %shard_map.105), calls=%async_computation.1 | async-start | bytes 131072 | tf_op jit(solution)/shard_map/all_to_all | solution.py:363
  23.6 3.8 %collective-permute-start.2 = (bf16[2,64,256]{2,1,0:T(8,128)(2,1)}, bf16[2,64,256]{2,1,0:T(8,128)(2,1)S(1)}, u32[]{:S(2)}, u32[]{:S(2)}) collective-permute-start(bf16[2,64,256]{2,1,0:T(8,128)(2,1)} %get-tuple-element.24), channel_id=1, source_target_pairs={{0,12},{2,14},{4,8},{6,10},{8,4},{10,6},{12,0},{14,2},{1,13},{3,15... | collective-permute-start | bytes 196616 | tf_op jit(solution)/shard_map/ppermute | solution.py:352
  27.5 1.5 %collective-permute-start.3 = (bf16[2,64,256]{2,1,0:T(8,128)(2,1)}, bf16[2,64,256]{2,1,0:T(8,128)(2,1)S(1)}, u32[]{:S(2)}, u32[]{:S(2)}) collective-permute-start(bf16[2,64,256]{2,1,0:T(8,128)(2,1)} %get-tuple-element.25), channel_id=1, source_target_pairs={{0,14},{2,12},{4,10},{6,8},{8,6},{10,4},{12,2},{14,0},{1,15},{3,13... | collective-permute-start | bytes 196616 | tf_op jit(solution)/shard_map/ppermute | solution.py:352
  28.9 0.0 collective-permute-start.4
  29.0 0.0 collective-permute-done.refs_0_
  29.0 0.0 copy-done.2
  29.0 0.2 collective-permute-start.5
  29.2 0.0 collective-permute-done.1.refs_1_
  29.2 0.0 copy-done.1
  29.2 3.3 %collective-permute-start.6 = (bf16[2,64,256]{2,1,0:T(8,128)(2,1)S(1)}, bf16[2,64,256]{2,1,0:T(8,128)(2,1)S(1)}, u32[]{:S(2)}, u32[]{:S(2)}) collective-permute-start(bf16[2,64,256]{2,1,0:T(8,128)(2,1)S(1)} %copy-done.1), channel_id=1, source_target_pairs={{0,6},{2,4},{4,2},{6,0},{8,14},{10,12},{12,10},{14,8},{1,7},{3,5},... | collective-permute-start | bytes 196616 | tf_op jit(solution)/shard_map/ppermute | solution.py:352
  32.4 0.0 collective-permute-done.2.refs_2_
  32.4 2.3 %collective-permute-done.3.refs_3_ = bf16[2,64,256]{2,1,0:T(8,128)(2,1)S(1)} collective-permute-done((bf16[2,64,256]{2,1,0:T(8,128)(2,1)}, bf16[2,64,256]{2,1,0:T(8,128)(2,1)S(1)}, u32[]{:S(2)}, u32[]{:S(2)}) %collective-permute-start.3) | collective-permute-done | bytes 65568 | tf_op jit(solution)/shard_map/ppermute | solution.py:352
  34.8 0.0 collective-permute-done.4.refs_4_
  34.8 0.0 collective-permute-done.5.refs_5_
  34.8 1.3 %collective-permute-done.6.refs_6_ = bf16[2,64,256]{2,1,0:T(8,128)(2,1)S(1)} collective-permute-done((bf16[2,64,256]{2,1,0:T(8,128)(2,1)S(1)}, bf16[2,64,256]{2,1,0:T(8,128)(2,1)S(1)}, u32[]{:S(2)}, u32[]{:S(2)}) %collective-permute-start.6) | collective-permute-done | bytes 65568 | tf_op jit(solution)/shard_map/ppermute | solution.py:352
  36.0 0.0 all-to-all-done.1.back_ref
  36.1 1.5 %shard_map.106 = (bf16[2,1,8,64,256]{4,3,2,1,0:T(8,128)(2,1)}, bf16[8,4096]{1,0:T(8,128)(2,1)}) custom-call(bf16[8,8,512]{2,1,0:T(8,128)(2,1)S(1)} %all-to-all-done.1.back_ref, bf16[2,64,256]{2,1,0:T(8,128)(2,1)S(1)} %collective-permute-done.refs_0_, bf16[2,64,256]{2,1,0:T(8,128)(2,1)S(1)} %collective-permute-done.1.refs_1_, ...), custom_call_target="tpu_custom_call" | custom-call | bytes 1048576 | tf_op jit(solution)/shard_map/pallas_call | solution.py:365
Async XLA Ops:
  0.6 14.6 %all-to-all-start = ((bf16[8,8,512]{2,1,0:T(8,128)(2,1)}), bf16[8,8,512]{2,1,0:T(8,128)(2,1)S(1)}, u32[]{:S(2)}, u32[]{:S(2)}) async-start(bf16[8,8,512]{2,1,0:T(8,128)(2,1)} %bitcast.5), calls=%async_computation | async-start | bytes 131072 | tf_op jit(solution)/shard_map/all_to_all | solution.py:324
  7.9 0.7 %copy-start = (f32[1,128]{1,0:T(1,128)S(1)}, f32[1,128]{1,0:T(1,128)}, u32[]{:S(2)}) copy-start(f32[1,128]{1,0:T(1,128)} %constant.8.rates_ref) | copy-start | bytes 1540
  10.7 18.2 %collective-permute-start = (bf16[2,64,256]{2,1,0:T(8,128)(2,1)}, bf16[2,64,256]{2,1,0:T(8,128)(2,1)S(1)}, u32[]{:S(2)}, u32[]{:S(2)}) collective-permute-start(bf16[2,64,256]{2,1,0:T(8,128)(2,1)} %get-tuple-element.22), channel_id=1, source_target_pairs={{0,8},{2,10},{4,12},{6,14},{8,0},{10,2},{12,4},{14,6},{1,9},{3,11}... | collective-permute-start | bytes 196616 | tf_op jit(solution)/shard_map/ppermute | solution.py:352
  13.7 15.4 %collective-permute-start.1 = (bf16[2,64,256]{2,1,0:T(8,128)(2,1)}, bf16[2,64,256]{2,1,0:T(8,128)(2,1)S(1)}, u32[]{:S(2)}, u32[]{:S(2)}) collective-permute-start(bf16[2,64,256]{2,1,0:T(8,128)(2,1)} %get-tuple-element.23), channel_id=1, source_target_pairs={{0,10},{2,8},{4,14},{6,12},{8,2},{10,0},{12,6},{14,4},{1,11},{3,9}... | collective-permute-start | bytes 196616 | tf_op jit(solution)/shard_map/ppermute | solution.py:352
  19.0 10.0 %copy-start.2 = (bf16[2,64,256]{2,1,0:T(8,128)(2,1)S(1)}, bf16[2,64,256]{2,1,0:T(8,128)(2,1)}, u32[]{:S(2)}) copy-start(bf16[2,64,256]{2,1,0:T(8,128)(2,1)} %get-tuple-element.27) | copy-start | bytes 196612
  19.0 10.2 %copy-start.1 = (bf16[2,64,256]{2,1,0:T(8,128)(2,1)S(1)}, bf16[2,64,256]{2,1,0:T(8,128)(2,1)}, u32[]{:S(2)}) copy-start(bf16[2,64,256]{2,1,0:T(8,128)(2,1)} %get-tuple-element.28) | copy-start | bytes 196612
  19.0 17.1 %all-to-all-start.1 = ((bf16[8,8,512]{2,1,0:T(8,128)(2,1)}), bf16[8,8,512]{2,1,0:T(8,128)(2,1)S(1)}, u32[]{:S(2)}, u32[]{:S(2)}) async-start(bf16[8,8,512]{2,1,0:T(8,128)(2,1)} %shard_map.105), calls=%async_computation.1 | async-start | bytes 131072 | tf_op jit(solution)/shard_map/all_to_all | solution.py:363
  23.6 8.8 %collective-permute-start.2 = (bf16[2,64,256]{2,1,0:T(8,128)(2,1)}, bf16[2,64,256]{2,1,0:T(8,128)(2,1)S(1)}, u32[]{:S(2)}, u32[]{:S(2)}) collective-permute-start(bf16[2,64,256]{2,1,0:T(8,128)(2,1)} %get-tuple-element.24), channel_id=1, source_target_pairs={{0,12},{2,14},{4,8},{6,10},{8,4},{10,6},{12,0},{14,2},{1,13},{3,15... | collective-permute-start | bytes 196616 | tf_op jit(solution)/shard_map/ppermute | solution.py:352
  27.5 7.3 %collective-permute-start.3 = (bf16[2,64,256]{2,1,0:T(8,128)(2,1)}, bf16[2,64,256]{2,1,0:T(8,128)(2,1)S(1)}, u32[]{:S(2)}, u32[]{:S(2)}) collective-permute-start(bf16[2,64,256]{2,1,0:T(8,128)(2,1)} %get-tuple-element.25), channel_id=1, source_target_pairs={{0,14},{2,12},{4,10},{6,8},{8,6},{10,4},{12,2},{14,0},{1,15},{3,13... | collective-permute-start | bytes 196616 | tf_op jit(solution)/shard_map/ppermute | solution.py:352
  28.9 5.8 %collective-permute-start.4 = (bf16[2,64,256]{2,1,0:T(8,128)(2,1)}, bf16[2,64,256]{2,1,0:T(8,128)(2,1)S(1)}, u32[]{:S(2)}, u32[]{:S(2)}) collective-permute-start(bf16[2,64,256]{2,1,0:T(8,128)(2,1)} %get-tuple-element.26), channel_id=1, source_target_pairs={{0,2},{2,0},{4,6},{6,4},{8,10},{10,8},{12,14},{14,12},{1,3},{3,1},... | collective-permute-start | bytes 196616 | tf_op jit(solution)/shard_map/ppermute | solution.py:352
  29.0 5.8 %collective-permute-start.5 = (bf16[2,64,256]{2,1,0:T(8,128)(2,1)S(1)}, bf16[2,64,256]{2,1,0:T(8,128)(2,1)S(1)}, u32[]{:S(2)}, u32[]{:S(2)}) collective-permute-start(bf16[2,64,256]{2,1,0:T(8,128)(2,1)S(1)} %copy-done.2), channel_id=1, source_target_pairs={{0,4},{2,6},{4,0},{6,2},{8,12},{10,14},{12,8},{14,10},{1,5},{3,7},... | collective-permute-start | bytes 196616 | tf_op jit(solution)/shard_map/ppermute | solution.py:352
  29.2 6.9 %collective-permute-start.6 = (bf16[2,64,256]{2,1,0:T(8,128)(2,1)S(1)}, bf16[2,64,256]{2,1,0:T(8,128)(2,1)S(1)}, u32[]{:S(2)}, u32[]{:S(2)}) collective-permute-start(bf16[2,64,256]{2,1,0:T(8,128)(2,1)S(1)} %copy-done.1), channel_id=1, source_target_pairs={{0,6},{2,4},{4,2},{6,0},{8,14},{10,12},{12,10},{14,8},{1,7},{3,5},... | collective-permute-start | bytes 196616 | tf_op jit(solution)/shard_map/ppermute | solution.py:352

commit v3 on v2

--- a/solution.py
+++ b/solution.py
@@ -182,11 +182,12 @@
     return [*range(count // 2, count), *range(1, count // 2), 0]
 
 
-def prepare_kernel(count, core_count, prefix_length, request_rows, rates_ref, stored_assign, stored_lengths, stored_kv, *refs):
+def prepare_kernel(count, core_count, prefix_length, request_rows, stored_rates, stored_assign, stored_lengths, stored_kv, *refs):
     stored, refs = refs[:4], refs[4:]
     blocks, refs = refs[:count], refs[count:]
-    which_ref, live_ref, *fetched, kv_ref, cut_ref, assign_ref, lengths_ref, sems, out_sems = refs
+    which_ref, live_ref, *fetched, rates_ref, kv_ref, cut_ref, assign_ref, lengths_ref, sems, out_sems = refs
     first_copies = [
+        pltpu.make_async_copy(stored_rates, rates_ref, sems.at[7]),
         pltpu.make_async_copy(stored_kv, kv_ref, sems.at[4]),
         pltpu.make_async_copy(stored_assign, assign_ref, sems.at[5]),
         pltpu.make_async_copy(stored_lengths, lengths_ref, sems.at[6]),
@@ -196,6 +197,7 @@
     copies = [pltpu.make_async_copy(a, b, sems.at[i]) for i, (a, b) in enumerate(zip(stored, fetched))]
     for copy in copies:
         copy.start()
+    first_copies[0].wait()
     place = lax.axis_index("seq")
     rows = kv_ref.shape[1]
     width = kv_ref.shape[2] // count
@@ -205,7 +207,7 @@
     cosine = jnp.cos(angles)
     sine = jnp.sin(angles)
     sine = jnp.where(lax.broadcasted_iota(jnp.int32, (rows, HD), 1) < HD // 2, -sine, sine)
-    for copy in first_copies:
+    for copy in first_copies[1:]:
         copy.wait()
     for slot, k in enumerate(turns(count)):
         start = jnp.bitwise_xor(place, k) * width
@@ -238,36 +240,47 @@
     seq_count, span, group_width = q_ref.shape
     requests = seq_count * span
     per_kv = NQH // KVH
-    heads_here = keys_ref.shape[2] // HD
+    width = keys_ref.shape[2]
+    heads_here = width // HD
     length = keys_ref.shape[1] // NPFX
     slots = skeys_ref.shape[3]
     queries = q_ref[...].reshape(requests, group_width)
-    column = lax.broadcasted_iota(jnp.int32, (span * per_kv, span * slots), 1)
-    low = lax.broadcasted_iota(jnp.int32, (span * per_kv, span * slots), 0) % span * slots
+    heads = [(h, j) for h in range(heads_here) for j in range(per_kv)]
+    query = {(h, j): queries[:, (h * per_kv + j) * HD : (h * per_kv + j + 1) * HD] for h, j in heads}
+    query32 = {key: value.astype(jnp.float32) for key, value in query.items()}
+    blank = jnp.zeros((span, HD), jnp.float32)
+    tall = span * len(heads)
+    column = lax.broadcasted_iota(jnp.int32, (tall, span * slots), 1)
+    low = lax.broadcasted_iota(jnp.int32, (tall, span * slots), 0) % span * slots
+    added, more, found = {}, {}, []
+    blocks = [slice(b * span, (b + 1) * span) for b in range(seq_count)]
+    for rows in blocks:
+        part = jnp.concatenate(
+            [
+                jnp.concatenate([query32[h, j][rows] if g == h else blank for g in range(heads_here)], axis=1)
+                for h, j in heads
+            ],
+            axis=0,
+        ).astype(jnp.bfloat16)
+        skeys = skeys_ref[0, 0, rows].reshape(span * slots, width)
+        found.append(lax.dot_general(part, skeys, NT, preferred_element_type=jnp.float32))
+    for b, rows in enumerate(blocks):
+        live = jnp.concatenate([live_ref[rows, :1]] * len(heads), axis=0)
+        found[b] = jnp.where((column >= low) & (column < low + live), weigh(found[b]), 0.0)
+    for b, rows in enumerate(blocks):
+        svalues = svalues_ref[0, 0, rows].reshape(span * slots, width)
+        sums = jnp.sum(found[b], axis=1, keepdims=True)
+        products = jnp.dot(found[b].astype(jnp.bfloat16), svalues, preferred_element_type=jnp.float32)
+        for i, (h, j) in enumerate(heads):
+            more[h, j, b] = sums[i * span : (i + 1) * span]
+            added[h, j, b] = products[i * span : (i + 1) * span, h * HD : (h + 1) * HD]
     for h in range(heads_here):
         columns = slice(h * HD, (h + 1) * HD)
-        query = jnp.concatenate(
-            [queries[:, (h * per_kv + j) * HD : (h * per_kv + j + 1) * HD] for j in range(per_kv)], axis=0
-        )
-        query32 = query.astype(jnp.float32)
-        picked = [
-            [slice(j * requests + b * span, j * requests + (b + 1) * span) for j in range(per_kv)]
-            for b in range(seq_count)
-        ]
-        added, more = [], []
-        for b in range(seq_count):
-            part = jnp.concatenate([query32[rows] for rows in picked[b]], axis=0).astype(jnp.bfloat16)
-            skeys = skeys_ref[0, 0, b * span : (b + 1) * span, :, columns].reshape(span * slots, HD)
-            svalues = svalues_ref[0, 0, b * span : (b + 1) * span, :, columns].reshape(span * slots, HD)
-            recent = weigh(lax.dot_general(part, skeys, NT, preferred_element_type=jnp.float32))
-            live = jnp.concatenate([live_ref[rows, :1] for rows in picked[b]], axis=0)
-            recent = jnp.where((column >= low) & (column < low + live), recent, 0.0)
-            more.append(jnp.sum(recent, axis=1, keepdims=True))
-            added.append(lax.dot_general(recent.astype(jnp.bfloat16), svalues, NN, preferred_element_type=jnp.float32))
-        scores = lax.dot_general(query, keys_ref[0, :length, columns], NT, preferred_element_type=jnp.float32)
+        stacked = jnp.concatenate([query[h, j] for j in range(per_kv)], axis=0)
+        scores = lax.dot_general(stacked, keys_ref[0, :length, columns], NT, preferred_element_type=jnp.float32)
         for p in range(1, NPFX):
             other = lax.dot_general(
-                query, keys_ref[0, p * length : (p + 1) * length, columns], NT, preferred_element_type=jnp.float32
+                stacked, keys_ref[0, p * length : (p + 1) * length, columns], NT, preferred_element_type=jnp.float32
             )
             scores = jnp.where(which_ref[:, :1] == p, other, scores)
         weights = weigh(scores)
@@ -281,9 +294,7 @@
             numerator = jnp.where(which_ref[...] == p, other, numerator)
 
         def regroup(parts):
-            return jnp.concatenate(
-                [parts[b][j * span : (j + 1) * span] for j in range(per_kv) for b in range(seq_count)], axis=0
-            )
+            return jnp.concatenate([parts[h, j, b] for j in range(per_kv) for b in range(seq_count)], axis=0)
 
         result = (numerator + regroup(added)) * (1.0 / (total + regroup(more)))
         for j in range(per_kv):
@@ -326,26 +337,26 @@
     )
     stored = (old_keys, old_values, suffix_keys, suffix_values)
     block = pltpu.HBM((2, prefix_rows, width), jnp.bfloat16)
-    mine = jax.ShapeDtypeStruct((2, prefix_rows, width), jnp.bfloat16)
-    column = jax.ShapeDtypeStruct((tall, WIDE), jnp.int32)
+    mine = pltpu.VMEM((2, prefix_rows, width), jnp.bfloat16)
+    column = pltpu.VMEM((tall, WIDE), jnp.int32)
     prepared = pl.pallas_call(
         functools.partial(prepare_kernel, seq_count, core_count, prefix_length, request_rows),
-        out_shape=[block] * (seq_count - 1) + [mine] + [column] * 2 + [jax.ShapeDtypeStruct(x.shape, x.dtype) for x in stored],
-        in_specs=[VMEM] + [HBM] * 7,
+        out_shape=[block] * (seq_count - 1) + [mine] + [column] * 2 + [pltpu.VMEM(x.shape, x.dtype) for x in stored],
+        in_specs=[HBM] * 8,
         out_specs=[HBM] * (seq_count - 1) + [VMEM] * 7,
         scratch_shapes=[
+            pltpu.VMEM((1, HD), jnp.float32),
             pltpu.VMEM(new_kv.shape, jnp.bfloat16),
             pltpu.VMEM((seq_count - 1, 2, prefix_rows, width), jnp.bfloat16),
             pltpu.VMEM((1, assign.shape[0]), jnp.int32),
             pltpu.VMEM((1, assign.shape[0]), jnp.int32),
-            pltpu.SemaphoreType.DMA((7,)),
+            pltpu.SemaphoreType.DMA((8,)),
             pltpu.SemaphoreType.DMA((seq_count - 1,)),
         ],
         cost_estimate=pl.CostEstimate(flops=1000, bytes_accessed=1000, transcendentals=0),
         compiler_params=pltpu.CompilerParams(vmem_limit_bytes=24 * 2**20),
     )(
-        jnp.asarray(rates).reshape(1, HD),
-        *(pin(x, pltpu.HBM) for x in (assign.reshape(1, -1), lengths.reshape(1, -1), new_kv, *stored)),
+        *(pin(x, pltpu.HBM) for x in (jnp.asarray(rates).reshape(1, HD), assign.reshape(1, -1), lengths.reshape(1, -1), new_kv, *stored)),
     )
     blocks, (which, live, *fetched) = prepared[:seq_count], prepared[seq_count:]
     pieces = [
@@ -354,7 +365,7 @@
     ]
     attended = pl.pallas_call(
         attend_kernel,
-        out_shape=jax.ShapeDtypeStruct((seq_count, request_rows, group_width), jnp.bfloat16),
+        out_shape=pltpu.VMEM((seq_count, request_rows, group_width), jnp.bfloat16),
         in_specs=[VMEM] * 7,
         out_specs=VMEM,
         compiler_params=pltpu.CompilerParams(vmem_limit_bytes=16 * 2**20),

time: 37.9 us -> 35.3 us (0.931)
  Pallas kernels: 7.44 us -> 5.52 us
  local copies, waits for them, and re-layouts: 0.66 us -> 0.01 us
    pallas_call x1, Pallas kernels: 3.77 us -> 1.83 us  [local(): pl.pallas_call(attend_kernel, out_shape=pltpu.VMEM((seq_count, request_ro...]
    unnamed x6 -> x4, local copies, waits for them, and re-layouts: 0.66 us -> 0.01 us
  transfers between devices with their start and end apart: 9 -> 9, of which waited for: 2 -> 3; matrix products, arithmetic and copies ran while one was open for 0% -> 0% of each run, Pallas kernels for 16% -> 12%
where the time goes in v3:
time: 35.3 us; the launch traced here: 35 us
  starting transfers between devices  24.9 us (71%)
  Pallas kernels  5.52 us (16%)
  waiting for transfers between devices  3.87 us (11%)
  between operations  0.65 us (2%)
    ppermute x7, starting transfers between devices, local(): lax.ppermute(block, 'seq', [(i, i ^ k) for i in range(seq_count)])  13.2 us
    all_to_all x1, starting transfers between devices, local(): lax.all_to_all(queries.reshape(request_rows, seq_count, group_width).tran...  7.26 us
    all_to_all x1, starting transfers between devices, local(): back = lax.all_to_all(attended, 'seq', 0, 0, tiled=True)  4.43 us
    ppermute x7, waiting for transfers between devices, local(): lax.ppermute(block, 'seq', [(i, i ^ k) for i in range(seq_count)])  3.62 us
    pallas_call x1, Pallas kernels, local(): pl.pallas_call(functools.partial(prepare_kernel, seq_count, core_count, p...  2.21 us
    pallas_call x1, Pallas kernels, local(): pl.pallas_call(attend_kernel, out_shape=pltpu.VMEM((seq_count, request_ro...  1.83 us
    pallas_call x1, Pallas kernels, local(): pl.pallas_call(functools.partial(finish_kernel, seq_count), out_shape=(ja...  1.48 us
  transfers between devices with their start and end apart: 9, of which 3 were waited for; matrix products, arithmetic and copies ran while one was open for 0% of the time, Pallas kernels for 12%

profile of v3, /device:TPU:0, one launch (start us, length us, event | category | flops | bytes accessed | tf_op | source)
XLA Modules:
  0.0 35.0 jit_solution(2916197305821770503)
XLA Ops:
  0.6 7.3 %all-to-all-start = ((bf16[8,8,512]{2,1,0:T(8,128)(2,1)}), bf16[8,8,512]{2,1,0:T(8,128)(2,1)S(1)}, u32[]{:S(2)}, u32[]{:S(2)}) async-start(bf16[8,8,512]{2,1,0:T(8,128)(2,1)} %bitcast.5), calls=%async_computation | async-start | bytes 131072 | tf_op jit(solution)/shard_map/all_to_all | solution.py:335
  7.9 2.2 %shard_map.104 = (bf16[2,64,256]{2,1,0:T(8,128)(2,1)}, bf16[2,64,256]{2,1,0:T(8,128)(2,1)}, bf16[2,64,256]{2,1,0:T(8,128)(2,1)}, bf16[2,64,256]{2,1,0:T(8,128)(2...) custom-call(f32[1,128]{1,0:T(1,128)} %constant.8.stored_rates, ...), custom_call_target="tpu_custom_call" | custom-call | flops 1000 | bytes 1000 | tf_op jit(solution)/shard_map/pallas_call | solution.py:342
  10.1 3.0 %collective-permute-start = (bf16[2,64,256]{2,1,0:T(8,128)(2,1)}, bf16[2,64,256]{2,1,0:T(8,128)(2,1)S(1)}, u32[]{:S(2)}, u32[]{:S(2)}) collective-permute-start(bf16[2,64,256]{2,1,0:T(8,128)(2,1)} %get-tuple-element.22), channel_id=1, source_target_pairs={{0,8},{2,10},{4,12},{6,14},{8,0},{10,2},{12,4},{14,6},{1,9},{3,11}... | collective-permute-start | bytes 196616 | tf_op jit(solution)/shard_map/ppermute | solution.py:363
  13.1 1.5 %collective-permute-start.1 = (bf16[2,64,256]{2,1,0:T(8,128)(2,1)}, bf16[2,64,256]{2,1,0:T(8,128)(2,1)S(1)}, u32[]{:S(2)}, u32[]{:S(2)}) collective-permute-start(bf16[2,64,256]{2,1,0:T(8,128)(2,1)} %get-tuple-element.23), channel_id=1, source_target_pairs={{0,10},{2,8},{4,14},{6,12},{8,2},{10,0},{12,6},{14,4},{1,11},{3,9}... | collective-permute-start | bytes 196616 | tf_op jit(solution)/shard_map/ppermute | solution.py:363
  14.6 0.2 all-to-all-done.q_ref
  14.8 1.8 %shard_map.105 = bf16[8,8,512]{2,1,0:T(8,128)(2,1)} custom-call(bf16[8,8,512]{2,1,0:T(8,128)(2,1)S(1)} %all-to-all-done.q_ref, bf16[1,1024,256]{2,1,0:T(8,128)(2,1)S(1)} %get-tuple-element.16.keys_ref, bf16[1,1024,256]{2,1,0:T(8,128)(2,1)S(1)} %get-tuple-element.17.values_ref, bf16[1,1,64,32,256]{4,3,2,1,0:T(8,128)(2,1)S(1)} %get-tuple-element.18.skeys_ref, ...), custom_call_target="tpu_custom_call" | custom-call | flops 1048576 | bytes 1048576 | tf_op jit(solution)/shard_map/pallas_call | solution.py:366
  16.6 0.0 copy-start.1
  16.6 0.0 copy-start
  16.6 4.4 %all-to-all-start.1 = ((bf16[8,8,512]{2,1,0:T(8,128)(2,1)}), bf16[8,8,512]{2,1,0:T(8,128)(2,1)S(1)}, u32[]{:S(2)}, u32[]{:S(2)}) async-start(bf16[8,8,512]{2,1,0:T(8,128)(2,1)} %shard_map.105), calls=%async_computation.1 | async-start | bytes 131072 | tf_op jit(solution)/shard_map/all_to_all | solution.py:374
  21.1 3.8 %collective-permute-start.2 = (bf16[2,64,256]{2,1,0:T(8,128)(2,1)}, bf16[2,64,256]{2,1,0:T(8,128)(2,1)S(1)}, u32[]{:S(2)}, u32[]{:S(2)}) collective-permute-start(bf16[2,64,256]{2,1,0:T(8,128)(2,1)} %get-tuple-element.24), channel_id=1, source_target_pairs={{0,12},{2,14},{4,8},{6,10},{8,4},{10,6},{12,0},{14,2},{1,13},{3,15... | collective-permute-start | bytes 196616 | tf_op jit(solution)/shard_map/ppermute | solution.py:363
  24.9 1.5 %collective-permute-start.3 = (bf16[2,64,256]{2,1,0:T(8,128)(2,1)}, bf16[2,64,256]{2,1,0:T(8,128)(2,1)S(1)}, u32[]{:S(2)}, u32[]{:S(2)}) collective-permute-start(bf16[2,64,256]{2,1,0:T(8,128)(2,1)} %get-tuple-element.25), channel_id=1, source_target_pairs={{0,14},{2,12},{4,10},{6,8},{8,6},{10,4},{12,2},{14,0},{1,15},{3,13... | collective-permute-start | bytes 196616 | tf_op jit(solution)/shard_map/ppermute | solution.py:363
  26.4 0.0 collective-permute-start.4
  26.4 0.0 collective-permute-done.refs_0_
  26.4 0.0 copy-done.1
  26.4 0.2 collective-permute-start.5
  26.6 0.0 collective-permute-done.1.refs_1_
  26.6 0.0 copy-done
  26.6 3.3 %collective-permute-start.6 = (bf16[2,64,256]{2,1,0:T(8,128)(2,1)S(1)}, bf16[2,64,256]{2,1,0:T(8,128)(2,1)S(1)}, u32[]{:S(2)}, u32[]{:S(2)}) collective-permute-start(bf16[2,64,256]{2,1,0:T(8,128)(2,1)S(1)} %copy-done), channel_id=1, source_target_pairs={{0,6},{2,4},{4,2},{6,0},{8,14},{10,12},{12,10},{14,8},{1,7},{3,5},... | collective-permute-start | bytes 196616 | tf_op jit(solution)/shard_map/ppermute | solution.py:363
  29.9 0.0 collective-permute-done.2.refs_2_
  29.9 2.3 %collective-permute-done.3.refs_3_ = bf16[2,64,256]{2,1,0:T(8,128)(2,1)S(1)} collective-permute-done((bf16[2,64,256]{2,1,0:T(8,128)(2,1)}, bf16[2,64,256]{2,1,0:T(8,128)(2,1)S(1)}, u32[]{:S(2)}, u32[]{:S(2)}) %collective-permute-start.3) | collective-permute-done | bytes 65568 | tf_op jit(solution)/shard_map/ppermute | solution.py:363
  32.2 0.0 collective-permute-done.4.refs_4_
  32.2 0.0 collective-permute-done.5.refs_5_
  32.2 1.3 %collective-permute-done.6.refs_6_ = bf16[2,64,256]{2,1,0:T(8,128)(2,1)S(1)} collective-permute-done((bf16[2,64,256]{2,1,0:T(8,128)(2,1)S(1)}, bf16[2,64,256]{2,1,0:T(8,128)(2,1)S(1)}, u32[]{:S(2)}, u32[]{:S(2)}) %collective-permute-start.6) | collective-permute-done | bytes 65568 | tf_op jit(solution)/shard_map/ppermute | solution.py:363
  33.5 0.0 all-to-all-done.1.back_ref
  33.5 1.5 %shard_map.106 = (bf16[2,1,8,64,256]{4,3,2,1,0:T(8,128)(2,1)}, bf16[8,4096]{1,0:T(8,128)(2,1)}) custom-call(bf16[8,8,512]{2,1,0:T(8,128)(2,1)S(1)} %all-to-all-done.1.back_ref, bf16[2,64,256]{2,1,0:T(8,128)(2,1)S(1)} %collective-permute-done.refs_0_, bf16[2,64,256]{2,1,0:T(8,128)(2,1)S(1)} %collective-permute-done.1.refs_1_, ...), custom_call_target="tpu_custom_call" | custom-call | bytes 1048576 | tf_op jit(solution)/shard_map/pallas_call | solution.py:376
Async XLA Ops:
  0.6 14.2 %all-to-all-start = ((bf16[8,8,512]{2,1,0:T(8,128)(2,1)}), bf16[8,8,512]{2,1,0:T(8,128)(2,1)S(1)}, u32[]{:S(2)}, u32[]{:S(2)}) async-start(bf16[8,8,512]{2,1,0:T(8,128)(2,1)} %bitcast.5), calls=%async_computation | async-start | bytes 131072 | tf_op jit(solution)/shard_map/all_to_all | solution.py:335
  10.1 16.3 %collective-permute-start = (bf16[2,64,256]{2,1,0:T(8,128)(2,1)}, bf16[2,64,256]{2,1,0:T(8,128)(2,1)S(1)}, u32[]{:S(2)}, u32[]{:S(2)}) collective-permute-start(bf16[2,64,256]{2,1,0:T(8,128)(2,1)} %get-tuple-element.22), channel_id=1, source_target_pairs={{0,8},{2,10},{4,12},{6,14},{8,0},{10,2},{12,4},{14,6},{1,9},{3,11}... | collective-permute-start | bytes 196616 | tf_op jit(solution)/shard_map/ppermute | solution.py:363
  13.1 13.5 %collective-permute-start.1 = (bf16[2,64,256]{2,1,0:T(8,128)(2,1)}, bf16[2,64,256]{2,1,0:T(8,128)(2,1)S(1)}, u32[]{:S(2)}, u32[]{:S(2)}) collective-permute-start(bf16[2,64,256]{2,1,0:T(8,128)(2,1)} %get-tuple-element.23), channel_id=1, source_target_pairs={{0,10},{2,8},{4,14},{6,12},{8,2},{10,0},{12,6},{14,4},{1,11},{3,9}... | collective-permute-start | bytes 196616 | tf_op jit(solution)/shard_map/ppermute | solution.py:363
  16.6 9.8 %copy-start.1 = (bf16[2,64,256]{2,1,0:T(8,128)(2,1)S(1)}, bf16[2,64,256]{2,1,0:T(8,128)(2,1)}, u32[]{:S(2)}) copy-start(bf16[2,64,256]{2,1,0:T(8,128)(2,1)} %get-tuple-element.27) | copy-start | bytes 196612
  16.6 10.0 %copy-start = (bf16[2,64,256]{2,1,0:T(8,128)(2,1)S(1)}, bf16[2,64,256]{2,1,0:T(8,128)(2,1)}, u32[]{:S(2)}) copy-start(bf16[2,64,256]{2,1,0:T(8,128)(2,1)} %get-tuple-element.28) | copy-start | bytes 196612
  16.6 16.8 %all-to-all-start.1 = ((bf16[8,8,512]{2,1,0:T(8,128)(2,1)}), bf16[8,8,512]{2,1,0:T(8,128)(2,1)S(1)}, u32[]{:S(2)}, u32[]{:S(2)}) async-start(bf16[8,8,512]{2,1,0:T(8,128)(2,1)} %shard_map.105), calls=%async_computation.1 | async-start | bytes 131072 | tf_op jit(solution)/shard_map/all_to_all | solution.py:374
  21.1 8.8 %collective-permute-start.2 = (bf16[2,64,256]{2,1,0:T(8,128)(2,1)}, bf16[2,64,256]{2,1,0:T(8,128)(2,1)S(1)}, u32[]{:S(2)}, u32[]{:S(2)}) collective-permute-start(bf16[2,64,256]{2,1,0:T(8,128)(2,1)} %get-tuple-element.24), channel_id=1, source_target_pairs={{0,12},{2,14},{4,8},{6,10},{8,4},{10,6},{12,0},{14,2},{1,13},{3,15... | collective-permute-start | bytes 196616 | tf_op jit(solution)/shard_map/ppermute | solution.py:363
  24.9 7.3 %collective-permute-start.3 = (bf16[2,64,256]{2,1,0:T(8,128)(2,1)}, bf16[2,64,256]{2,1,0:T(8,128)(2,1)S(1)}, u32[]{:S(2)}, u32[]{:S(2)}) collective-permute-start(bf16[2,64,256]{2,1,0:T(8,128)(2,1)} %get-tuple-element.25), channel_id=1, source_target_pairs={{0,14},{2,12},{4,10},{6,8},{8,6},{10,4},{12,2},{14,0},{1,15},{3,13... | collective-permute-start | bytes 196616 | tf_op jit(solution)/shard_map/ppermute | solution.py:363
  26.4 5.8 %collective-permute-start.4 = (bf16[2,64,256]{2,1,0:T(8,128)(2,1)}, bf16[2,64,256]{2,1,0:T(8,128)(2,1)S(1)}, u32[]{:S(2)}, u32[]{:S(2)}) collective-permute-start(bf16[2,64,256]{2,1,0:T(8,128)(2,1)} %get-tuple-element.26), channel_id=1, source_target_pairs={{0,2},{2,0},{4,6},{6,4},{8,10},{10,8},{12,14},{14,12},{1,3},{3,1},... | collective-permute-start | bytes 196616 | tf_op jit(solution)/shard_map/ppermute | solution.py:363
  26.4 5.8 %collective-permute-start.5 = (bf16[2,64,256]{2,1,0:T(8,128)(2,1)S(1)}, bf16[2,64,256]{2,1,0:T(8,128)(2,1)S(1)}, u32[]{:S(2)}, u32[]{:S(2)}) collective-permute-start(bf16[2,64,256]{2,1,0:T(8,128)(2,1)S(1)} %copy-done.1), channel_id=1, source_target_pairs={{0,4},{2,6},{4,0},{6,2},{8,12},{10,14},{12,8},{14,10},{1,5},{3,7},... | collective-permute-start | bytes 196616 | tf_op jit(solution)/shard_map/ppermute | solution.py:363
  26.6 6.9 %collective-permute-start.6 = (bf16[2,64,256]{2,1,0:T(8,128)(2,1)S(1)}, bf16[2,64,256]{2,1,0:T(8,128)(2,1)S(1)}, u32[]{:S(2)}, u32[]{:S(2)}) collective-permute-start(bf16[2,64,256]{2,1,0:T(8,128)(2,1)S(1)} %copy-done), channel_id=1, source_target_pairs={{0,6},{2,4},{4,2},{6,0},{8,14},{10,12},{12,10},{14,8},{1,7},{3,5},... | collective-permute-start | bytes 196616 | tf_op jit(solution)/shard_map/ppermute | solution.py:363

commit v4 on v3

--- a/solution.py
+++ b/solution.py
@@ -178,24 +178,32 @@
 WIDE = 128
 
 
-def turns(count):
-    return [*range(count // 2, count), *range(1, count // 2), 0]
-
-
-def prepare_kernel(count, core_count, prefix_length, request_rows, stored_rates, stored_assign, stored_lengths, stored_kv, *refs):
-    stored, refs = refs[:4], refs[4:]
-    blocks, refs = refs[:count], refs[count:]
-    which_ref, live_ref, *fetched, rates_ref, kv_ref, cut_ref, assign_ref, lengths_ref, sems, out_sems = refs
+def own_column(values_ref, tall, request_rows, core_count):
+    shape = (tall, values_ref.shape[1])
+    row = lax.broadcasted_iota(jnp.int32, shape, 0) % (values_ref.shape[1] // core_count)
+    wanted = (row // request_rows * core_count + lax.axis_index("pd")) * request_rows + row % request_rows
+    picked = jnp.where(lax.broadcasted_iota(jnp.int32, shape, 1) == wanted, values_ref[...], 0)
+    return jnp.sum(picked.astype(jnp.float32), axis=1, keepdims=True).astype(jnp.int32)
+
+
+def prepare_kernel(count, core_count, prefix_length, request_rows, riding, *refs):
+    (stored_rates, stored_assign, stored_lengths, stored_kv), stored, refs = refs[:4], refs[4:7], refs[7:]
+    own_ref, *pieces = refs[: count // 2]
+    which_ref, live_ref, ride_ref, *fetched = refs[count // 2 : count // 2 + 6]
+    rates_ref, assign_ref, lengths_ref, kv_ref, cut_ref, sems, out_sems = refs[count // 2 + 6 :]
     first_copies = [
-        pltpu.make_async_copy(stored_rates, rates_ref, sems.at[7]),
-        pltpu.make_async_copy(stored_kv, kv_ref, sems.at[4]),
-        pltpu.make_async_copy(stored_assign, assign_ref, sems.at[5]),
-        pltpu.make_async_copy(stored_lengths, lengths_ref, sems.at[6]),
+        pltpu.make_async_copy(a, b, sems.at[i])
+        for i, (a, b) in enumerate(
+            (
+                (stored_rates, rates_ref),
+                (stored_kv, kv_ref),
+                (stored_assign, assign_ref),
+                (stored_lengths, lengths_ref),
+            )
+        )
     ]
-    for copy in first_copies:
-        copy.start()
-    copies = [pltpu.make_async_copy(a, b, sems.at[i]) for i, (a, b) in enumerate(zip(stored, fetched))]
-    for copy in copies:
+    copies = [pltpu.make_async_copy(a, b, sems.at[4 + i]) for i, (a, b) in enumerate(zip(stored, fetched))]
+    for copy in first_copies + copies:
         copy.start()
     first_copies[0].wait()
     place = lax.axis_index("seq")
@@ -209,18 +217,21 @@
     sine = jnp.where(lax.broadcasted_iota(jnp.int32, (rows, HD), 1) < HD // 2, -sine, sine)
     for copy in first_copies[1:]:
         copy.wait()
-    for slot, k in enumerate(turns(count)):
-        start = jnp.bitwise_xor(place, k) * width
-        for h in range(width // HD):
-            columns = pl.ds(pl.multiple_of(start + h * HD, HD), HD)
-            keys = kv_ref[0, :, columns].astype(jnp.float32)
-            turned = pltpu.roll(keys, HD // 2, 1)
-            cut = blocks[slot] if k == 0 else cut_ref.at[slot]
-            cut[0, :, h * HD : (h + 1) * HD] = (keys * cosine + turned * sine).astype(jnp.bfloat16)
-            cut[1, :, h * HD : (h + 1) * HD] = kv_ref[1, :, columns]
-        if k:
-            copies.append(pltpu.make_async_copy(cut_ref.at[slot], blocks[slot], out_sems.at[slot]))
+    for j in reversed(range(count // 2)):
+        cut = cut_ref.at[j - 1] if j else own_ref
+        for d in range(2):
+            start = jnp.bitwise_xor(place, 2 * j + d) * width
+            for h in range(width // HD):
+                columns = pl.ds(pl.multiple_of(start + h * HD, HD), HD)
+                keys = kv_ref[0, :, columns].astype(jnp.float32)
+                turned = pltpu.roll(keys, HD // 2, 1)
+                cut[d, :rows, h * HD : (h + 1) * HD] = (keys * cosine + turned * sine).astype(jnp.bfloat16)
+                cut[d, rows:, h * HD : (h + 1) * HD] = kv_ref[1, : rows - riding, columns]
+        if j:
+            copies.append(pltpu.make_async_copy(cut, pieces[j - 1], out_sems.at[j - 1]))
             copies[-1].start()
+    for s in range(count):
+        ride_ref[s] = kv_ref[1, rows - riding :, s * width : (s + 1) * width]
     tall = which_ref.shape[0]
     which_ref[...] = jnp.broadcast_to(own_column(assign_ref, tall, request_rows, core_count), which_ref.shape)
     live_ref[...] = jnp.broadcast_to(own_column(lengths_ref, tall, request_rows, core_count), live_ref.shape)
@@ -228,15 +239,11 @@
         copy.wait()
 
 
-def own_column(values_ref, tall, request_rows, core_count):
-    shape = (tall, values_ref.shape[1])
-    row = lax.broadcasted_iota(jnp.int32, shape, 0) % (values_ref.shape[1] // core_count)
-    wanted = (row // request_rows * core_count + lax.axis_index("pd")) * request_rows + row % request_rows
-    picked = jnp.where(lax.broadcasted_iota(jnp.int32, shape, 1) == wanted, values_ref[...], 0)
-    return jnp.sum(picked.astype(jnp.float32), axis=1, keepdims=True).astype(jnp.int32)
-
-
-def attend_kernel(q_ref, keys_ref, values_ref, skeys_ref, svalues_ref, which_ref, live_ref, out_ref):
+def attend_kernel(
+    q_ref, stored_values, keys_ref, skeys_ref, svalues_ref, which_ref, live_ref, ride_ref, out_ref, values_ref, sem
+):
+    fetch = pltpu.make_async_copy(stored_values, values_ref, sem)
+    fetch.start()
     seq_count, span, group_width = q_ref.shape
     requests = seq_count * span
     per_kv = NQH // KVH
@@ -274,6 +281,8 @@
         for i, (h, j) in enumerate(heads):
             more[h, j, b] = sums[i * span : (i + 1) * span]
             added[h, j, b] = products[i * span : (i + 1) * span, h * HD : (h + 1) * HD]
+    results = []
+    fetch.wait()
     for h in range(heads_here):
         columns = slice(h * HD, (h + 1) * HD)
         stacked = jnp.concatenate([query[h, j] for j in range(per_kv)], axis=0)
@@ -298,24 +307,61 @@
 
         result = (numerator + regroup(added)) * (1.0 / (total + regroup(more)))
         for j in range(per_kv):
-            head = h * per_kv + j
-            out_ref[:, :, head * HD : (head + 1) * HD] = result[j * requests : (j + 1) * requests].reshape(
-                seq_count, span, HD
-            ).astype(jnp.bfloat16)
-
-
-def finish_kernel(count, back_ref, *refs):
-    *pieces, cache_ref, attention_ref, sems = refs
+            results.append(result[j * requests : (j + 1) * requests].reshape(seq_count, span, HD))
+    for c in range(heads_here):
+        out_ref[:, : per_kv * span, c * HD : (c + 1) * HD] = jnp.concatenate(
+            [results[t * heads_here + c] for t in range(per_kv)], axis=1
+        ).astype(jnp.bfloat16)
+    out_ref[:, per_kv * span :, :] = ride_ref[...]
+
+
+def forward_kernel(*refs):
+    *pieces, out_ref = refs
+    for j, piece in enumerate(pieces):
+        out_ref[j] = piece[1]
+
+
+def forward(pieces):
+    return pl.pallas_call(
+        forward_kernel,
+        out_shape=jax.ShapeDtypeStruct((len(pieces), *pieces[0].shape[1:]), pieces[0].dtype),
+        in_specs=[VMEM] * len(pieces),
+        out_specs=VMEM,
+        cost_estimate=pl.CostEstimate(flops=2**34, bytes_accessed=1000, transcendentals=0),
+    )(*(pin(piece) for piece in pieces))
+
+
+def finish_kernel(count, back_ref, far_ref, *refs):
+    *near, cache_ref, attention_ref, sems = refs
     place = lax.axis_index("seq")
-    copies = [
-        pltpu.make_async_copy(piece, cache_ref.at[:, 0, jnp.bitwise_xor(place, k)], sems.at[k])
-        for k, piece in zip(turns(count), pieces)
-    ]
+    rows = cache_ref.shape[3]
+    request_rows = attention_ref.shape[0]
+    width = back_ref.shape[2]
+    parts = attention_ref.shape[1] // (count * width)
+    riding = back_ref.shape[1] - parts * request_rows
+    copies = []
+    for j in range(count // 2):
+        for d, piece in ((0, near[j].at[0]), (1, far_ref.at[j])):
+            source = jnp.bitwise_xor(place, 2 * j + d)
+            copies += [
+                pltpu.make_async_copy(piece.at[:rows], cache_ref.at[0, 0, source], sems.at[2 * j + d, 0]),
+                pltpu.make_async_copy(
+                    piece.at[rows:], cache_ref.at[1, 0, source, : rows - riding], sems.at[2 * j + d, 1]
+                ),
+            ]
+    copies.append(
+        pltpu.make_async_copy(
+            back_ref.at[:, parts * request_rows :], cache_ref.at[1, 0, :, rows - riding :], sems.at[0, 2]
+        )
+    )
     for copy in copies:
         copy.start()
-    width = back_ref.shape[2]
     for s in range(count):
-        attention_ref[:, s * width : (s + 1) * width] = back_ref[s]
+        block = back_ref[s, : parts * request_rows].astype(jnp.float32)
+        for t in range(parts):
+            attention_ref[:, (s * parts + t) * width : (s * parts + t + 1) * width] = block[
+                t * request_rows : (t + 1) * request_rows
+            ].astype(jnp.bfloat16)
     for copy in copies:
         copy.wait()
 
@@ -325,6 +371,7 @@
     core_count = lax.axis_size("pd")
     if seq_count > KVH or seq_count & (seq_count - 1):
         return general(new_kv, old_keys, old_values, suffix_keys, suffix_values, queries, lengths, assign)
+    half = seq_count // 2
     request_rows = queries.shape[0]
     prefix_rows = new_kv.shape[1]
     group_width = queries.shape[1] // seq_count
@@ -332,45 +379,60 @@
     tall = NQH // KVH * seq_count * request_rows
     prefix_length = prefix_rows * seq_count * core_count // NPFX
     rates = (10000.0 ** (-2.0 * (np.arange(HD) % (HD // 2)) / HD)).astype(np.float32)
+
+    def swap(x, k):
+        return lax.ppermute(x, "seq", [(i, i ^ k) for i in range(seq_count)])
+
     asked = lax.all_to_all(
         queries.reshape(request_rows, seq_count, group_width).transpose(1, 0, 2), "seq", 0, 0, tiled=True
     )
-    stored = (old_keys, old_values, suffix_keys, suffix_values)
-    block = pltpu.HBM((2, prefix_rows, width), jnp.bfloat16)
-    mine = pltpu.VMEM((2, prefix_rows, width), jnp.bfloat16)
+    stored = (old_keys, suffix_keys, suffix_values)
+    riding = 32
+    piece = (2, 2 * prefix_rows - riding, width)
+    packed = NQH // KVH * request_rows + riding
     column = pltpu.VMEM((tall, WIDE), jnp.int32)
     prepared = pl.pallas_call(
-        functools.partial(prepare_kernel, seq_count, core_count, prefix_length, request_rows),
-        out_shape=[block] * (seq_count - 1) + [mine] + [column] * 2 + [pltpu.VMEM(x.shape, x.dtype) for x in stored],
-        in_specs=[HBM] * 8,
-        out_specs=[HBM] * (seq_count - 1) + [VMEM] * 7,
+        functools.partial(prepare_kernel, seq_count, core_count, prefix_length, request_rows, riding),
+        out_shape=[pltpu.VMEM(piece, jnp.bfloat16)]
+        + [pltpu.HBM(piece, jnp.bfloat16)] * (half - 1)
+        + [column] * 2
+        + [pltpu.VMEM((seq_count, riding, width), jnp.bfloat16)]
+        + [pltpu.VMEM(x.shape, x.dtype) for x in stored],
+        in_specs=[HBM] * 7,
+        out_specs=[VMEM] + [HBM] * (half - 1) + [VMEM] * 6,
         scratch_shapes=[
             pltpu.VMEM((1, HD), jnp.float32),
-            pltpu.VMEM(new_kv.shape, jnp.bfloat16),
-            pltpu.VMEM((seq_count - 1, 2, prefix_rows, width), jnp.bfloat16),
             pltpu.VMEM((1, assign.shape[0]), jnp.int32),
             pltpu.VMEM((1, assign.shape[0]), jnp.int32),
-            pltpu.SemaphoreType.DMA((8,)),
-            pltpu.SemaphoreType.DMA((seq_count - 1,)),
+            pltpu.VMEM(new_kv.shape, jnp.bfloat16),
+            pltpu.VMEM((half - 1, *piece), jnp.bfloat16),
+            pltpu.SemaphoreType.DMA((7,)),
+            pltpu.SemaphoreType.DMA((half - 1,)),
         ],
-        cost_estimate=pl.CostEstimate(flops=1000, bytes_accessed=1000, transcendentals=0),
-        compiler_params=pltpu.CompilerParams(vmem_limit_bytes=24 * 2**20),
+        cost_estimate=pl.CostEstimate(flops=2**33, bytes_accessed=1000, transcendentals=0),
+        compiler_params=pltpu.CompilerParams(vmem_limit_bytes=16 * 2**20),
     )(
-        *(pin(x, pltpu.HBM) for x in (jnp.asarray(rates).reshape(1, HD), assign.reshape(1, -1), lengths.reshape(1, -1), new_kv, *stored)),
-    )
-    blocks, (which, live, *fetched) = prepared[:seq_count], prepared[seq_count:]
-    pieces = [
-        lax.ppermute(block, "seq", [(i, i ^ k) for i in range(seq_count)]) if k else block
-        for k, block in zip(turns(seq_count), blocks)
-    ]
+        *(
+            pin(x, pltpu.HBM)
+            for x in (
+                jnp.asarray(rates).reshape(1, HD), assign.reshape(1, -1), lengths.reshape(1, -1), new_kv, *stored
+            )
+        )
+    )
+    kv_cuts, (which, live, ride, *fetched) = prepared[:half], prepared[half:]
+    kv_near = [kv_cuts[0]]
+    for j in range(1, half):
+        kv_near.append(swap(kv_cuts[j], 2 * j))
     attended = pl.pallas_call(
         attend_kernel,
-        out_shape=pltpu.VMEM((seq_count, request_rows, group_width), jnp.bfloat16),
-        in_specs=[VMEM] * 7,
+        out_shape=pltpu.VMEM((seq_count, packed, width), jnp.bfloat16),
+        in_specs=[VMEM, HBM] + [VMEM] * 6,
         out_specs=VMEM,
+        scratch_shapes=[pltpu.VMEM(old_values.shape, jnp.bfloat16), pltpu.SemaphoreType.DMA(())],
         compiler_params=pltpu.CompilerParams(vmem_limit_bytes=16 * 2**20),
-        cost_estimate=pl.CostEstimate(flops=2**20, bytes_accessed=2**20, transcendentals=2**10),
-    )(pin(asked), *(pin(x) for x in fetched), pin(which), pin(live))
+        cost_estimate=pl.CostEstimate(flops=2**30, bytes_accessed=2**20, transcendentals=2**10),
+    )(pin(asked), pin(old_values, pltpu.HBM), *(pin(x) for x in fetched), pin(which), pin(live), pin(ride))
+    kv_far = swap(forward(kv_near), 1)
     back = lax.all_to_all(attended, "seq", 0, 0, tiled=True)
     return tuple(
         pl.pallas_call(
@@ -379,11 +441,11 @@
                 jax.ShapeDtypeStruct((2, 1, seq_count, prefix_rows, width), jnp.bfloat16),
                 jax.ShapeDtypeStruct((request_rows, NQH * HD), jnp.bfloat16),
             ),
-            in_specs=[VMEM] * (seq_count + 1),
+            in_specs=[VMEM] * (half + 2),
             out_specs=(HBM, VMEM),
-            scratch_shapes=[pltpu.SemaphoreType.DMA((seq_count,))],
+            scratch_shapes=[pltpu.SemaphoreType.DMA((seq_count, 3))],
             cost_estimate=pl.CostEstimate(flops=0, bytes_accessed=2**20, transcendentals=0),
-        )(pin(back), *(pin(piece) for piece in pieces))
+        )(*(pin(x) for x in (back, kv_far, *kv_near)))
     )
 
 

time: 35.3 us -> 33.1 us (0.938)
  starting transfers between devices: 24.9 us -> 19.4 us
  Pallas kernels: 5.52 us -> 7.25 us
  waiting for transfers between devices: 3.87 us -> 5.44 us
    ppermute x7 -> x4, starting transfers between devices: 13.2 us -> 6.54 us  [swap(): return lax.ppermute(x, 'seq', [(i, i ^ k) for i in range(seq_count)])]
    pallas_call x1 -> x2, Pallas kernels: 1.83 us -> 3.6 us  [the longest x1 2.92 us: local(): pl.pallas_call(attend_kernel, out_shape=pltpu.VMEM((seq_count, packed, wi...]
    all_to_all x1, starting transfers between devices: 4.43 us -> 5.56 us  [local(): back = lax.all_to_all(attended, 'seq', 0, 0, tiled=True)]
    ppermute x7 -> x4, waiting for transfers between devices: 3.62 us -> 4.75 us  [swap(): return lax.ppermute(x, 'seq', [(i, i ^ k) for i in range(seq_count)])]
  transfers between devices with their start and end apart: 9 -> 6, of which waited for: 3 -> 3; matrix products, arithmetic and copies ran while one was open for 0% -> 0% of each run, Pallas kernels for 12% -> 17%
where the time goes in v4:
time: 33.1 us; the launch traced here: 32.7 us
  starting transfers between devices  19.4 us (59%)
  Pallas kernels  7.25 us (22%)
  waiting for transfers between devices  5.44 us (16%)
  between operations  0.67 us (2%)
    all_to_all x1, starting transfers between devices, local(): lax.all_to_all(queries.reshape(request_rows, seq_count, group_width).tran...  7.26 us
    ppermute x4, starting transfers between devices, swap(): return lax.ppermute(x, 'seq', [(i, i ^ k) for i in range(seq_count)])  6.54 us
    all_to_all x1, starting transfers between devices, local(): back = lax.all_to_all(attended, 'seq', 0, 0, tiled=True)  5.56 us
    ppermute x4, waiting for transfers between devices, swap(): return lax.ppermute(x, 'seq', [(i, i ^ k) for i in range(seq_count)])  4.75 us
    pallas_call x1, Pallas kernels, local(): pl.pallas_call(attend_kernel, out_shape=pltpu.VMEM((seq_count, packed, wi...  2.92 us
    pallas_call x1, Pallas kernels, local(): pl.pallas_call(functools.partial(prepare_kernel, seq_count, core_count, p...  2.01 us
    pallas_call x1, Pallas kernels, local(): pl.pallas_call(functools.partial(finish_kernel, seq_count), out_shape=(ja...  1.63 us
    pallas_call x1, Pallas kernels, forward(): pl.pallas_call(forward_kernel, out_shape=jax.ShapeDtypeStruct((len(pieces...  0.68 us
  transfers between devices with their start and end apart: 6, of which 3 were waited for; matrix products, arithmetic and copies ran while one was open for 0% of the time, Pallas kernels for 17%

profile of v4, /device:TPU:0, one launch (start us, length us, event | category | flops | bytes accessed | tf_op | source)
XLA Modules:
  0.0 32.7 jit_solution(7487373573820495339)
XLA Ops:
  0.6 7.3 %all-to-all-start = ((bf16[8,8,512]{2,1,0:T(8,128)(2,1)}), bf16[8,8,512]{2,1,0:T(8,128)(2,1)S(1)}, u32[]{:S(2)}, u32[]{:S(2)}) async-start(bf16[8,8,512]{2,1,0:T(8,128)(2,1)} %bitcast.5), calls=%async_computation | async-start | bytes 131072 | tf_op jit(solution)/shard_map/all_to_all | solution.py:386
  7.9 2.0 %shard_map.104 = (bf16[2,96,256]{2,1,0:T(8,128)(2,1)S(1)}, bf16[2,96,256]{2,1,0:T(8,128)(2,1)}, bf16[2,96,256]{2,1,0:T(8,128)(2,1)}, bf16[2,96,256]{2,1,0:T(8,12...) custom-call(f32[1,128]{1,0:T(1,128)} %constant.8.refs_0_, ...), custom_call_target="tpu_custom_call" | custom-call | flops 8589934592 | bytes 1000 | tf_op jit(solution)/shard_map/pallas_call | solution.py:394
  9.9 2.1 %collective-permute-start = (bf16[2,96,256]{2,1,0:T(8,128)(2,1)}, bf16[2,96,256]{2,1,0:T(8,128)(2,1)S(1)}, u32[]{:S(2)}, u32[]{:S(2)}) collective-permute-start(bf16[2,96,256]{2,1,0:T(8,128)(2,1)} %get-tuple-element.19), channel_id=1, source_target_pairs={{0,4},{2,6},{4,0},{6,2},{8,12},{10,14},{12,8},{14,10},{1,5},{3,7},... | collective-permute-start | bytes 294920 | tf_op jit(solution)/shard_map/ppermute | solution.py:384
  12.0 2.4 %collective-permute-start.1 = (bf16[2,96,256]{2,1,0:T(8,128)(2,1)}, bf16[2,96,256]{2,1,0:T(8,128)(2,1)S(1)}, u32[]{:S(2)}, u32[]{:S(2)}) collective-permute-start(bf16[2,96,256]{2,1,0:T(8,128)(2,1)} %get-tuple-element.20), channel_id=1, source_target_pairs={{0,8},{2,10},{4,12},{6,14},{8,0},{10,2},{12,4},{14,6},{1,9},{3,11}... | collective-permute-start | bytes 294920 | tf_op jit(solution)/shard_map/ppermute | solution.py:384
  14.4 0.1 collective-permute-start.2
  14.4 0.4 %all-to-all-done.q_ref = bf16[8,8,512]{2,1,0:T(8,128)(2,1)S(1)} async-done(((bf16[8,8,512]{2,1,0:T(8,128)(2,1)}), bf16[8,8,512]{2,1,0:T(8,128)(2,1)S(1)}, u32[]{:S(2)}, u32[]{:S(2)}) %all-to-all-start) | async-done | bytes 65568 | tf_op jit(solution)/shard_map/all_to_all | solution.py:386
  14.8 2.9 %shard_map.105 = bf16[8,48,256]{2,1,0:T(8,128)(2,1)} custom-call(bf16[8,8,512]{2,1,0:T(8,128)(2,1)S(1)} %all-to-all-done.q_ref, bf16[1,1024,256]{2,1,0:T(8,128)(2,1)} %stored_values.1, bf16[1,1024,256]{2,1,0:T(8,128)(2,1)S(1)} %get-tuple-element.12.keys_ref, bf16[1,1,64,32,256]{4,3,2,1,0:T(8,128)(2,1)S(1)} %get-tuple-element.13.skeys_ref, ...), custom_call_target="tpu_custom_call" | custom-call | flops 1073741824 | bytes 1048576 | tf_op jit(solution)/shard_map/pallas_call | solution.py:426
  17.8 5.6 %all-to-all-start.1 = ((bf16[8,48,256]{2,1,0:T(8,128)(2,1)}), bf16[8,48,256]{2,1,0:T(8,128)(2,1)S(1)}, u32[]{:S(2)}, u32[]{:S(2)}) async-start(bf16[8,48,256]{2,1,0:T(8,128)(2,1)} %shard_map.105), calls=%async_computation.1 | async-start | bytes 393216 | tf_op jit(solution)/shard_map/all_to_all | solution.py:436
  23.3 0.0 collective-permute-done.refs_1_
  23.3 0.0 collective-permute-done.1.refs_2_
  23.3 0.0 collective-permute-done.2.refs_3_
  23.3 0.7 %shard_map.106 = bf16[4,96,256]{2,1,0:T(8,128)(2,1)} custom-call(bf16[2,96,256]{2,1,0:T(8,128)(2,1)S(1)} %get-tuple-element.18.refs_0_, bf16[2,96,256]{2,1,0:T(8,128)(2,1)S(1)} %collective-permute-done.refs_1_, bf16[2,96,256]{2,1,0:T(8,128)(2,1)S(1)} %collective-permute-done.1.refs_2_, bf16[2,96,256]{2,1,0:T(8,128)(2,1)S(1)} %collective-permute-done.2.refs_3_), custom_call_target="tpu_custom_call" | custom-call | flops 17179869184 | bytes 1000 | tf_op jit(solution)/shard_map/pallas_call | solution.py:325
  24.0 2.0 %collective-permute-start.3 = (bf16[4,96,256]{2,1,0:T(8,128)(2,1)}, bf16[4,96,256]{2,1,0:T(8,128)(2,1)S(1)}, u32[]{:S(2)}, u32[]{:S(2)}) collective-permute-start(bf16[4,96,256]{2,1,0:T(8,128)(2,1)} %shard_map.106), channel_id=1, source_target_pairs={{0,2},{2,0},{4,6},{6,4},{8,10},{10,8},{12,14},{14,12},{1,3},{3,1},... | collective-permute-start | bytes 589832 | tf_op jit(solution)/shard_map/ppermute | solution.py:384
  26.0 4.7 %collective-permute-done.3.far_ref = bf16[4,96,256]{2,1,0:T(8,128)(2,1)S(1)} collective-permute-done((bf16[4,96,256]{2,1,0:T(8,128)(2,1)}, bf16[4,96,256]{2,1,0:T(8,128)(2,1)S(1)}, u32[]{:S(2)}, u32[]{:S(2)}) %collective-permute-start.3) | collective-permute-done | bytes 196640 | tf_op jit(solution)/shard_map/ppermute | solution.py:384
  30.8 0.3 all-to-all-done.1.back_ref
  31.1 1.6 %shard_map.107 = (bf16[2,1,8,64,256]{4,3,2,1,0:T(8,128)(2,1)}, bf16[8,4096]{1,0:T(8,128)(2,1)}) custom-call(bf16[8,48,256]{2,1,0:T(8,128)(2,1)S(1)} %all-to-all-done.1.back_ref, bf16[4,96,256]{2,1,0:T(8,128)(2,1)S(1)} %collective-permute-done.3.far_ref, bf16[2,96,256]{2,1,0:T(8,128)(2,1)S(1)} %get-tuple-element.18.refs_0_, ...), custom_call_target="tpu_custom_call" | custom-call | bytes 1048576 | tf_op jit(solution)/shard_map/pallas_call | solution.py:438
Async XLA Ops:
  0.6 14.2 %all-to-all-start = ((bf16[8,8,512]{2,1,0:T(8,128)(2,1)}), bf16[8,8,512]{2,1,0:T(8,128)(2,1)S(1)}, u32[]{:S(2)}, u32[]{:S(2)}) async-start(bf16[8,8,512]{2,1,0:T(8,128)(2,1)} %bitcast.5), calls=%async_computation | async-start | bytes 131072 | tf_op jit(solution)/shard_map/all_to_all | solution.py:386
  9.9 13.4 %collective-permute-start = (bf16[2,96,256]{2,1,0:T(8,128)(2,1)}, bf16[2,96,256]{2,1,0:T(8,128)(2,1)S(1)}, u32[]{:S(2)}, u32[]{:S(2)}) collective-permute-start(bf16[2,96,256]{2,1,0:T(8,128)(2,1)} %get-tuple-element.19), channel_id=1, source_target_pairs={{0,4},{2,6},{4,0},{6,2},{8,12},{10,14},{12,8},{14,10},{1,5},{3,7},... | collective-permute-start | bytes 294920 | tf_op jit(solution)/shard_map/ppermute | solution.py:384
  12.0 11.3 %collective-permute-start.1 = (bf16[2,96,256]{2,1,0:T(8,128)(2,1)}, bf16[2,96,256]{2,1,0:T(8,128)(2,1)S(1)}, u32[]{:S(2)}, u32[]{:S(2)}) collective-permute-start(bf16[2,96,256]{2,1,0:T(8,128)(2,1)} %get-tuple-element.20), channel_id=1, source_target_pairs={{0,8},{2,10},{4,12},{6,14},{8,0},{10,2},{12,4},{14,6},{1,9},{3,11}... | collective-permute-start | bytes 294920 | tf_op jit(solution)/shard_map/ppermute | solution.py:384
  14.4 9.0 %collective-permute-start.2 = (bf16[2,96,256]{2,1,0:T(8,128)(2,1)}, bf16[2,96,256]{2,1,0:T(8,128)(2,1)S(1)}, u32[]{:S(2)}, u32[]{:S(2)}) collective-permute-start(bf16[2,96,256]{2,1,0:T(8,128)(2,1)} %get-tuple-element.21), channel_id=1, source_target_pairs={{0,12},{2,14},{4,8},{6,10},{8,4},{10,6},{12,0},{14,2},{1,13},{3,15... | collective-permute-start | bytes 294920 | tf_op jit(solution)/shard_map/ppermute | solution.py:384
  17.8 13.3 %all-to-all-start.1 = ((bf16[8,48,256]{2,1,0:T(8,128)(2,1)}), bf16[8,48,256]{2,1,0:T(8,128)(2,1)S(1)}, u32[]{:S(2)}, u32[]{:S(2)}) async-start(bf16[8,48,256]{2,1,0:T(8,128)(2,1)} %shard_map.105), calls=%async_computation.1 | async-start | bytes 393216 | tf_op jit(solution)/shard_map/all_to_all | solution.py:436
  24.0 6.8 %collective-permute-start.3 = (bf16[4,96,256]{2,1,0:T(8,128)(2,1)}, bf16[4,96,256]{2,1,0:T(8,128)(2,1)S(1)}, u32[]{:S(2)}, u32[]{:S(2)}) collective-permute-start(bf16[4,96,256]{2,1,0:T(8,128)(2,1)} %shard_map.106), channel_id=1, source_target_pairs={{0,2},{2,0},{4,6},{6,4},{8,10},{10,8},{12,14},{14,12},{1,3},{3,1},... | collective-permute-start | bytes 589832 | tf_op jit(solution)/shard_map/ppermute | solution.py:384

commit v5 on v4

--- a/solution.py
+++ b/solution.py
@@ -175,7 +175,6 @@
 
 VMEM = pl.BlockSpec(memory_space=pltpu.VMEM)
 HBM = pl.BlockSpec(memory_space=pltpu.HBM)
-WIDE = 128
 
 
 def own_column(values_ref, tall, request_rows, core_count):
@@ -186,23 +185,21 @@
     return jnp.sum(picked.astype(jnp.float32), axis=1, keepdims=True).astype(jnp.int32)
 
 
-def prepare_kernel(count, core_count, prefix_length, request_rows, riding, *refs):
-    (stored_rates, stored_assign, stored_lengths, stored_kv), stored, refs = refs[:4], refs[4:7], refs[7:]
+def prepare_kernel(count, core_count, prefix_length, riding, *refs):
+    (stored_rates, stored_kv), stored, refs = refs[:2], refs[2:5], refs[5:]
     own_ref, *pieces = refs[: count // 2]
-    which_ref, live_ref, ride_ref, *fetched = refs[count // 2 : count // 2 + 6]
-    rates_ref, assign_ref, lengths_ref, kv_ref, cut_ref, sems, out_sems = refs[count // 2 + 6 :]
+    ride_ref, *fetched = refs[count // 2 : count // 2 + 4]
+    rates_ref, kv_ref, sems = refs[count // 2 + 4 :]
     first_copies = [
         pltpu.make_async_copy(a, b, sems.at[i])
         for i, (a, b) in enumerate(
             (
                 (stored_rates, rates_ref),
                 (stored_kv, kv_ref),
-                (stored_assign, assign_ref),
-                (stored_lengths, lengths_ref),
             )
         )
     ]
-    copies = [pltpu.make_async_copy(a, b, sems.at[4 + i]) for i, (a, b) in enumerate(zip(stored, fetched))]
+    copies = [pltpu.make_async_copy(a, b, sems.at[2 + i]) for i, (a, b) in enumerate(zip(stored, fetched))]
     for copy in first_copies + copies:
         copy.start()
     first_copies[0].wait()
@@ -218,7 +215,7 @@
     for copy in first_copies[1:]:
         copy.wait()
     for j in reversed(range(count // 2)):
-        cut = cut_ref.at[j - 1] if j else own_ref
+        cut = pieces[j - 1] if j else own_ref
         for d in range(2):
             start = jnp.bitwise_xor(place, 2 * j + d) * width
             for h in range(width // HD):
@@ -227,23 +224,38 @@
                 turned = pltpu.roll(keys, HD // 2, 1)
                 cut[d, :rows, h * HD : (h + 1) * HD] = (keys * cosine + turned * sine).astype(jnp.bfloat16)
                 cut[d, rows:, h * HD : (h + 1) * HD] = kv_ref[1, : rows - riding, columns]
-        if j:
-            copies.append(pltpu.make_async_copy(cut, pieces[j - 1], out_sems.at[j - 1]))
-            copies[-1].start()
     for s in range(count):
         ride_ref[s] = kv_ref[1, rows - riding :, s * width : (s + 1) * width]
-    tall = which_ref.shape[0]
-    which_ref[...] = jnp.broadcast_to(own_column(assign_ref, tall, request_rows, core_count), which_ref.shape)
-    live_ref[...] = jnp.broadcast_to(own_column(lengths_ref, tall, request_rows, core_count), live_ref.shape)
     for copy in copies:
         copy.wait()
 
 
+def fetch(stored, target, sems):
+    parts = sems.shape[0]
+    leading = stored.shape[:-3] if len(stored.shape) > 3 else stored.shape[:1]
+    index = (0,) * len(leading)
+    rows = stored.shape[len(leading)] // parts
+    copies = []
+    for i in range(parts):
+        at = (*index, pl.ds(i * rows, rows))
+        copies.append(pltpu.make_async_copy(stored.at[at], target.at[at], sems.at[i]))
+        copies[-1].start()
+    return copies
+
+
 def attend_kernel(
-    q_ref, stored_values, keys_ref, skeys_ref, svalues_ref, which_ref, live_ref, ride_ref, out_ref, values_ref, sem
+    core_count, q_ref, stored_assign, stored_lengths, stored_svalues,
+    keys_ref, skeys_ref, values_ref, ride_ref, stored_out, svalues_ref, out_ref, assign_ref, lengths_ref, sems, out_sems,
 ):
-    fetch = pltpu.make_async_copy(stored_values, values_ref, sem)
-    fetch.start()
+    small = [
+        pltpu.make_async_copy(stored_assign, assign_ref, out_sems.at[2]),
+        pltpu.make_async_copy(stored_lengths, lengths_ref, out_sems.at[3]),
+    ]
+    for copy in small:
+        copy.start()
+    fetches = [
+        fetch(a, b, sems.at[i]) for i, (a, b) in enumerate(((stored_svalues, svalues_ref),))
+    ]
     seq_count, span, group_width = q_ref.shape
     requests = seq_count * span
     per_kv = NQH // KVH
@@ -259,21 +271,58 @@
     tall = span * len(heads)
     column = lax.broadcasted_iota(jnp.int32, (tall, span * slots), 1)
     low = lax.broadcasted_iota(jnp.int32, (tall, span * slots), 0) % span * slots
-    added, more, found = {}, {}, []
+    ride = pltpu.make_async_copy(ride_ref, stored_out.at[:, per_kv * span :], out_sems.at[0])
+    ride.start()
+    for copy in small:
+        copy.wait()
+    which = own_column(assign_ref, per_kv * requests, span, core_count)
+    live = own_column(lengths_ref, requests, span, core_count)
+    scores = []
+    for h in range(heads_here):
+        columns = slice(h * HD, (h + 1) * HD)
+        stacked = jnp.concatenate([query[h, j] for j in range(per_kv)], axis=0)
+        chosen = lax.dot_general(stacked, keys_ref[0, :length, columns], NT, preferred_element_type=jnp.float32)
+        for p in range(1, NPFX):
+            other = lax.dot_general(
+                stacked, keys_ref[0, p * length : (p + 1) * length, columns], NT, preferred_element_type=jnp.float32
+            )
+            chosen = jnp.where(which == p, other, chosen)
+        scores.append(chosen)
     blocks = [slice(b * span, (b + 1) * span) for b in range(seq_count)]
-    for rows in blocks:
-        part = jnp.concatenate(
+    parts = [
+        jnp.concatenate(
             [
                 jnp.concatenate([query32[h, j][rows] if g == h else blank for g in range(heads_here)], axis=1)
                 for h, j in heads
             ],
             axis=0,
         ).astype(jnp.bfloat16)
-        skeys = skeys_ref[0, 0, rows].reshape(span * slots, width)
-        found.append(lax.dot_general(part, skeys, NT, preferred_element_type=jnp.float32))
+        for rows in blocks
+    ]
+    found = [
+        lax.dot_general(
+            part, skeys_ref[0, 0, rows].reshape(span * slots, width), NT, preferred_element_type=jnp.float32
+        )
+        for rows, part in zip(blocks, parts)
+    ]
+    weights = [weigh(chosen) for chosen in scores]
     for b, rows in enumerate(blocks):
-        live = jnp.concatenate([live_ref[rows, :1]] * len(heads), axis=0)
-        found[b] = jnp.where((column >= low) & (column < low + live), weigh(found[b]), 0.0)
+        slots_live = jnp.concatenate([live[rows]] * len(heads), axis=0)
+        found[b] = jnp.where((column >= low) & (column < low + slots_live), weigh(found[b]), 0.0)
+    numerators = []
+    for h in range(heads_here):
+        columns = slice(h * HD, (h + 1) * HD)
+        rounded = weights[h].astype(jnp.bfloat16)
+        numerator = jnp.dot(rounded, values_ref[0, :length, columns], preferred_element_type=jnp.float32)
+        for p in range(1, NPFX):
+            other = jnp.dot(
+                rounded, values_ref[0, p * length : (p + 1) * length, columns], preferred_element_type=jnp.float32
+            )
+            numerator = jnp.where(which == p, other, numerator)
+        numerators.append(numerator)
+    added, more = {}, {}
+    for copy in fetches[0]:
+        copy.wait()
     for b, rows in enumerate(blocks):
         svalues = svalues_ref[0, 0, rows].reshape(span * slots, width)
         sums = jnp.sum(found[b], axis=1, keepdims=True)
@@ -282,37 +331,23 @@
             more[h, j, b] = sums[i * span : (i + 1) * span]
             added[h, j, b] = products[i * span : (i + 1) * span, h * HD : (h + 1) * HD]
     results = []
-    fetch.wait()
     for h in range(heads_here):
-        columns = slice(h * HD, (h + 1) * HD)
-        stacked = jnp.concatenate([query[h, j] for j in range(per_kv)], axis=0)
-        scores = lax.dot_general(stacked, keys_ref[0, :length, columns], NT, preferred_element_type=jnp.float32)
-        for p in range(1, NPFX):
-            other = lax.dot_general(
-                stacked, keys_ref[0, p * length : (p + 1) * length, columns], NT, preferred_element_type=jnp.float32
-            )
-            scores = jnp.where(which_ref[:, :1] == p, other, scores)
-        weights = weigh(scores)
-        total = jnp.sum(weights, axis=1, keepdims=True)
-        rounded = weights.astype(jnp.bfloat16)
-        numerator = jnp.dot(rounded, values_ref[0, :length, columns], preferred_element_type=jnp.float32)
-        for p in range(1, NPFX):
-            other = jnp.dot(
-                rounded, values_ref[0, p * length : (p + 1) * length, columns], preferred_element_type=jnp.float32
-            )
-            numerator = jnp.where(which_ref[...] == p, other, numerator)
-
-        def regroup(parts):
-            return jnp.concatenate([parts[h, j, b] for j in range(per_kv) for b in range(seq_count)], axis=0)
-
-        result = (numerator + regroup(added)) * (1.0 / (total + regroup(more)))
+
+        def regroup(cut):
+            return jnp.concatenate([cut[h, j, b] for j in range(per_kv) for b in range(seq_count)], axis=0)
+
+        total = jnp.sum(weights[h], axis=1, keepdims=True) + regroup(more)
+        result = (numerators[h] + regroup(added)) * (1.0 / total)
         for j in range(per_kv):
             results.append(result[j * requests : (j + 1) * requests].reshape(seq_count, span, HD))
     for c in range(heads_here):
-        out_ref[:, : per_kv * span, c * HD : (c + 1) * HD] = jnp.concatenate(
+        out_ref[:, :, c * HD : (c + 1) * HD] = jnp.concatenate(
             [results[t * heads_here + c] for t in range(per_kv)], axis=1
         ).astype(jnp.bfloat16)
-    out_ref[:, per_kv * span :, :] = ride_ref[...]
+    out = pltpu.make_async_copy(out_ref, stored_out.at[:, : per_kv * span], out_sems.at[1])
+    out.start()
+    ride.wait()
+    out.wait()
 
 
 def forward_kernel(*refs):
@@ -324,7 +359,7 @@
 def forward(pieces):
     return pl.pallas_call(
         forward_kernel,
-        out_shape=jax.ShapeDtypeStruct((len(pieces), *pieces[0].shape[1:]), pieces[0].dtype),
+        out_shape=pltpu.VMEM((len(pieces), *pieces[0].shape[1:]), pieces[0].dtype),
         in_specs=[VMEM] * len(pieces),
         out_specs=VMEM,
         cost_estimate=pl.CostEstimate(flops=2**34, bytes_accessed=1000, transcendentals=0),
@@ -332,7 +367,7 @@
 
 
 def finish_kernel(count, back_ref, far_ref, *refs):
-    *near, cache_ref, attention_ref, sems = refs
+    *near, cache_ref, stored_attention, attention_ref, sems = refs
     place = lax.axis_index("seq")
     rows = cache_ref.shape[3]
     request_rows = attention_ref.shape[0]
@@ -356,12 +391,14 @@
     )
     for copy in copies:
         copy.start()
+    copies.append(pltpu.make_async_copy(attention_ref, stored_attention, sems.at[1, 2]))
     for s in range(count):
         block = back_ref[s, : parts * request_rows].astype(jnp.float32)
         for t in range(parts):
             attention_ref[:, (s * parts + t) * width : (s * parts + t + 1) * width] = block[
                 t * request_rows : (t + 1) * request_rows
             ].astype(jnp.bfloat16)
+    copies[-1].start()
     for copy in copies:
         copy.wait()
 
@@ -376,7 +413,6 @@
     prefix_rows = new_kv.shape[1]
     group_width = queries.shape[1] // seq_count
     width = new_kv.shape[2] // seq_count
-    tall = NQH // KVH * seq_count * request_rows
     prefix_length = prefix_rows * seq_count * core_count // NPFX
     rates = (10000.0 ** (-2.0 * (np.arange(HD) % (HD // 2)) / HD)).astype(np.float32)
 
@@ -386,28 +422,23 @@
     asked = lax.all_to_all(
         queries.reshape(request_rows, seq_count, group_width).transpose(1, 0, 2), "seq", 0, 0, tiled=True
     )
-    stored = (old_keys, suffix_keys, suffix_values)
+    early = (old_keys, suffix_keys, old_values, )
+    late = (suffix_values,)
     riding = 32
     piece = (2, 2 * prefix_rows - riding, width)
     packed = NQH // KVH * request_rows + riding
-    column = pltpu.VMEM((tall, WIDE), jnp.int32)
     prepared = pl.pallas_call(
-        functools.partial(prepare_kernel, seq_count, core_count, prefix_length, request_rows, riding),
+        functools.partial(prepare_kernel, seq_count, core_count, prefix_length, riding),
         out_shape=[pltpu.VMEM(piece, jnp.bfloat16)]
-        + [pltpu.HBM(piece, jnp.bfloat16)] * (half - 1)
-        + [column] * 2
+        + [pltpu.VMEM(piece, jnp.bfloat16)] * (half - 1)
         + [pltpu.VMEM((seq_count, riding, width), jnp.bfloat16)]
-        + [pltpu.VMEM(x.shape, x.dtype) for x in stored],
-        in_specs=[HBM] * 7,
-        out_specs=[VMEM] + [HBM] * (half - 1) + [VMEM] * 6,
+        + [pltpu.VMEM(x.shape, x.dtype) for x in early],
+        in_specs=[HBM] * 5,
+        out_specs=[VMEM] * (half + 4),
         scratch_shapes=[
             pltpu.VMEM((1, HD), jnp.float32),
-            pltpu.VMEM((1, assign.shape[0]), jnp.int32),
-            pltpu.VMEM((1, assign.shape[0]), jnp.int32),
             pltpu.VMEM(new_kv.shape, jnp.bfloat16),
-            pltpu.VMEM((half - 1, *piece), jnp.bfloat16),
-            pltpu.SemaphoreType.DMA((7,)),
-            pltpu.SemaphoreType.DMA((half - 1,)),
+            pltpu.SemaphoreType.DMA((5,)),
         ],
         cost_estimate=pl.CostEstimate(flops=2**33, bytes_accessed=1000, transcendentals=0),
         compiler_params=pltpu.CompilerParams(vmem_limit_bytes=16 * 2**20),
@@ -415,23 +446,35 @@
         *(
             pin(x, pltpu.HBM)
             for x in (
-                jnp.asarray(rates).reshape(1, HD), assign.reshape(1, -1), lengths.reshape(1, -1), new_kv, *stored
+                jnp.asarray(rates).reshape(1, HD), new_kv, *early
             )
         )
     )
-    kv_cuts, (which, live, ride, *fetched) = prepared[:half], prepared[half:]
+    kv_cuts, (ride, *fetched) = prepared[:half], prepared[half:]
     kv_near = [kv_cuts[0]]
     for j in range(1, half):
         kv_near.append(swap(kv_cuts[j], 2 * j))
     attended = pl.pallas_call(
-        attend_kernel,
-        out_shape=pltpu.VMEM((seq_count, packed, width), jnp.bfloat16),
-        in_specs=[VMEM, HBM] + [VMEM] * 6,
-        out_specs=VMEM,
-        scratch_shapes=[pltpu.VMEM(old_values.shape, jnp.bfloat16), pltpu.SemaphoreType.DMA(())],
+        functools.partial(attend_kernel, core_count),
+        out_shape=pltpu.HBM((seq_count, packed, width), jnp.bfloat16),
+        in_specs=[VMEM] + [HBM] * (2 + len(late)) + [VMEM] * (len(early) + 1),
+        out_specs=HBM,
+        scratch_shapes=[
+            *(pltpu.VMEM(x.shape, x.dtype) for x in late),
+            pltpu.VMEM((seq_count, packed - riding, width), jnp.bfloat16),
+            pltpu.VMEM((1, assign.shape[0]), jnp.int32),
+            pltpu.VMEM((1, assign.shape[0]), jnp.int32),
+            pltpu.SemaphoreType.DMA((len(late), 4)),
+            pltpu.SemaphoreType.DMA((4,)),
+        ],
         compiler_params=pltpu.CompilerParams(vmem_limit_bytes=16 * 2**20),
         cost_estimate=pl.CostEstimate(flops=2**30, bytes_accessed=2**20, transcendentals=2**10),
-    )(pin(asked), pin(old_values, pltpu.HBM), *(pin(x) for x in fetched), pin(which), pin(live), pin(ride))
+    )(
+        pin(asked),
+        *(pin(x, pltpu.HBM) for x in (assign.reshape(1, -1), lengths.reshape(1, -1), *late)),
+        *(pin(x) for x in fetched),
+        pin(ride),
+    )
     kv_far = swap(forward(kv_near), 1)
     back = lax.all_to_all(attended, "seq", 0, 0, tiled=True)
     return tuple(
@@ -442,8 +485,11 @@
                 jax.ShapeDtypeStruct((request_rows, NQH * HD), jnp.bfloat16),
             ),
             in_specs=[VMEM] * (half + 2),
-            out_specs=(HBM, VMEM),
-            scratch_shapes=[pltpu.SemaphoreType.DMA((seq_count, 3))],
+            out_specs=(HBM, HBM),
+            scratch_shapes=[
+                pltpu.VMEM((request_rows, NQH * HD), jnp.bfloat16),
+                pltpu.SemaphoreType.DMA((seq_count, 3)),
+            ],
             cost_estimate=pl.CostEstimate(flops=0, bytes_accessed=2**20, transcendentals=0),
         )(*(pin(x) for x in (back, kv_far, *kv_near)))
     )

time: 33.1 us -> 31.9 us (0.964)
  Pallas kernels: 7.25 us -> 5.42 us
  waiting for transfers between devices: 5.44 us -> 6.3 us
    pallas_call x2, Pallas kernels: 3.6 us -> 2.67 us  [the longest x1 2.65 us: local(): pl.pallas_call(functools.partial(attend_kernel, core_count), out_shape=pl...]
    pallas_call x1, Pallas kernels: 1.63 us -> 1.02 us  [local(): pl.pallas_call(functools.partial(finish_kernel, seq_count), out_shape=(ja...]
    all_to_all x1, waiting for transfers between devices: 0.32 us -> 0.77 us  [local(): back = lax.all_to_all(attended, 'seq', 0, 0, tiled=True)]
  transfers between devices with their start and end apart: 6 -> 6, of which waited for: 3 -> 3; matrix products, arithmetic and copies ran while one was open for 0% -> 0% of each run, Pallas kernels for 17% -> 14%
where the time goes in v5:
time: 31.9 us; the launch traced here: 31.6 us
  starting transfers between devices  19.2 us (60%)
  waiting for transfers between devices  6.3 us (20%)
  Pallas kernels  5.42 us (17%)
  between operations  0.68 us (2%)
    all_to_all x1, starting transfers between devices, local(): lax.all_to_all(queries.reshape(request_rows, seq_count, group_width).tran...  7.26 us
    ppermute x4, starting transfers between devices, swap(): return lax.ppermute(x, 'seq', [(i, i ^ k) for i in range(seq_count)])  6.61 us
    all_to_all x1, starting transfers between devices, local(): back = lax.all_to_all(attended, 'seq', 0, 0, tiled=True)  5.29 us
    ppermute x4, waiting for transfers between devices, swap(): return lax.ppermute(x, 'seq', [(i, i ^ k) for i in range(seq_count)])  4.89 us
    pallas_call x1, Pallas kernels, local(): pl.pallas_call(functools.partial(attend_kernel, core_count), out_shape=pl...  2.65 us
    pallas_call x1, Pallas kernels, local(): pl.pallas_call(functools.partial(prepare_kernel, seq_count, core_count, p...  1.73 us
    pallas_call x1, Pallas kernels, local(): pl.pallas_call(functools.partial(finish_kernel, seq_count), out_shape=(ja...  1.02 us
    all_to_all x1, waiting for transfers between devices, local(): back = lax.all_to_all(attended, 'seq', 0, 0, tiled=True)  0.77 us
  transfers between devices with their start and end apart: 6, of which 3 were waited for; matrix products, arithmetic and copies ran while one was open for 0% of the time, Pallas kernels for 14%

profile of v5, /device:TPU:0, one launch (start us, length us, event | category | flops | bytes accessed | tf_op | source)
XLA Modules:
  0.0 31.6 jit_solution(1208033730078211588)
XLA Ops:
  0.6 7.3 %all-to-all-start = ((bf16[8,8,512]{2,1,0:T(8,128)(2,1)}), bf16[8,8,512]{2,1,0:T(8,128)(2,1)S(1)}, u32[]{:S(2)}, u32[]{:S(2)}) async-start(bf16[8,8,512]{2,1,0:T(8,128)(2,1)} %bitcast.5), calls=%async_computation | async-start | bytes 131072 | tf_op jit(solution)/shard_map/all_to_all | solution.py:422
  7.9 1.7 %shard_map.104 = (bf16[2,96,256]{2,1,0:T(8,128)(2,1)S(1)}, bf16[2,96,256]{2,1,0:T(8,128)(2,1)S(1)}, bf16[2,96,256]{2,1,0:T(8,128)(2,1)S(1)}, bf16[2,96,256]{2,1,...) custom-call(f32[1,128]{1,0:T(1,128)} %constant.8.refs_0_, ...), custom_call_target="tpu_custom_call" | custom-call | flops 8589934592 | bytes 1000 | tf_op jit(solution)/shard_map/pallas_call | solution.py:430
  9.6 2.1 %collective-permute-start = (bf16[2,96,256]{2,1,0:T(8,128)(2,1)S(1)}, bf16[2,96,256]{2,1,0:T(8,128)(2,1)S(1)}, u32[]{:S(2)}, u32[]{:S(2)}) collective-permute-start(bf16[2,96,256]{2,1,0:T(8,128)(2,1)S(1)} %get-tuple-element.15), channel_id=1, source_target_pairs={{0,4},{2,6},{4,0},{6,2},{8,12},{10,14},{12,8},{14,10},{1,5},{3,7},... | collective-permute-start | bytes 294920 | tf_op jit(solution)/shard_map/ppermute | solution.py:420
  11.7 2.4 %collective-permute-start.1 = (bf16[2,96,256]{2,1,0:T(8,128)(2,1)S(1)}, bf16[2,96,256]{2,1,0:T(8,128)(2,1)S(1)}, u32[]{:S(2)}, u32[]{:S(2)}) collective-permute-start(bf16[2,96,256]{2,1,0:T(8,128)(2,1)S(1)} %get-tuple-element.16), channel_id=1, source_target_pairs={{0,8},{2,10},{4,12},{6,14},{8,0},{10,2},{12,4},{14,6},{1,9},{3,11}... | collective-permute-start | bytes 294920 | tf_op jit(solution)/shard_map/ppermute | solution.py:420
  14.1 0.1 collective-permute-start.2
  14.2 0.6 %all-to-all-done.q_ref = bf16[8,8,512]{2,1,0:T(8,128)(2,1)S(1)} async-done(((bf16[8,8,512]{2,1,0:T(8,128)(2,1)}), bf16[8,8,512]{2,1,0:T(8,128)(2,1)S(1)}, u32[]{:S(2)}, u32[]{:S(2)}) %all-to-all-start) | async-done | bytes 65568 | tf_op jit(solution)/shard_map/all_to_all | solution.py:422
  14.8 2.7 %shard_map.105 = bf16[8,48,256]{2,1,0:T(8,128)(2,1)} custom-call(bf16[8,8,512]{2,1,0:T(8,128)(2,1)S(1)} %all-to-all-done.q_ref, s32[1,128]{1,0:T(1,128)} %bitcast.6, s32[1,128]{1,0:T(1,128)} %bitcast.7, bf16[1,1,64,32,256]{4,3,2,1,0:T(8,128)(2,1)} %stored_svalues.1, bf16[1,1024,256]{2,1,0:T(8,128)(2,1)S(1)} %get-tuple-element.10.keys_ref, ...), custom_call_target="tpu_custom_call" | custom-call | flops 1073741824 | bytes 1048576 | tf_op jit(solution)/shard_map/pallas_call | solution.py:457
  17.5 5.3 %all-to-all-start.1 = ((bf16[8,48,256]{2,1,0:T(8,128)(2,1)}), bf16[8,48,256]{2,1,0:T(8,128)(2,1)S(1)}, u32[]{:S(2)}, u32[]{:S(2)}) async-start(bf16[8,48,256]{2,1,0:T(8,128)(2,1)} %shard_map.105), calls=%async_computation.1 | async-start | bytes 393216 | tf_op jit(solution)/shard_map/all_to_all | solution.py:479
  22.8 0.0 collective-permute-done.refs_1_
  22.8 0.0 collective-permute-done.1.refs_2_
  22.8 0.0 collective-permute-done.2.refs_3_
  22.8 2.1 %collective-permute-start.3 = (bf16[4,96,256]{2,1,0:T(8,128)(2,1)S(1)}, bf16[4,96,256]{2,1,0:T(8,128)(2,1)S(1)}, u32[]{:S(2)}, u32[]{:S(2)}) collective-permute-start(bf16[4,96,256]{2,1,0:T(8,128)(2,1)S(1)} %shard_map.106), channel_id=1, source_target_pairs={{0,2},{2,0},{4,6},{6,4},{8,10},{10,8},{12,14},{14,12},{1,3},{3,1},... | collective-permute-start | bytes 589832 | tf_op jit(solution)/shard_map/ppermute | solution.py:420
  24.9 4.9 %collective-permute-done.3.far_ref = bf16[4,96,256]{2,1,0:T(8,128)(2,1)S(1)} collective-permute-done((bf16[4,96,256]{2,1,0:T(8,128)(2,1)S(1)}, bf16[4,96,256]{2,1,0:T(8,128)(2,1)S(1)}, u32[]{:S(2)}, u32[]{:S(2)}) %collective-permute-start.3) | collective-permute-done | bytes 196640 | tf_op jit(solution)/shard_map/ppermute | solution.py:420
  29.8 0.8 %all-to-all-done.1.back_ref = bf16[8,48,256]{2,1,0:T(8,128)(2,1)S(1)} async-done(((bf16[8,48,256]{2,1,0:T(8,128)(2,1)}), bf16[8,48,256]{2,1,0:T(8,128)(2,1)S(1)}, u32[]{:S(2)}, u32[]{:S(2)}) %all-to-all-start.1) | async-done | bytes 196640 | tf_op jit(solution)/shard_map/all_to_all | solution.py:479
  30.5 1.0 %shard_map.107 = (bf16[2,1,8,64,256]{4,3,2,1,0:T(8,128)(2,1)}, bf16[8,4096]{1,0:T(8,128)(2,1)}) custom-call(bf16[8,48,256]{2,1,0:T(8,128)(2,1)S(1)} %all-to-all-done.1.back_ref, bf16[4,96,256]{2,1,0:T(8,128)(2,1)S(1)} %collective-permute-done.3.far_ref, bf16[2,96,256]{2,1,0:T(8,128)(2,1)S(1)} %get-tuple-element.14.refs_0_, ...), custom_call_target="tpu_custom_call" | custom-call | bytes 1048576 | tf_op jit(solution)/shard_map/pallas_call | solution.py:481
  (1 shorter events, 0.0 us)
Async XLA Ops:
  0.6 14.2 %all-to-all-start = ((bf16[8,8,512]{2,1,0:T(8,128)(2,1)}), bf16[8,8,512]{2,1,0:T(8,128)(2,1)S(1)}, u32[]{:S(2)}, u32[]{:S(2)}) async-start(bf16[8,8,512]{2,1,0:T(8,128)(2,1)} %bitcast.5), calls=%async_computation | async-start | bytes 131072 | tf_op jit(solution)/shard_map/all_to_all | solution.py:422
  9.6 13.1 %collective-permute-start = (bf16[2,96,256]{2,1,0:T(8,128)(2,1)S(1)}, bf16[2,96,256]{2,1,0:T(8,128)(2,1)S(1)}, u32[]{:S(2)}, u32[]{:S(2)}) collective-permute-start(bf16[2,96,256]{2,1,0:T(8,128)(2,1)S(1)} %get-tuple-element.15), channel_id=1, source_target_pairs={{0,4},{2,6},{4,0},{6,2},{8,12},{10,14},{12,8},{14,10},{1,5},{3,7},... | collective-permute-start | bytes 294920 | tf_op jit(solution)/shard_map/ppermute | solution.py:420
  11.7 11.1 %collective-permute-start.1 = (bf16[2,96,256]{2,1,0:T(8,128)(2,1)S(1)}, bf16[2,96,256]{2,1,0:T(8,128)(2,1)S(1)}, u32[]{:S(2)}, u32[]{:S(2)}) collective-permute-start(bf16[2,96,256]{2,1,0:T(8,128)(2,1)S(1)} %get-tuple-element.16), channel_id=1, source_target_pairs={{0,8},{2,10},{4,12},{6,14},{8,0},{10,2},{12,4},{14,6},{1,9},{3,11}... | collective-permute-start | bytes 294920 | tf_op jit(solution)/shard_map/ppermute | solution.py:420
  14.1 8.7 %collective-permute-start.2 = (bf16[2,96,256]{2,1,0:T(8,128)(2,1)S(1)}, bf16[2,96,256]{2,1,0:T(8,128)(2,1)S(1)}, u32[]{:S(2)}, u32[]{:S(2)}) collective-permute-start(bf16[2,96,256]{2,1,0:T(8,128)(2,1)S(1)} %get-tuple-element.17), channel_id=1, source_target_pairs={{0,12},{2,14},{4,8},{6,10},{8,4},{10,6},{12,0},{14,2},{1,13},{3,15... | collective-permute-start | bytes 294920 | tf_op jit(solution)/shard_map/ppermute | solution.py:420
  17.5 13.1 %all-to-all-start.1 = ((bf16[8,48,256]{2,1,0:T(8,128)(2,1)}), bf16[8,48,256]{2,1,0:T(8,128)(2,1)S(1)}, u32[]{:S(2)}, u32[]{:S(2)}) async-start(bf16[8,48,256]{2,1,0:T(8,128)(2,1)} %shard_map.105), calls=%async_computation.1 | async-start | bytes 393216 | tf_op jit(solution)/shard_map/all_to_all | solution.py:479
  22.8 7.0 %collective-permute-start.3 = (bf16[4,96,256]{2,1,0:T(8,128)(2,1)S(1)}, bf16[4,96,256]{2,1,0:T(8,128)(2,1)S(1)}, u32[]{:S(2)}, u32[]{:S(2)}) collective-permute-start(bf16[4,96,256]{2,1,0:T(8,128)(2,1)S(1)} %shard_map.106), channel_id=1, source_target_pairs={{0,2},{2,0},{4,6},{6,4},{8,10},{10,8},{12,14},{14,12},{1,3},{3,1},... | collective-permute-start | bytes 589832 | tf_op jit(solution)/shard_map/ppermute | solution.py:420

commit v6 on v5

--- a/solution.py
+++ b/solution.py
@@ -3,7 +3,6 @@
 
 import jax
 import jax.numpy as jnp
-import numpy as np
 from jax import lax
 from jax.experimental import pallas as pl
 from jax.experimental.pallas import tpu as pltpu
@@ -185,49 +184,33 @@
     return jnp.sum(picked.astype(jnp.float32), axis=1, keepdims=True).astype(jnp.int32)
 
 
-def prepare_kernel(count, core_count, prefix_length, riding, *refs):
-    (stored_rates, stored_kv), stored, refs = refs[:2], refs[2:5], refs[5:]
-    own_ref, *pieces = refs[: count // 2]
-    ride_ref, *fetched = refs[count // 2 : count // 2 + 4]
-    rates_ref, kv_ref, sems = refs[count // 2 + 4 :]
-    first_copies = [
-        pltpu.make_async_copy(a, b, sems.at[i])
-        for i, (a, b) in enumerate(
-            (
-                (stored_rates, rates_ref),
-                (stored_kv, kv_ref),
-            )
-        )
-    ]
-    copies = [pltpu.make_async_copy(a, b, sems.at[2 + i]) for i, (a, b) in enumerate(zip(stored, fetched))]
-    for copy in first_copies + copies:
-        copy.start()
-    first_copies[0].wait()
+def rates_kernel(rates_ref):
+    step = lax.broadcasted_iota(jnp.int32, rates_ref.shape, 1) % (HD // 2)
+    rates_ref[...] = jnp.exp2(step.astype(jnp.float32) * (-2.0 / HD * math.log2(10000.0)))
+
+
+def prepare_kernel(count, core_count, prefix_length, riding, rates_ref, kv_ref, *refs):
+    *pieces, ride_ref = refs
     place = lax.axis_index("seq")
     rows = kv_ref.shape[1]
     width = kv_ref.shape[2] // count
     first = (place * core_count + lax.axis_index("pd")) * rows
     position = (first + lax.broadcasted_iota(jnp.int32, (rows, HD), 0)) % prefix_length
-    angles = position.astype(jnp.float32) * rates_ref[...]
+    angles = position.astype(jnp.float32) * rates_ref[:1]
     cosine = jnp.cos(angles)
     sine = jnp.sin(angles)
     sine = jnp.where(lax.broadcasted_iota(jnp.int32, (rows, HD), 1) < HD // 2, -sine, sine)
-    for copy in first_copies[1:]:
-        copy.wait()
     for j in reversed(range(count // 2)):
-        cut = pieces[j - 1] if j else own_ref
         for d in range(2):
             start = jnp.bitwise_xor(place, 2 * j + d) * width
             for h in range(width // HD):
                 columns = pl.ds(pl.multiple_of(start + h * HD, HD), HD)
                 keys = kv_ref[0, :, columns].astype(jnp.float32)
                 turned = pltpu.roll(keys, HD // 2, 1)
-                cut[d, :rows, h * HD : (h + 1) * HD] = (keys * cosine + turned * sine).astype(jnp.bfloat16)
-                cut[d, rows:, h * HD : (h + 1) * HD] = kv_ref[1, : rows - riding, columns]
+                pieces[j][d, :rows, h * HD : (h + 1) * HD] = (keys * cosine + turned * sine).astype(jnp.bfloat16)
+                pieces[j][d, rows:, h * HD : (h + 1) * HD] = kv_ref[1, : rows - riding, columns]
     for s in range(count):
         ride_ref[s] = kv_ref[1, rows - riding :, s * width : (s + 1) * width]
-    for copy in copies:
-        copy.wait()
 
 
 def fetch(stored, target, sems):
@@ -273,46 +256,43 @@
     low = lax.broadcasted_iota(jnp.int32, (tall, span * slots), 0) % span * slots
     ride = pltpu.make_async_copy(ride_ref, stored_out.at[:, per_kv * span :], out_sems.at[0])
     ride.start()
-    for copy in small:
-        copy.wait()
-    which = own_column(assign_ref, per_kv * requests, span, core_count)
-    live = own_column(lengths_ref, requests, span, core_count)
-    scores = []
-    for h in range(heads_here):
-        columns = slice(h * HD, (h + 1) * HD)
-        stacked = jnp.concatenate([query[h, j] for j in range(per_kv)], axis=0)
-        chosen = lax.dot_general(stacked, keys_ref[0, :length, columns], NT, preferred_element_type=jnp.float32)
-        for p in range(1, NPFX):
-            other = lax.dot_general(
-                stacked, keys_ref[0, p * length : (p + 1) * length, columns], NT, preferred_element_type=jnp.float32
-            )
-            chosen = jnp.where(which == p, other, chosen)
-        scores.append(chosen)
     blocks = [slice(b * span, (b + 1) * span) for b in range(seq_count)]
-    parts = [
-        jnp.concatenate(
+    found = []
+    for rows in blocks:
+        part = jnp.concatenate(
             [
                 jnp.concatenate([query32[h, j][rows] if g == h else blank for g in range(heads_here)], axis=1)
                 for h, j in heads
             ],
             axis=0,
         ).astype(jnp.bfloat16)
-        for rows in blocks
-    ]
-    found = [
-        lax.dot_general(
-            part, skeys_ref[0, 0, rows].reshape(span * slots, width), NT, preferred_element_type=jnp.float32
-        )
-        for rows, part in zip(blocks, parts)
-    ]
-    weights = [weigh(chosen) for chosen in scores]
+        skeys = skeys_ref[0, 0, rows].reshape(span * slots, width)
+        found.append(lax.dot_general(part, skeys, NT, preferred_element_type=jnp.float32))
+    for copy in small:
+        copy.wait()
+    which = own_column(assign_ref, per_kv * requests, span, core_count)
+    live = own_column(lengths_ref, requests, span, core_count)
+    added, more = {}, {}
     for b, rows in enumerate(blocks):
         slots_live = jnp.concatenate([live[rows]] * len(heads), axis=0)
-        found[b] = jnp.where((column >= low) & (column < low + slots_live), weigh(found[b]), 0.0)
-    numerators = []
+        weights = jnp.where((column >= low) & (column < low + slots_live), weigh(found[b]), 0.0)
+        sums = jnp.sum(weights, axis=1, keepdims=True)
+        for i, (h, j) in enumerate(heads):
+            more[h, j, b] = sums[i * span : (i + 1) * span]
+        found[b] = weights.astype(jnp.bfloat16)
+    numerators, totals = [], []
     for h in range(heads_here):
         columns = slice(h * HD, (h + 1) * HD)
-        rounded = weights[h].astype(jnp.bfloat16)
+        stacked = jnp.concatenate([query[h, j] for j in range(per_kv)], axis=0)
+        scores = lax.dot_general(stacked, keys_ref[0, :length, columns], NT, preferred_element_type=jnp.float32)
+        for p in range(1, NPFX):
+            other = lax.dot_general(
+                stacked, keys_ref[0, p * length : (p + 1) * length, columns], NT, preferred_element_type=jnp.float32
+            )
+            scores = jnp.where(which == p, other, scores)
+        weights = weigh(scores)
+        totals.append(jnp.sum(weights, axis=1, keepdims=True))
+        rounded = weights.astype(jnp.bfloat16)
         numerator = jnp.dot(rounded, values_ref[0, :length, columns], preferred_element_type=jnp.float32)
         for p in range(1, NPFX):
             other = jnp.dot(
@@ -320,15 +300,12 @@
             )
             numerator = jnp.where(which == p, other, numerator)
         numerators.append(numerator)
-    added, more = {}, {}
     for copy in fetches[0]:
         copy.wait()
     for b, rows in enumerate(blocks):
         svalues = svalues_ref[0, 0, rows].reshape(span * slots, width)
-        sums = jnp.sum(found[b], axis=1, keepdims=True)
-        products = jnp.dot(found[b].astype(jnp.bfloat16), svalues, preferred_element_type=jnp.float32)
+        products = jnp.dot(found[b], svalues, preferred_element_type=jnp.float32)
         for i, (h, j) in enumerate(heads):
-            more[h, j, b] = sums[i * span : (i + 1) * span]
             added[h, j, b] = products[i * span : (i + 1) * span, h * HD : (h + 1) * HD]
     results = []
     for h in range(heads_here):
@@ -336,8 +313,7 @@
         def regroup(cut):
             return jnp.concatenate([cut[h, j, b] for j in range(per_kv) for b in range(seq_count)], axis=0)
 
-        total = jnp.sum(weights[h], axis=1, keepdims=True) + regroup(more)
-        result = (numerators[h] + regroup(added)) * (1.0 / total)
+        result = (numerators[h] + regroup(added)) * (1.0 / (totals[h] + regroup(more)))
         for j in range(per_kv):
             results.append(result[j * requests : (j + 1) * requests].reshape(seq_count, span, HD))
     for c in range(heads_here):
@@ -414,7 +390,13 @@
     group_width = queries.shape[1] // seq_count
     width = new_kv.shape[2] // seq_count
     prefix_length = prefix_rows * seq_count * core_count // NPFX
-    rates = (10000.0 ** (-2.0 * (np.arange(HD) % (HD // 2)) / HD)).astype(np.float32)
+    rates = pl.pallas_call(
+        rates_kernel,
+        out_shape=pltpu.VMEM((8, HD), jnp.float32),
+        out_specs=VMEM,
+        cost_estimate=pl.CostEstimate(flops=2**33, bytes_accessed=1000, transcendentals=0),
+    )()
+    queries, rates = lax.optimization_barrier((queries, rates))
 
     def swap(x, k):
         return lax.ppermute(x, "seq", [(i, i ^ k) for i in range(seq_count)])
@@ -422,35 +404,19 @@
     asked = lax.all_to_all(
         queries.reshape(request_rows, seq_count, group_width).transpose(1, 0, 2), "seq", 0, 0, tiled=True
     )
-    early = (old_keys, suffix_keys, old_values, )
+    early = (old_keys, suffix_keys, old_values)
     late = (suffix_values,)
     riding = 32
     piece = (2, 2 * prefix_rows - riding, width)
     packed = NQH // KVH * request_rows + riding
-    prepared = pl.pallas_call(
+    *kv_cuts, ride = pl.pallas_call(
         functools.partial(prepare_kernel, seq_count, core_count, prefix_length, riding),
-        out_shape=[pltpu.VMEM(piece, jnp.bfloat16)]
-        + [pltpu.VMEM(piece, jnp.bfloat16)] * (half - 1)
-        + [pltpu.VMEM((seq_count, riding, width), jnp.bfloat16)]
-        + [pltpu.VMEM(x.shape, x.dtype) for x in early],
-        in_specs=[HBM] * 5,
-        out_specs=[VMEM] * (half + 4),
-        scratch_shapes=[
-            pltpu.VMEM((1, HD), jnp.float32),
-            pltpu.VMEM(new_kv.shape, jnp.bfloat16),
-            pltpu.SemaphoreType.DMA((5,)),
-        ],
+        out_shape=[pltpu.VMEM(piece, jnp.bfloat16)] * half + [pltpu.VMEM((seq_count, riding, width), jnp.bfloat16)],
+        in_specs=[VMEM] * 2,
+        out_specs=[VMEM] * (half + 1),
         cost_estimate=pl.CostEstimate(flops=2**33, bytes_accessed=1000, transcendentals=0),
         compiler_params=pltpu.CompilerParams(vmem_limit_bytes=16 * 2**20),
-    )(
-        *(
-            pin(x, pltpu.HBM)
-            for x in (
-                jnp.asarray(rates).reshape(1, HD), new_kv, *early
-            )
-        )
-    )
-    kv_cuts, (ride, *fetched) = prepared[:half], prepared[half:]
+    )(pin(rates), pin(new_kv))
     kv_near = [kv_cuts[0]]
     for j in range(1, half):
         kv_near.append(swap(kv_cuts[j], 2 * j))
@@ -472,7 +438,7 @@
     )(
         pin(asked),
         *(pin(x, pltpu.HBM) for x in (assign.reshape(1, -1), lengths.reshape(1, -1), *late)),
-        *(pin(x) for x in fetched),
+        *(pin(x) for x in early),
         pin(ride),
     )
     kv_far = swap(forward(kv_near), 1)

time: 31.9 us -> 30.5 us (0.956)
  waiting for transfers between devices: 6.3 us -> 8.21 us
  starting transfers between devices: 19.2 us -> 17.4 us
  Pallas kernels: 5.42 us -> 3.84 us
    all_to_all x1, waiting for transfers between devices: 0.64 us -> 2.55 us  [local(): lax.all_to_all(queries.reshape(request_rows, seq_count, group_width).tran...]
    all_to_all x1, starting transfers between devices: 5.29 us -> 3.4 us  [local(): back = lax.all_to_all(attended, 'seq', 0, 0, tiled=True)]
    pallas_call x1, Pallas kernels: 1.73 us -> 0.29 us  [local(): pl.pallas_call(functools.partial(prepare_kernel, seq_count, core_count, p...]
  transfers between devices with their start and end apart: 6 -> 6, of which waited for: 3 -> 3; matrix products, arithmetic and copies ran while one was open for 0% -> 0% of each run, Pallas kernels for 14% -> 9%
where the time goes in v6:
time: 30.5 us; the launch traced here: 30.2 us
  starting transfers between devices  17.4 us (57%)
  waiting for transfers between devices  8.21 us (27%)
  Pallas kernels  3.84 us (13%)
  between operations  0.73 us (2%)
    all_to_all x1, starting transfers between devices, local(): lax.all_to_all(queries.reshape(request_rows, seq_count, group_width).tran...  7.4 us
    ppermute x4, starting transfers between devices, swap(): return lax.ppermute(x, 'seq', [(i, i ^ k) for i in range(seq_count)])  6.57 us
    ppermute x4, waiting for transfers between devices, swap(): return lax.ppermute(x, 'seq', [(i, i ^ k) for i in range(seq_count)])  4.88 us
    all_to_all x1, starting transfers between devices, local(): back = lax.all_to_all(attended, 'seq', 0, 0, tiled=True)  3.4 us
    all_to_all x1, waiting for transfers between devices, local(): lax.all_to_all(queries.reshape(request_rows, seq_count, group_width).tran...  2.55 us
    pallas_call x1, Pallas kernels, local(): pl.pallas_call(functools.partial(attend_kernel, core_count), out_shape=pl...  2.51 us
    pallas_call x1, Pallas kernels, local(): pl.pallas_call(functools.partial(finish_kernel, seq_count), out_shape=(ja...  1.02 us
    all_to_all x1, waiting for transfers between devices, local(): back = lax.all_to_all(attended, 'seq', 0, 0, tiled=True)  0.78 us
  transfers between devices with their start and end apart: 6, of which 3 were waited for; matrix products, arithmetic and copies ran while one was open for 0% of the time, Pallas kernels for 9%

profile of v6, /device:TPU:0, one launch (start us, length us, event | category | flops | bytes accessed | tf_op | source)
XLA Modules:
  0.0 30.2 jit_solution(2020639503960744612)
XLA Ops:
  0.6 0.0 copy-start.1
  0.7 7.4 %all-to-all-start = ((bf16[8,8,512]{2,1,0:T(8,128)(2,1)}), bf16[8,8,512]{2,1,0:T(8,128)(2,1)S(1)}, u32[]{:S(2)}, u32[]{:S(2)}) async-start(bf16[8,8,512]{2,1,0:T(8,128)(2,1)} %bitcast.1), calls=%async_computation | async-start | bytes 131072 | tf_op jit(solution)/shard_map/all_to_all | solution.py:404
  8.0 0.0 copy-done.1
  8.1 0.0 copy-start
  8.1 0.0 copy-start.2
  8.1 0.0 copy-start.3
  8.1 0.3 shard_map.96
  8.4 2.1 %collective-permute-start = (bf16[2,96,256]{2,1,0:T(8,128)(2,1)S(1)}, bf16[2,96,256]{2,1,0:T(8,128)(2,1)S(1)}, u32[]{:S(2)}, u32[]{:S(2)}) collective-permute-start(bf16[2,96,256]{2,1,0:T(8,128)(2,1)S(1)} %get-tuple-element.13), channel_id=1, source_target_pairs={{0,4},{2,6},{4,0},{6,2},{8,12},{10,14},{12,8},{14,10},{1,5},{3,7},... | collective-permute-start | bytes 294920 | tf_op jit(solution)/shard_map/ppermute | solution.py:402
  10.5 2.4 %collective-permute-start.1 = (bf16[2,96,256]{2,1,0:T(8,128)(2,1)S(1)}, bf16[2,96,256]{2,1,0:T(8,128)(2,1)S(1)}, u32[]{:S(2)}, u32[]{:S(2)}) collective-permute-start(bf16[2,96,256]{2,1,0:T(8,128)(2,1)S(1)} %get-tuple-element.14), channel_id=1, source_target_pairs={{0,8},{2,10},{4,12},{6,14},{8,0},{10,2},{12,4},{14,6},{1,9},{3,11}... | collective-permute-start | bytes 294920 | tf_op jit(solution)/shard_map/ppermute | solution.py:402
  12.8 0.1 collective-permute-start.2
  12.9 2.5 %all-to-all-done.q_ref = bf16[8,8,512]{2,1,0:T(8,128)(2,1)S(1)} async-done(((bf16[8,8,512]{2,1,0:T(8,128)(2,1)}), bf16[8,8,512]{2,1,0:T(8,128)(2,1)S(1)}, u32[]{:S(2)}, u32[]{:S(2)}) %all-to-all-start) | async-done | bytes 65568 | tf_op jit(solution)/shard_map/all_to_all | solution.py:404
  15.5 0.0 copy-done
  15.5 0.0 copy-done.2
  15.5 0.0 copy-done.3
  15.5 2.5 %shard_map.97 = bf16[8,48,256]{2,1,0:T(8,128)(2,1)} custom-call(bf16[8,8,512]{2,1,0:T(8,128)(2,1)S(1)} %all-to-all-done.q_ref, s32[1,128]{1,0:T(1,128)} %bitcast.5, s32[1,128]{1,0:T(1,128)} %bitcast.6, bf16[1,1,64,32,256]{4,3,2,1,0:T(8,128)(2,1)} %stored_svalues.1, bf16[1,1024,256]{2,1,0:T(8,128)(2,1)S(1)} %copy-done.2, ...), custom_call_target="tpu_custom_call" | custom-call | flops 1073741824 | bytes 1048576 | tf_op jit(solution)/shard_map/pallas_call | solution.py:423
  18.0 3.4 %all-to-all-start.1 = ((bf16[8,48,256]{2,1,0:T(8,128)(2,1)}), bf16[8,48,256]{2,1,0:T(8,128)(2,1)S(1)}, u32[]{:S(2)}, u32[]{:S(2)}) async-start(bf16[8,48,256]{2,1,0:T(8,128)(2,1)} %shard_map.97), calls=%async_computation.1 | async-start | bytes 393216 | tf_op jit(solution)/shard_map/all_to_all | solution.py:445
  21.4 0.0 collective-permute-done.refs_1_
  21.4 0.0 collective-permute-done.1.refs_2_
  21.4 0.0 collective-permute-done.2.refs_3_
  21.4 2.1 %collective-permute-start.3 = (bf16[4,96,256]{2,1,0:T(8,128)(2,1)S(1)}, bf16[4,96,256]{2,1,0:T(8,128)(2,1)S(1)}, u32[]{:S(2)}, u32[]{:S(2)}) collective-permute-start(bf16[4,96,256]{2,1,0:T(8,128)(2,1)S(1)} %shard_map.98), channel_id=1, source_target_pairs={{0,2},{2,0},{4,6},{6,4},{8,10},{10,8},{12,14},{14,12},{1,3},{3,1},... | collective-permute-start | bytes 589832 | tf_op jit(solution)/shard_map/ppermute | solution.py:402
  23.5 4.9 %collective-permute-done.3.far_ref = bf16[4,96,256]{2,1,0:T(8,128)(2,1)S(1)} collective-permute-done((bf16[4,96,256]{2,1,0:T(8,128)(2,1)S(1)}, bf16[4,96,256]{2,1,0:T(8,128)(2,1)S(1)}, u32[]{:S(2)}, u32[]{:S(2)}) %collective-permute-start.3) | collective-permute-done | bytes 196640 | tf_op jit(solution)/shard_map/ppermute | solution.py:402
  28.4 0.8 %all-to-all-done.1.back_ref = bf16[8,48,256]{2,1,0:T(8,128)(2,1)S(1)} async-done(((bf16[8,48,256]{2,1,0:T(8,128)(2,1)}), bf16[8,48,256]{2,1,0:T(8,128)(2,1)S(1)}, u32[]{:S(2)}, u32[]{:S(2)}) %all-to-all-start.1) | async-done | bytes 196640 | tf_op jit(solution)/shard_map/all_to_all | solution.py:445
  29.2 1.0 %shard_map.99 = (bf16[2,1,8,64,256]{4,3,2,1,0:T(8,128)(2,1)}, bf16[8,4096]{1,0:T(8,128)(2,1)}) custom-call(bf16[8,48,256]{2,1,0:T(8,128)(2,1)S(1)} %all-to-all-done.1.back_ref, bf16[4,96,256]{2,1,0:T(8,128)(2,1)S(1)} %collective-permute-done.3.far_ref, bf16[2,96,256]{2,1,0:T(8,128)(2,1)S(1)} %get-tuple-element.12.refs_0_, ...), custom_call_target="tpu_custom_call" | custom-call | bytes 1048576 | tf_op jit(solution)/shard_map/pallas_call | solution.py:447
  (2 shorter events, 0.0 us)
Async XLA Ops:
  0.6 7.4 %copy-start.1 = (bf16[2,64,2048]{2,1,0:T(8,128)(2,1)S(1)}, bf16[2,64,2048]{2,1,0:T(8,128)(2,1)}, u32[]{:S(2)}) copy-start(bf16[2,64,2048]{2,1,0:T(8,128)(2,1)} %kv_ref.1) | copy-start | bytes 1572868
  0.7 14.8 %all-to-all-start = ((bf16[8,8,512]{2,1,0:T(8,128)(2,1)}), bf16[8,8,512]{2,1,0:T(8,128)(2,1)S(1)}, u32[]{:S(2)}, u32[]{:S(2)}) async-start(bf16[8,8,512]{2,1,0:T(8,128)(2,1)} %bitcast.1), calls=%async_computation | async-start | bytes 131072 | tf_op jit(solution)/shard_map/all_to_all | solution.py:404
  8.1 7.4 %copy-start = (bf16[1,1,64,32,256]{4,3,2,1,0:T(8,128)(2,1)S(1)}, bf16[1,1,64,32,256]{4,3,2,1,0:T(8,128)(2,1)}, u32[]{:S(2)}) copy-start(bf16[1,1,64,32,256]{4,3,2,1,0:T(8,128)(2,1)} %skeys_ref.1) | copy-start | bytes 3145732
  8.1 7.4 %copy-start.2 = (bf16[1,1024,256]{2,1,0:T(8,128)(2,1)S(1)}, bf16[1,1024,256]{2,1,0:T(8,128)(2,1)}, u32[]{:S(2)}) copy-start(bf16[1,1024,256]{2,1,0:T(8,128)(2,1)} %keys_ref.1) | copy-start | bytes 1572868
  8.1 7.4 %copy-start.3 = (bf16[1,1024,256]{2,1,0:T(8,128)(2,1)S(1)}, bf16[1,1024,256]{2,1,0:T(8,128)(2,1)}, u32[]{:S(2)}) copy-start(bf16[1,1024,256]{2,1,0:T(8,128)(2,1)} %values_ref.1) | copy-start | bytes 1572868
  8.4 13.0 %collective-permute-start = (bf16[2,96,256]{2,1,0:T(8,128)(2,1)S(1)}, bf16[2,96,256]{2,1,0:T(8,128)(2,1)S(1)}, u32[]{:S(2)}, u32[]{:S(2)}) collective-permute-start(bf16[2,96,256]{2,1,0:T(8,128)(2,1)S(1)} %get-tuple-element.13), channel_id=1, source_target_pairs={{0,4},{2,6},{4,0},{6,2},{8,12},{10,14},{12,8},{14,10},{1,5},{3,7},... | collective-permute-start | bytes 294920 | tf_op jit(solution)/shard_map/ppermute | solution.py:402
  10.5 10.9 %collective-permute-start.1 = (bf16[2,96,256]{2,1,0:T(8,128)(2,1)S(1)}, bf16[2,96,256]{2,1,0:T(8,128)(2,1)S(1)}, u32[]{:S(2)}, u32[]{:S(2)}) collective-permute-start(bf16[2,96,256]{2,1,0:T(8,128)(2,1)S(1)} %get-tuple-element.14), channel_id=1, source_target_pairs={{0,8},{2,10},{4,12},{6,14},{8,0},{10,2},{12,4},{14,6},{1,9},{3,11}... | collective-permute-start | bytes 294920 | tf_op jit(solution)/shard_map/ppermute | solution.py:402
  12.8 8.6 %collective-permute-start.2 = (bf16[2,96,256]{2,1,0:T(8,128)(2,1)S(1)}, bf16[2,96,256]{2,1,0:T(8,128)(2,1)S(1)}, u32[]{:S(2)}, u32[]{:S(2)}) collective-permute-start(bf16[2,96,256]{2,1,0:T(8,128)(2,1)S(1)} %get-tuple-element.15), channel_id=1, source_target_pairs={{0,12},{2,14},{4,8},{6,10},{8,4},{10,6},{12,0},{14,2},{1,13},{3,15... | collective-permute-start | bytes 294920 | tf_op jit(solution)/shard_map/ppermute | solution.py:402
  18.0 11.2 %all-to-all-start.1 = ((bf16[8,48,256]{2,1,0:T(8,128)(2,1)}), bf16[8,48,256]{2,1,0:T(8,128)(2,1)S(1)}, u32[]{:S(2)}, u32[]{:S(2)}) async-start(bf16[8,48,256]{2,1,0:T(8,128)(2,1)} %shard_map.97), calls=%async_computation.1 | async-start | bytes 393216 | tf_op jit(solution)/shard_map/all_to_all | solution.py:445
  21.4 6.9 %collective-permute-start.3 = (bf16[4,96,256]{2,1,0:T(8,128)(2,1)S(1)}, bf16[4,96,256]{2,1,0:T(8,128)(2,1)S(1)}, u32[]{:S(2)}, u32[]{:S(2)}) collective-permute-start(bf16[4,96,256]{2,1,0:T(8,128)(2,1)S(1)} %shard_map.98), channel_id=1, source_target_pairs={{0,2},{2,0},{4,6},{6,4},{8,10},{10,8},{12,14},{14,12},{1,3},{3,1},... | collective-permute-start | bytes 589832 | tf_op jit(solution)/shard_map/ppermute | solution.py:402

commit v7 on v6

--- a/solution.py
+++ b/solution.py
@@ -342,41 +342,45 @@
     )(*(pin(piece) for piece in pieces))
 
 
-def finish_kernel(count, back_ref, far_ref, *refs):
-    *near, cache_ref, stored_attention, attention_ref, sems = refs
+def cache_kernel(count, far_ref, *refs):
+    *near, cache_ref, sems = refs
     place = lax.axis_index("seq")
     rows = cache_ref.shape[3]
-    request_rows = attention_ref.shape[0]
-    width = back_ref.shape[2]
-    parts = attention_ref.shape[1] // (count * width)
-    riding = back_ref.shape[1] - parts * request_rows
+    kept = far_ref.shape[1] - rows
     copies = []
     for j in range(count // 2):
         for d, piece in ((0, near[j].at[0]), (1, far_ref.at[j])):
             source = jnp.bitwise_xor(place, 2 * j + d)
             copies += [
                 pltpu.make_async_copy(piece.at[:rows], cache_ref.at[0, 0, source], sems.at[2 * j + d, 0]),
-                pltpu.make_async_copy(
-                    piece.at[rows:], cache_ref.at[1, 0, source, : rows - riding], sems.at[2 * j + d, 1]
-                ),
+                pltpu.make_async_copy(piece.at[rows:], cache_ref.at[1, 0, source, :kept], sems.at[2 * j + d, 1]),
             ]
-    copies.append(
-        pltpu.make_async_copy(
-            back_ref.at[:, parts * request_rows :], cache_ref.at[1, 0, :, rows - riding :], sems.at[0, 2]
-        )
-    )
     for copy in copies:
         copy.start()
-    copies.append(pltpu.make_async_copy(attention_ref, stored_attention, sems.at[1, 2]))
+    for copy in copies:
+        copy.wait()
+
+
+def finish_kernel(back_ref, _, cache_ref, stored_attention, attention_ref, sems):
+    count, packed, width = back_ref.shape
+    rows = cache_ref.shape[3]
+    request_rows = attention_ref.shape[0]
+    parts = attention_ref.shape[1] // (count * width)
+    kept = rows - (packed - parts * request_rows)
+    ride = pltpu.make_async_copy(
+        back_ref.at[:, parts * request_rows :], cache_ref.at[1, 0, :, kept:], sems.at[0]
+    )
+    ride.start()
     for s in range(count):
         block = back_ref[s, : parts * request_rows].astype(jnp.float32)
         for t in range(parts):
             attention_ref[:, (s * parts + t) * width : (s * parts + t + 1) * width] = block[
                 t * request_rows : (t + 1) * request_rows
             ].astype(jnp.bfloat16)
-    copies[-1].start()
-    for copy in copies:
-        copy.wait()
+    out = pltpu.make_async_copy(attention_ref, stored_attention, sems.at[1])
+    out.start()
+    ride.wait()
+    out.wait()
 
 
 def local(new_kv, old_keys, old_values, suffix_keys, suffix_values, queries, lengths, assign):
@@ -443,21 +447,31 @@
     )
     kv_far = swap(forward(kv_near), 1)
     back = lax.all_to_all(attended, "seq", 0, 0, tiled=True)
+    cache_shape = (2, 1, seq_count, prefix_rows, width)
+    cache = pl.pallas_call(
+        functools.partial(cache_kernel, seq_count),
+        out_shape=pltpu.HBM(cache_shape, jnp.bfloat16),
+        in_specs=[VMEM] * (half + 1),
+        out_specs=HBM,
+        scratch_shapes=[pltpu.SemaphoreType.DMA((seq_count, 2))],
+        cost_estimate=pl.CostEstimate(flops=2**30, bytes_accessed=2**20, transcendentals=0),
+    )(*(pin(x) for x in (kv_far, *kv_near)))
     return tuple(
         pl.pallas_call(
-            functools.partial(finish_kernel, seq_count),
+            finish_kernel,
             out_shape=(
-                jax.ShapeDtypeStruct((2, 1, seq_count, prefix_rows, width), jnp.bfloat16),
-                jax.ShapeDtypeStruct((request_rows, NQH * HD), jnp.bfloat16),
+                pltpu.HBM(cache_shape, jnp.bfloat16),
+                pltpu.HBM((request_rows, NQH * HD), jnp.bfloat16),
             ),
-            in_specs=[VMEM] * (half + 2),
+            in_specs=[VMEM, HBM],
             out_specs=(HBM, HBM),
             scratch_shapes=[
                 pltpu.VMEM((request_rows, NQH * HD), jnp.bfloat16),
-                pltpu.SemaphoreType.DMA((seq_count, 3)),
+                pltpu.SemaphoreType.DMA((2,)),
             ],
+            input_output_aliases={1: 0},
             cost_estimate=pl.CostEstimate(flops=0, bytes_accessed=2**20, transcendentals=0),
-        )(*(pin(x) for x in (back, kv_far, *kv_near)))
+        )(pin(back), cache)
     )
 
 

time: 30.5 us -> 30.3 us (level)
  waiting for transfers between devices: 8.21 us -> 7.44 us
  Pallas kernels: 3.84 us -> 4.39 us
    all_to_all x1, waiting for transfers between devices: 0.78 us -> 0.01 us  [local(): back = lax.all_to_all(attended, 'seq', 0, 0, tiled=True)]
    pallas_call x1 -> x2, Pallas kernels: 1.02 us -> 1.56 us  [the longest x1 0.87 us: local(): pl.pallas_call(functools.partial(cache_kernel, seq_count), out_shape=pltp...]
  transfers between devices with their start and end apart: 6 -> 6, of which waited for: 3 -> 2; matrix products, arithmetic and copies ran while one was open for 0% -> 0% of each run, Pallas kernels for 9% -> 12%
where the time goes in v7:
time: 30.3 us; the launch traced here: 30 us
  starting transfers between devices  17.4 us (57%)
  waiting for transfers between devices  7.44 us (25%)
  Pallas kernels  4.39 us (14%)
  between operations  0.75 us (2%)
    all_to_all x1, starting transfers between devices, local(): lax.all_to_all(queries.reshape(request_rows, seq_count, group_width).tran...  7.4 us
    ppermute x4, starting transfers between devices, swap(): return lax.ppermute(x, 'seq', [(i, i ^ k) for i in range(seq_count)])  6.57 us
    ppermute x4, waiting for transfers between devices, swap(): return lax.ppermute(x, 'seq', [(i, i ^ k) for i in range(seq_count)])  4.88 us
    all_to_all x1, starting transfers between devices, local(): back = lax.all_to_all(attended, 'seq', 0, 0, tiled=True)  3.4 us
    all_to_all x1, waiting for transfers between devices, local(): lax.all_to_all(queries.reshape(request_rows, seq_count, group_width).tran...  2.55 us
    pallas_call x1, Pallas kernels, local(): pl.pallas_call(functools.partial(attend_kernel, core_count), out_shape=pl...  2.51 us
    pallas_call x1, Pallas kernels, local(): pl.pallas_call(functools.partial(cache_kernel, seq_count), out_shape=pltp...  0.87 us
    pallas_call x1, Pallas kernels, local(): pl.pallas_call(finish_kernel, out_shape=(pltpu.HBM(cache_shape, jnp.bfloa...  0.7 us
  transfers between devices with their start and end apart: 6, of which 2 were waited for; matrix products, arithmetic and copies ran while one was open for 0% of the time, Pallas kernels for 12%

profile of v7, /device:TPU:0, one launch (start us, length us, event | category | flops | bytes accessed | tf_op | source)
XLA Modules:
  0.0 30.0 jit_solution(18334007826528562961)
XLA Ops:
  0.6 0.0 copy-start.1
  0.7 7.4 %all-to-all-start = ((bf16[8,8,512]{2,1,0:T(8,128)(2,1)}), bf16[8,8,512]{2,1,0:T(8,128)(2,1)S(1)}, u32[]{:S(2)}, u32[]{:S(2)}) async-start(bf16[8,8,512]{2,1,0:T(8,128)(2,1)} %bitcast.1), calls=%async_computation | async-start | bytes 131072 | tf_op jit(solution)/shard_map/all_to_all | solution.py:408
  8.0 0.0 copy-done.1
  8.1 0.0 copy-start
  8.1 0.0 copy-start.2
  8.1 0.0 copy-start.3
  8.1 0.3 shard_map.96
  8.4 2.1 %collective-permute-start = (bf16[2,96,256]{2,1,0:T(8,128)(2,1)S(1)}, bf16[2,96,256]{2,1,0:T(8,128)(2,1)S(1)}, u32[]{:S(2)}, u32[]{:S(2)}) collective-permute-start(bf16[2,96,256]{2,1,0:T(8,128)(2,1)S(1)} %get-tuple-element.13), channel_id=1, source_target_pairs={{0,4},{2,6},{4,0},{6,2},{8,12},{10,14},{12,8},{14,10},{1,5},{3,7},... | collective-permute-start | bytes 294920 | tf_op jit(solution)/shard_map/ppermute | solution.py:406
  10.5 2.4 %collective-permute-start.1 = (bf16[2,96,256]{2,1,0:T(8,128)(2,1)S(1)}, bf16[2,96,256]{2,1,0:T(8,128)(2,1)S(1)}, u32[]{:S(2)}, u32[]{:S(2)}) collective-permute-start(bf16[2,96,256]{2,1,0:T(8,128)(2,1)S(1)} %get-tuple-element.14), channel_id=1, source_target_pairs={{0,8},{2,10},{4,12},{6,14},{8,0},{10,2},{12,4},{14,6},{1,9},{3,11}... | collective-permute-start | bytes 294920 | tf_op jit(solution)/shard_map/ppermute | solution.py:406
  12.8 0.1 collective-permute-start.2
  12.9 2.5 %all-to-all-done.q_ref = bf16[8,8,512]{2,1,0:T(8,128)(2,1)S(1)} async-done(((bf16[8,8,512]{2,1,0:T(8,128)(2,1)}), bf16[8,8,512]{2,1,0:T(8,128)(2,1)S(1)}, u32[]{:S(2)}, u32[]{:S(2)}) %all-to-all-start) | async-done | bytes 65568 | tf_op jit(solution)/shard_map/all_to_all | solution.py:408
  15.5 0.0 copy-done
  15.5 0.0 copy-done.2
  15.5 0.0 copy-done.3
  15.5 2.5 %shard_map.97 = bf16[8,48,256]{2,1,0:T(8,128)(2,1)} custom-call(bf16[8,8,512]{2,1,0:T(8,128)(2,1)S(1)} %all-to-all-done.q_ref, s32[1,128]{1,0:T(1,128)} %bitcast.5, s32[1,128]{1,0:T(1,128)} %bitcast.6, bf16[1,1,64,32,256]{4,3,2,1,0:T(8,128)(2,1)} %stored_svalues.1, bf16[1,1024,256]{2,1,0:T(8,128)(2,1)S(1)} %copy-done.2, ...), custom_call_target="tpu_custom_call" | custom-call | flops 1073741824 | bytes 1048576 | tf_op jit(solution)/shard_map/pallas_call | solution.py:427
  18.0 3.4 %all-to-all-start.1 = ((bf16[8,48,256]{2,1,0:T(8,128)(2,1)}), bf16[8,48,256]{2,1,0:T(8,128)(2,1)S(1)}, u32[]{:S(2)}, u32[]{:S(2)}) async-start(bf16[8,48,256]{2,1,0:T(8,128)(2,1)} %shard_map.97), calls=%async_computation.1 | async-start | bytes 393216 | tf_op jit(solution)/shard_map/all_to_all | solution.py:449
  21.4 0.0 collective-permute-done.refs_1_
  21.4 0.0 collective-permute-done.1.refs_2_
  21.4 0.0 collective-permute-done.2.refs_3_
  21.4 2.1 %collective-permute-start.3 = (bf16[4,96,256]{2,1,0:T(8,128)(2,1)S(1)}, bf16[4,96,256]{2,1,0:T(8,128)(2,1)S(1)}, u32[]{:S(2)}, u32[]{:S(2)}) collective-permute-start(bf16[4,96,256]{2,1,0:T(8,128)(2,1)S(1)} %shard_map.98), channel_id=1, source_target_pairs={{0,2},{2,0},{4,6},{6,4},{8,10},{10,8},{12,14},{14,12},{1,3},{3,1},... | collective-permute-start | bytes 589832 | tf_op jit(solution)/shard_map/ppermute | solution.py:406
  23.5 4.9 %collective-permute-done.3.far_ref = bf16[4,96,256]{2,1,0:T(8,128)(2,1)S(1)} collective-permute-done((bf16[4,96,256]{2,1,0:T(8,128)(2,1)S(1)}, bf16[4,96,256]{2,1,0:T(8,128)(2,1)S(1)}, u32[]{:S(2)}, u32[]{:S(2)}) %collective-permute-start.3) | collective-permute-done | bytes 196640 | tf_op jit(solution)/shard_map/ppermute | solution.py:406
  28.4 0.9 %shard_map.99._ = bf16[2,1,8,64,256]{4,3,2,1,0:T(8,128)(2,1)} custom-call(bf16[4,96,256]{2,1,0:T(8,128)(2,1)S(1)} %collective-permute-done.3.far_ref, bf16[2,96,256]{2,1,0:T(8,128)(2,1)S(1)} %get-tuple-element.12.refs_0_, bf16[2,96,256]{2,1,0:T(8,128)(2,1)S(1)} %collective-permute-done.refs_1_, bf16[2,96,256]{2,1,0:T(8,128)(2,1)S(1)} %collective-permute-done.1.refs_2_, ...), custom_call_target="tpu_custom_call" | custom-call | flops 1073741824 | bytes 1048576 | tf_op jit(solution)/shard_map/pallas_call | solution.py:451
  29.3 0.0 all-to-all-done.1.back_ref
  29.3 0.7 %shard_map.100 = (bf16[2,1,8,64,256]{4,3,2,1,0:T(8,128)(2,1)}, bf16[8,4096]{1,0:T(8,128)(2,1)}) custom-call(bf16[8,48,256]{2,1,0:T(8,128)(2,1)S(1)} %all-to-all-done.1.back_ref, bf16[2,1,8,64,256]{4,3,2,1,0:T(8,128)(2,1)} %shard_map.99._), custom_call_target="tpu_custom_call", output_to_operand_aliasing={{0}: (1, {})} | custom-call | bytes 1048576 | tf_op jit(solution)/shard_map/pallas_call | solution.py:460
  (2 shorter events, 0.0 us)
Async XLA Ops:
  0.6 7.4 %copy-start.1 = (bf16[2,64,2048]{2,1,0:T(8,128)(2,1)S(1)}, bf16[2,64,2048]{2,1,0:T(8,128)(2,1)}, u32[]{:S(2)}) copy-start(bf16[2,64,2048]{2,1,0:T(8,128)(2,1)} %kv_ref.1) | copy-start | bytes 1572868
  0.7 14.8 %all-to-all-start = ((bf16[8,8,512]{2,1,0:T(8,128)(2,1)}), bf16[8,8,512]{2,1,0:T(8,128)(2,1)S(1)}, u32[]{:S(2)}, u32[]{:S(2)}) async-start(bf16[8,8,512]{2,1,0:T(8,128)(2,1)} %bitcast.1), calls=%async_computation | async-start | bytes 131072 | tf_op jit(solution)/shard_map/all_to_all | solution.py:408
  8.1 7.4 %copy-start = (bf16[1,1,64,32,256]{4,3,2,1,0:T(8,128)(2,1)S(1)}, bf16[1,1,64,32,256]{4,3,2,1,0:T(8,128)(2,1)}, u32[]{:S(2)}) copy-start(bf16[1,1,64,32,256]{4,3,2,1,0:T(8,128)(2,1)} %skeys_ref.1) | copy-start | bytes 3145732
  8.1 7.4 %copy-start.2 = (bf16[1,1024,256]{2,1,0:T(8,128)(2,1)S(1)}, bf16[1,1024,256]{2,1,0:T(8,128)(2,1)}, u32[]{:S(2)}) copy-start(bf16[1,1024,256]{2,1,0:T(8,128)(2,1)} %keys_ref.1) | copy-start | bytes 1572868
  8.1 7.4 %copy-start.3 = (bf16[1,1024,256]{2,1,0:T(8,128)(2,1)S(1)}, bf16[1,1024,256]{2,1,0:T(8,128)(2,1)}, u32[]{:S(2)}) copy-start(bf16[1,1024,256]{2,1,0:T(8,128)(2,1)} %values_ref.1) | copy-start | bytes 1572868
  8.4 13.0 %collective-permute-start = (bf16[2,96,256]{2,1,0:T(8,128)(2,1)S(1)}, bf16[2,96,256]{2,1,0:T(8,128)(2,1)S(1)}, u32[]{:S(2)}, u32[]{:S(2)}) collective-permute-start(bf16[2,96,256]{2,1,0:T(8,128)(2,1)S(1)} %get-tuple-element.13), channel_id=1, source_target_pairs={{0,4},{2,6},{4,0},{6,2},{8,12},{10,14},{12,8},{14,10},{1,5},{3,7},... | collective-permute-start | bytes 294920 | tf_op jit(solution)/shard_map/ppermute | solution.py:406
  10.5 10.9 %collective-permute-start.1 = (bf16[2,96,256]{2,1,0:T(8,128)(2,1)S(1)}, bf16[2,96,256]{2,1,0:T(8,128)(2,1)S(1)}, u32[]{:S(2)}, u32[]{:S(2)}) collective-permute-start(bf16[2,96,256]{2,1,0:T(8,128)(2,1)S(1)} %get-tuple-element.14), channel_id=1, source_target_pairs={{0,8},{2,10},{4,12},{6,14},{8,0},{10,2},{12,4},{14,6},{1,9},{3,11}... | collective-permute-start | bytes 294920 | tf_op jit(solution)/shard_map/ppermute | solution.py:406
  12.8 8.6 %collective-permute-start.2 = (bf16[2,96,256]{2,1,0:T(8,128)(2,1)S(1)}, bf16[2,96,256]{2,1,0:T(8,128)(2,1)S(1)}, u32[]{:S(2)}, u32[]{:S(2)}) collective-permute-start(bf16[2,96,256]{2,1,0:T(8,128)(2,1)S(1)} %get-tuple-element.15), channel_id=1, source_target_pairs={{0,12},{2,14},{4,8},{6,10},{8,4},{10,6},{12,0},{14,2},{1,13},{3,15... | collective-permute-start | bytes 294920 | tf_op jit(solution)/shard_map/ppermute | solution.py:406
  18.0 11.3 %all-to-all-start.1 = ((bf16[8,48,256]{2,1,0:T(8,128)(2,1)}), bf16[8,48,256]{2,1,0:T(8,128)(2,1)S(1)}, u32[]{:S(2)}, u32[]{:S(2)}) async-start(bf16[8,48,256]{2,1,0:T(8,128)(2,1)} %shard_map.97), calls=%async_computation.1 | async-start | bytes 393216 | tf_op jit(solution)/shard_map/all_to_all | solution.py:449
  21.4 6.9 %collective-permute-start.3 = (bf16[4,96,256]{2,1,0:T(8,128)(2,1)S(1)}, bf16[4,96,256]{2,1,0:T(8,128)(2,1)S(1)}, u32[]{:S(2)}, u32[]{:S(2)}) collective-permute-start(bf16[4,96,256]{2,1,0:T(8,128)(2,1)S(1)} %shard_map.98), channel_id=1, source_target_pairs={{0,2},{2,0},{4,6},{6,4},{8,10},{10,8},{12,14},{14,12},{1,3},{3,1},... | collective-permute-start | bytes 589832 | tf_op jit(solution)/shard_map/ppermute | solution.py:406

commit v8 on v7

--- a/solution.py
+++ b/solution.py
@@ -342,23 +342,34 @@
     )(*(pin(piece) for piece in pieces))
 
 
-def cache_kernel(count, far_ref, *refs):
-    *near, cache_ref, sems = refs
-    place = lax.axis_index("seq")
+def place_blocks(blocks, cache_ref, sems):
     rows = cache_ref.shape[3]
-    kept = far_ref.shape[1] - rows
     copies = []
-    for j in range(count // 2):
-        for d, piece in ((0, near[j].at[0]), (1, far_ref.at[j])):
-            source = jnp.bitwise_xor(place, 2 * j + d)
-            copies += [
-                pltpu.make_async_copy(piece.at[:rows], cache_ref.at[0, 0, source], sems.at[2 * j + d, 0]),
-                pltpu.make_async_copy(piece.at[rows:], cache_ref.at[1, 0, source, :kept], sems.at[2 * j + d, 1]),
-            ]
+    for i, (source, piece) in enumerate(blocks):
+        kept = piece.shape[0] - rows
+        copies += [
+            pltpu.make_async_copy(piece.at[:rows], cache_ref.at[0, 0, source], sems.at[i, 0]),
+            pltpu.make_async_copy(piece.at[rows:], cache_ref.at[1, 0, source, :kept], sems.at[i, 1]),
+        ]
     for copy in copies:
         copy.start()
     for copy in copies:
         copy.wait()
+
+
+def near_kernel(count, *refs):
+    *near, cache_ref, sems = refs
+    place = lax.axis_index("seq")
+    place_blocks(
+        [(jnp.bitwise_xor(place, 2 * j), near[i].at[0]) for i, j in enumerate(range(count // 2))], cache_ref, sems
+    )
+
+
+def far_kernel(count, far_ref, _, cache_ref, sems):
+    place = lax.axis_index("seq")
+    place_blocks(
+        [(jnp.bitwise_xor(place, 2 * j + 1), far_ref.at[j]) for j in range(count // 2)], cache_ref, sems
+    )
 
 
 def finish_kernel(back_ref, _, cache_ref, stored_attention, attention_ref, sems):
@@ -449,13 +460,22 @@
     back = lax.all_to_all(attended, "seq", 0, 0, tiled=True)
     cache_shape = (2, 1, seq_count, prefix_rows, width)
     cache = pl.pallas_call(
-        functools.partial(cache_kernel, seq_count),
+        functools.partial(near_kernel, seq_count),
         out_shape=pltpu.HBM(cache_shape, jnp.bfloat16),
-        in_specs=[VMEM] * (half + 1),
+        in_specs=[VMEM] * half,
         out_specs=HBM,
-        scratch_shapes=[pltpu.SemaphoreType.DMA((seq_count, 2))],
+        scratch_shapes=[pltpu.SemaphoreType.DMA((half, 2))],
         cost_estimate=pl.CostEstimate(flops=2**30, bytes_accessed=2**20, transcendentals=0),
-    )(*(pin(x) for x in (kv_far, *kv_near)))
+    )(*(pin(x) for x in kv_near))
+    cache = pl.pallas_call(
+        functools.partial(far_kernel, seq_count),
+        out_shape=pltpu.HBM(cache_shape, jnp.bfloat16),
+        in_specs=[VMEM, HBM],
+        out_specs=HBM,
+        scratch_shapes=[pltpu.SemaphoreType.DMA((half, 2))],
+        input_output_aliases={1: 0},
+        cost_estimate=pl.CostEstimate(flops=2**30, bytes_accessed=2**20, transcendentals=0),
+    )(pin(kv_far), cache)
     return tuple(
         pl.pallas_call(
             finish_kernel,

time: 30.3 us -> 30.2 us (level)
  waiting for transfers between devices: 7.44 us -> 6.73 us
  Pallas kernels: 4.39 us -> 4.98 us
    ppermute x4, waiting for transfers between devices: 4.88 us -> 4.14 us  [swap(): return lax.ppermute(x, 'seq', [(i, i ^ k) for i in range(seq_count)])]
    pallas_call x1 -> x2, Pallas kernels: 0.87 us -> 1.47 us  [the longest x1 0.73 us: local(): pl.pallas_call(functools.partial(far_kernel, seq_count), out_shape=pltpu....]
  transfers between devices with their start and end apart: 6 -> 6, of which waited for: 2 -> 2; matrix products, arithmetic and copies ran while one was open for 0% -> 0% of each run, Pallas kernels for 12% -> 14%
where the time goes in v8:
time: 30.2 us; the launch traced here: 29.9 us
  starting transfers between devices  17.4 us (58%)
  waiting for transfers between devices  6.73 us (22%)
  Pallas kernels  4.98 us (16%)
  between operations  0.75 us (2%)
    all_to_all x1, starting transfers between devices, local(): lax.all_to_all(queries.reshape(request_rows, seq_count, group_width).tran...  7.4 us
    ppermute x4, starting transfers between devices, swap(): return lax.ppermute(x, 'seq', [(i, i ^ k) for i in range(seq_count)])  6.57 us
    ppermute x4, waiting for transfers between devices, swap(): return lax.ppermute(x, 'seq', [(i, i ^ k) for i in range(seq_count)])  4.14 us
    all_to_all x1, starting transfers between devices, local(): back = lax.all_to_all(attended, 'seq', 0, 0, tiled=True)  3.4 us
    all_to_all x1, waiting for transfers between devices, local(): lax.all_to_all(queries.reshape(request_rows, seq_count, group_width).tran...  2.55 us
    pallas_call x1, Pallas kernels, local(): pl.pallas_call(functools.partial(attend_kernel, core_count), out_shape=pl...  2.51 us
    pallas_call x1, Pallas kernels, local(): pl.pallas_call(functools.partial(far_kernel, seq_count), out_shape=pltpu....  0.73 us
    pallas_call x1, Pallas kernels, local(): pl.pallas_call(functools.partial(near_kernel, seq_count), out_shape=pltpu...  0.73 us
  transfers between devices with their start and end apart: 6, of which 2 were waited for; matrix products, arithmetic and copies ran while one was open for 0% of the time, Pallas kernels for 14%

profile of v8, /device:TPU:0, one launch (start us, length us, event | category | flops | bytes accessed | tf_op | source)
XLA Modules:
  0.0 29.9 jit_solution(5741620061289967809)
XLA Ops:
  0.6 0.0 copy-start.1
  0.7 7.4 %all-to-all-start = ((bf16[8,8,512]{2,1,0:T(8,128)(2,1)}), bf16[8,8,512]{2,1,0:T(8,128)(2,1)S(1)}, u32[]{:S(2)}, u32[]{:S(2)}) async-start(bf16[8,8,512]{2,1,0:T(8,128)(2,1)} %bitcast.1), calls=%async_computation | async-start | bytes 131072 | tf_op jit(solution)/shard_map/all_to_all | solution.py:419
  8.0 0.0 copy-done.1
  8.1 0.0 copy-start
  8.1 0.0 copy-start.2
  8.1 0.0 copy-start.3
  8.1 0.3 shard_map.96
  8.4 2.1 %collective-permute-start = (bf16[2,96,256]{2,1,0:T(8,128)(2,1)S(1)}, bf16[2,96,256]{2,1,0:T(8,128)(2,1)S(1)}, u32[]{:S(2)}, u32[]{:S(2)}) collective-permute-start(bf16[2,96,256]{2,1,0:T(8,128)(2,1)S(1)} %get-tuple-element.13), channel_id=1, source_target_pairs={{0,4},{2,6},{4,0},{6,2},{8,12},{10,14},{12,8},{14,10},{1,5},{3,7},... | collective-permute-start | bytes 294920 | tf_op jit(solution)/shard_map/ppermute | solution.py:417
  10.5 2.4 %collective-permute-start.1 = (bf16[2,96,256]{2,1,0:T(8,128)(2,1)S(1)}, bf16[2,96,256]{2,1,0:T(8,128)(2,1)S(1)}, u32[]{:S(2)}, u32[]{:S(2)}) collective-permute-start(bf16[2,96,256]{2,1,0:T(8,128)(2,1)S(1)} %get-tuple-element.14), channel_id=1, source_target_pairs={{0,8},{2,10},{4,12},{6,14},{8,0},{10,2},{12,4},{14,6},{1,9},{3,11}... | collective-permute-start | bytes 294920 | tf_op jit(solution)/shard_map/ppermute | solution.py:417
  12.8 0.1 collective-permute-start.2
  12.9 2.5 %all-to-all-done.q_ref = bf16[8,8,512]{2,1,0:T(8,128)(2,1)S(1)} async-done(((bf16[8,8,512]{2,1,0:T(8,128)(2,1)}), bf16[8,8,512]{2,1,0:T(8,128)(2,1)S(1)}, u32[]{:S(2)}, u32[]{:S(2)}) %all-to-all-start) | async-done | bytes 65568 | tf_op jit(solution)/shard_map/all_to_all | solution.py:419
  15.5 0.0 copy-done
  15.5 0.0 copy-done.2
  15.5 0.0 copy-done.3
  15.5 2.5 %shard_map.97 = bf16[8,48,256]{2,1,0:T(8,128)(2,1)} custom-call(bf16[8,8,512]{2,1,0:T(8,128)(2,1)S(1)} %all-to-all-done.q_ref, s32[1,128]{1,0:T(1,128)} %bitcast.5, s32[1,128]{1,0:T(1,128)} %bitcast.6, bf16[1,1,64,32,256]{4,3,2,1,0:T(8,128)(2,1)} %stored_svalues.1, bf16[1,1024,256]{2,1,0:T(8,128)(2,1)S(1)} %copy-done.2, ...), custom_call_target="tpu_custom_call" | custom-call | flops 1073741824 | bytes 1048576 | tf_op jit(solution)/shard_map/pallas_call | solution.py:438
  18.0 3.4 %all-to-all-start.1 = ((bf16[8,48,256]{2,1,0:T(8,128)(2,1)}), bf16[8,48,256]{2,1,0:T(8,128)(2,1)S(1)}, u32[]{:S(2)}, u32[]{:S(2)}) async-start(bf16[8,48,256]{2,1,0:T(8,128)(2,1)} %shard_map.97), calls=%async_computation.1 | async-start | bytes 393216 | tf_op jit(solution)/shard_map/all_to_all | solution.py:460
  21.4 0.0 collective-permute-done.refs_1_
  21.4 0.0 collective-permute-done.1.refs_2_
  21.4 0.0 collective-permute-done.2.refs_3_
  21.4 2.1 %collective-permute-start.3 = (bf16[4,96,256]{2,1,0:T(8,128)(2,1)S(1)}, bf16[4,96,256]{2,1,0:T(8,128)(2,1)S(1)}, u32[]{:S(2)}, u32[]{:S(2)}) collective-permute-start(bf16[4,96,256]{2,1,0:T(8,128)(2,1)S(1)} %shard_map.98), channel_id=1, source_target_pairs={{0,2},{2,0},{4,6},{6,4},{8,10},{10,8},{12,14},{14,12},{1,3},{3,1},... | collective-permute-start | bytes 589832 | tf_op jit(solution)/shard_map/ppermute | solution.py:417
  23.5 0.7 %shard_map.99._ = bf16[2,1,8,64,256]{4,3,2,1,0:T(8,128)(2,1)} custom-call(bf16[2,96,256]{2,1,0:T(8,128)(2,1)S(1)} %get-tuple-element.12.refs_0_, bf16[2,96,256]{2,1,0:T(8,128)(2,1)S(1)} %collective-permute-done.refs_1_, bf16[2,96,256]{2,1,0:T(8,128)(2,1)S(1)} %collective-permute-done.1.refs_2_, bf16[2,96,256]{2,1,0:T(8,128)(2,1)S(1)} %collective-permute-done.2.refs_3_), custom_call_target="tpu_custom_call" | custom-call | flops 1073741824 | bytes 1048576 | tf_op jit(solution)/shard_map/pallas_call | solution.py:462
  24.2 4.1 %collective-permute-done.3.far_ref = bf16[4,96,256]{2,1,0:T(8,128)(2,1)S(1)} collective-permute-done((bf16[4,96,256]{2,1,0:T(8,128)(2,1)S(1)}, bf16[4,96,256]{2,1,0:T(8,128)(2,1)S(1)}, u32[]{:S(2)}, u32[]{:S(2)}) %collective-permute-start.3) | collective-permute-done | bytes 196640 | tf_op jit(solution)/shard_map/ppermute | solution.py:417
  28.4 0.7 %shard_map.100._ = bf16[2,1,8,64,256]{4,3,2,1,0:T(8,128)(2,1)} custom-call(bf16[4,96,256]{2,1,0:T(8,128)(2,1)S(1)} %collective-permute-done.3.far_ref, bf16[2,1,8,64,256]{4,3,2,1,0:T(8,128)(2,1)} %shard_map.99._), custom_call_target="tpu_custom_call", output_to_operand_aliasing={{}: (1, {})} | custom-call | flops 1073741824 | bytes 1048576 | tf_op jit(solution)/shard_map/pallas_call | solution.py:470
  29.1 0.0 all-to-all-done.1.back_ref
  29.2 0.7 %shard_map.101 = (bf16[2,1,8,64,256]{4,3,2,1,0:T(8,128)(2,1)}, bf16[8,4096]{1,0:T(8,128)(2,1)}) custom-call(bf16[8,48,256]{2,1,0:T(8,128)(2,1)S(1)} %all-to-all-done.1.back_ref, bf16[2,1,8,64,256]{4,3,2,1,0:T(8,128)(2,1)} %shard_map.100._), custom_call_target="tpu_custom_call", output_to_operand_aliasing={{0}: (1, {})} | custom-call | bytes 1048576 | tf_op jit(solution)/shard_map/pallas_call | solution.py:480
  (2 shorter events, 0.0 us)
Async XLA Ops:
  0.6 7.4 %copy-start.1 = (bf16[2,64,2048]{2,1,0:T(8,128)(2,1)S(1)}, bf16[2,64,2048]{2,1,0:T(8,128)(2,1)}, u32[]{:S(2)}) copy-start(bf16[2,64,2048]{2,1,0:T(8,128)(2,1)} %kv_ref.1) | copy-start | bytes 1572868
  0.7 14.8 %all-to-all-start = ((bf16[8,8,512]{2,1,0:T(8,128)(2,1)}), bf16[8,8,512]{2,1,0:T(8,128)(2,1)S(1)}, u32[]{:S(2)}, u32[]{:S(2)}) async-start(bf16[8,8,512]{2,1,0:T(8,128)(2,1)} %bitcast.1), calls=%async_computation | async-start | bytes 131072 | tf_op jit(solution)/shard_map/all_to_all | solution.py:419
  8.1 7.4 %copy-start = (bf16[1,1,64,32,256]{4,3,2,1,0:T(8,128)(2,1)S(1)}, bf16[1,1,64,32,256]{4,3,2,1,0:T(8,128)(2,1)}, u32[]{:S(2)}) copy-start(bf16[1,1,64,32,256]{4,3,2,1,0:T(8,128)(2,1)} %skeys_ref.1) | copy-start | bytes 3145732
  8.1 7.4 %copy-start.2 = (bf16[1,1024,256]{2,1,0:T(8,128)(2,1)S(1)}, bf16[1,1024,256]{2,1,0:T(8,128)(2,1)}, u32[]{:S(2)}) copy-start(bf16[1,1024,256]{2,1,0:T(8,128)(2,1)} %keys_ref.1) | copy-start | bytes 1572868
  8.1 7.4 %copy-start.3 = (bf16[1,1024,256]{2,1,0:T(8,128)(2,1)S(1)}, bf16[1,1024,256]{2,1,0:T(8,128)(2,1)}, u32[]{:S(2)}) copy-start(bf16[1,1024,256]{2,1,0:T(8,128)(2,1)} %values_ref.1) | copy-start | bytes 1572868
  8.4 13.0 %collective-permute-start = (bf16[2,96,256]{2,1,0:T(8,128)(2,1)S(1)}, bf16[2,96,256]{2,1,0:T(8,128)(2,1)S(1)}, u32[]{:S(2)}, u32[]{:S(2)}) collective-permute-start(bf16[2,96,256]{2,1,0:T(8,128)(2,1)S(1)} %get-tuple-element.13), channel_id=1, source_target_pairs={{0,4},{2,6},{4,0},{6,2},{8,12},{10,14},{12,8},{14,10},{1,5},{3,7},... | collective-permute-start | bytes 294920 | tf_op jit(solution)/shard_map/ppermute | solution.py:417
  10.5 10.9 %collective-permute-start.1 = (bf16[2,96,256]{2,1,0:T(8,128)(2,1)S(1)}, bf16[2,96,256]{2,1,0:T(8,128)(2,1)S(1)}, u32[]{:S(2)}, u32[]{:S(2)}) collective-permute-start(bf16[2,96,256]{2,1,0:T(8,128)(2,1)S(1)} %get-tuple-element.14), channel_id=1, source_target_pairs={{0,8},{2,10},{4,12},{6,14},{8,0},{10,2},{12,4},{14,6},{1,9},{3,11}... | collective-permute-start | bytes 294920 | tf_op jit(solution)/shard_map/ppermute | solution.py:417
  12.8 8.6 %collective-permute-start.2 = (bf16[2,96,256]{2,1,0:T(8,128)(2,1)S(1)}, bf16[2,96,256]{2,1,0:T(8,128)(2,1)S(1)}, u32[]{:S(2)}, u32[]{:S(2)}) collective-permute-start(bf16[2,96,256]{2,1,0:T(8,128)(2,1)S(1)} %get-tuple-element.15), channel_id=1, source_target_pairs={{0,12},{2,14},{4,8},{6,10},{8,4},{10,6},{12,0},{14,2},{1,13},{3,15... | collective-permute-start | bytes 294920 | tf_op jit(solution)/shard_map/ppermute | solution.py:417
  18.0 11.2 %all-to-all-start.1 = ((bf16[8,48,256]{2,1,0:T(8,128)(2,1)}), bf16[8,48,256]{2,1,0:T(8,128)(2,1)S(1)}, u32[]{:S(2)}, u32[]{:S(2)}) async-start(bf16[8,48,256]{2,1,0:T(8,128)(2,1)} %shard_map.97), calls=%async_computation.1 | async-start | bytes 393216 | tf_op jit(solution)/shard_map/all_to_all | solution.py:460
  21.4 6.9 %collective-permute-start.3 = (bf16[4,96,256]{2,1,0:T(8,128)(2,1)S(1)}, bf16[4,96,256]{2,1,0:T(8,128)(2,1)S(1)}, u32[]{:S(2)}, u32[]{:S(2)}) collective-permute-start(bf16[4,96,256]{2,1,0:T(8,128)(2,1)S(1)} %shard_map.98), channel_id=1, source_target_pairs={{0,2},{2,0},{4,6},{6,4},{8,10},{10,8},{12,14},{14,12},{1,3},{3,1},... | collective-permute-start | bytes 589832 | tf_op jit(solution)/shard_map/ppermute | solution.py:417
